TPU v7x, 32 devices: a whole 2x2x4 slice. The times are simulated.
32 devices in a mesh: rep: 2 (over x), region: 16 (over z, y, core).
Axes of the slice: x: 2, y: 2, z: 4, core: 2. Of those that a mesh axis runs over, the one named last changes fastest.
Arguments:
- nodes: bfloat16 [8192, 512], P(('rep', 'region')), parts along dimension 0, may hold values from -6 to 6
- edges: bfloat16 [65536, 512], P(('rep', 'region')), parts along dimension 0, may hold values from -6 to 6
- edge_cot: bfloat16 [65536, 512], P(('rep', 'region')), parts along dimension 0, may hold values from -6 to 6
- agg_cot: bfloat16 [8192, 512], P(('rep', 'region')), parts along dimension 0, may hold values from -6 to 6
- w_in: bfloat16 [1536, 512], replicated, may hold values from -0.15625 to 0.15625
- b_in: float32 [512], replicated, may hold values from -4 to 4
- w_out: bfloat16 [512, 512], replicated, may hold values from -0.25 to 0.25
- b_out: float32 [512], replicated, may hold values from -4 to 4
- gain: float32 [512], replicated, may hold values from 0.1 to 1.9
- send_rows: int32 [256, 16], P('region'), may hold values from 0 to 255, as said below
- edge_slot: int32 [32768], P('region'), may hold values from 0 to 255, as said below
- edge_receiver: int32 [32768], P('region'), may hold values from 0 to 255
- edge_count: int32 [16], P('region'), may hold values from 128 to 2048, as said below
Outputs:
- grad_edges: bfloat16 [65536, 512], P(('rep', 'region')), parts along dimension 0
- grad_nodes: float32 [8192, 512], P(('rep', 'region')), parts along dimension 0
- grad_w_in: bfloat16 [3072, 512], P('rep'), parts along dimension 0
- grad_w_out: bfloat16 [1024, 512], P('rep'), parts along dimension 0
- grad_vectors: bfloat16 [6, 512], P('rep'), parts along dimension 0
There are 2 independent parts, one for each index of `rep`. A program takes and returns all parts, laid end to end along the dimension named above; an argument that names none is the same for every part. Nothing has to cross between parts.
Inputs may be any that keep to these rules, and one draw needn't show every extreme that they name: `send_rows`: row p * 16 + q lists, in its first slots, the local rows of region p's nodes that region q's edges read as senders; the remaining slots hold 0 and no edge reads them. Region q uses all 16 slots from itself and from its two neighbours p = q - 1 and q + 1 (modulo 16), and at least 4 slots from every region. With s = edge_slot[e] for an edge of region q, s // 16 is the region that sends the row and s % 16 a used slot of row (s // 16) * 16 + q of send_rows. Edges at local positions edge_count[q] and above in region q are padding; every count is a multiple of 128, and in every draw one region holds 2048 real edges.
All inputs are finite; a program needn't handle non-finite values.
Results may differ from a plain program's by a relative error of at most 0.0055.
Values may be sent and summed in bfloat16 or wider, within the bound.
No kernel may reach another device: no remote copies, remote signals or barrier semaphores. Data moves between devices by JAX's collectives and lax.ppermute only.
A program may use at most 128 MiB of HBM per device.

v0:
```python
import math

import jax
import jax.numpy as jnp
from jax import lax
from jax.sharding import PartitionSpec as P


def edge_backward(edges, senders, receivers, message_cot, w_in, b_in, w_out, b_out, gain):
    features = edges.shape[1]
    joined = jnp.concatenate([edges, senders, receivers], axis=1)
    pre_act = jnp.dot(joined, w_in, preferred_element_type=jnp.float32) + b_in
    activated = jax.nn.silu(pre_act).astype(jnp.bfloat16)
    pre_norm = jnp.dot(activated, w_out, preferred_element_type=jnp.float32) + b_out
    row_mean = jnp.mean(pre_norm, axis=1, keepdims=True)
    centered = pre_norm - row_mean
    inv_std = lax.rsqrt(jnp.mean(centered * centered, axis=1, keepdims=True) + 1e-05)
    normed = centered * inv_std
    scaled = message_cot * gain
    d_norm = inv_std * (
        scaled
        - jnp.mean(scaled, axis=1, keepdims=True)
        - normed * jnp.mean(scaled * normed, axis=1, keepdims=True)
    )
    d_norm_b = d_norm.astype(jnp.bfloat16)
    dw_out = lax.dot_general(
        activated, d_norm_b, (((0,), (0,)), ((), ())), preferred_element_type=jnp.float32
    )
    d_act = lax.dot_general(
        d_norm_b, w_out, (((1,), (1,)), ((), ())), preferred_element_type=jnp.float32
    )
    sigmoid_pre = jax.nn.sigmoid(pre_act)
    d_pre = d_act * sigmoid_pre * (1.0 + pre_act * (1.0 - sigmoid_pre))
    d_pre_b = d_pre.astype(jnp.bfloat16)
    dw_in = lax.dot_general(
        joined, d_pre_b, (((0,), (0,)), ((), ())), preferred_element_type=jnp.float32
    )
    d_joined = lax.dot_general(
        d_pre_b, w_in, (((1,), (1,)), ((), ())), preferred_element_type=jnp.float32
    )
    vectors = jnp.stack(
        [jnp.sum(d_pre, axis=0), jnp.sum(d_norm, axis=0), jnp.sum(message_cot * normed, axis=0)]
    )
    grad_edge = (message_cot + d_joined[:, :features]).astype(jnp.bfloat16)
    return (
        grad_edge,
        d_joined[:, features : 2 * features],
        d_joined[:, 2 * features :],
        dw_in,
        dw_out,
        vectors,
    )


def body(
    nodes,
    edges,
    edge_cot,
    agg_cot,
    w_in,
    b_in,
    w_out,
    b_out,
    gain,
    send_rows,
    edge_slot,
    edge_receiver,
    edge_count,
):
    regions = lax.axis_size("region")
    features = nodes.shape[1]
    node_rows = nodes.shape[0]
    capacity = send_rows.shape[1]
    outgoing = jnp.take(nodes, send_rows.reshape(-1), axis=0).reshape(regions, capacity, features)
    incoming = lax.all_to_all(outgoing, "region", split_axis=0, concat_axis=0, tiled=True)
    halo_rows = incoming.reshape(regions * capacity, features)
    senders = jnp.take(halo_rows, edge_slot, axis=0)
    receivers = jnp.take(nodes, edge_receiver, axis=0)
    live_rows = (jnp.arange(edges.shape[0]) < edge_count[0]).astype(jnp.float32)
    message_cot = (
        edge_cot.astype(jnp.float32) + jnp.take(agg_cot, edge_receiver, axis=0).astype(jnp.float32)
    ) * live_rows[:, None]
    grad_edges, d_send, d_recv, dw_in, dw_out, vectors = edge_backward(
        edges, senders, receivers, message_cot, w_in, b_in, w_out, b_out, gain
    )
    slot_sums = jax.ops.segment_sum(d_send, edge_slot, num_segments=regions * capacity)
    returned = lax.all_to_all(
        slot_sums.reshape(regions, capacity, features).astype(jnp.bfloat16),
        "region",
        split_axis=0,
        concat_axis=0,
        tiled=True,
    ).astype(jnp.float32)
    grad_nodes = jax.ops.segment_sum(d_recv, edge_receiver, num_segments=node_rows)
    grad_nodes = grad_nodes + jax.ops.segment_sum(
        returned.reshape(regions * capacity, features),
        send_rows.reshape(-1),
        num_segments=node_rows,
    )
    clip_limit = math.sqrt(4.0 * features * features + 3.0 * features)
    sum_in, sum_out, sum_vec = lax.psum((dw_in, dw_out, vectors), "region")
    total_sq = jnp.sum(sum_in * sum_in) + jnp.sum(sum_out * sum_out) + jnp.sum(sum_vec * sum_vec)
    clip_scale = jnp.minimum(1.0, clip_limit / jnp.sqrt(total_sq + 1e-06))
    grad_w_in = (sum_in * clip_scale).astype(jnp.bfloat16)
    grad_w_out = (sum_out * clip_scale).astype(jnp.bfloat16)
    grad_vectors = (sum_vec * clip_scale).astype(jnp.bfloat16)
    return (grad_edges, grad_nodes, grad_w_in, grad_w_out, grad_vectors)


def solution(mesh):
    return jax.shard_map(
        body,
        mesh=mesh,
        in_specs=(
            P(("rep", "region"), None),
            P(("rep", "region"), None),
            P(("rep", "region"), None),
            P(("rep", "region"), None),
            P(),
            P(),
            P(),
            P(),
            P(),
            P("region", None),
            P("region"),
            P("region"),
            P("region"),
        ),
        out_specs=(
            P(("rep", "region"), None),
            P(("rep", "region"), None),
            P("rep", None),
            P("rep", None),
            P("rep", None),
        ),
        check_vma=False,
    )
```

profile of v0, /device:TPU:0, one launch (start us, length us, event | category | flops | bytes accessed | tf_op | source)
XLA Modules:
  0.0 221.9 jit_solution(5569035452445968621)
XLA Ops:
  7.2 0.0 copy-start
  7.2 0.0 copy-start.1
  7.2 0.9 reshape.97
  8.1 0.7 compare_and_fusion.2
  8.8 2.2 gather_fusion
  11.0 0.8 broadcast_select_fusion.3
  11.8 7.4 %all-to-all-start = ((bf16[16,16,512]{2,1,0:T(8,128)(2,1)}), bf16[16,16,512]{2,1,0:T(8,128)(2,1)S(1)}, u32[]{:S(2)}, u32[]{:S(2)}) async-start(bf16[16,16,512]{2,1,0:T(8,128)(2,1)} %broadcast_select_fusion.3), calls=%async_computation | async-start | bytes 524288 | tf_op jit(solution)/shard_map/all_to_all | solution.py:75
  19.2 0.0 all-reduce.3.cloned.1.call-start
  19.3 0.7 compare_and_fusion.1
  20.0 0.7 fusion.18
  20.7 0.7 fusion.19
  21.4 0.7 compare_and_fusion
  22.1 0.0 copy-done.1
  22.1 9.2 %gather_fusion.3 = bf16[2048,512]{1,0:T(8,128)(2,1)} fusion(bf16[256,512]{1,0:T(8,128)(2,1)S(1)} %copy-done.1, s32[2048]{0:T(1024)S(1)} %fusion.18), kind=kCustom, calls=%fused_computation.2.clone | custom fusion | bytes 4202496 | tf_op jit(solution)/shard_map/jit(_take)/gather | solution.py:78
  31.3 0.0 copy-done.2
  31.3 9.2 %gather_fusion.1 = bf16[2048,512]{1,0:T(8,128)(2,1)} fusion(bf16[256,512]{1,0:T(8,128)(2,1)S(1)} %copy-done.2, s32[2048]{0:T(1024)S(1)} %fusion.18), kind=kCustom, calls=%fused_computation.clone | custom fusion | bytes 4202496 | tf_op jit(solution)/shard_map/jit(_take)/gather | solution.py:81
  40.5 4.0 %copy.23 = bf16[2048,512]{0,1:T(8,128)(2,1)} copy(bf16[2048,512]{1,0:T(8,128)(2,1)} %gather_fusion.1) | data formatting | bytes 4194304 | tf_op jit(solution)/shard_map/jit(_take)/gather | solution.py:81
  44.4 4.0 %copy.22 = bf16[2048,512]{0,1:T(8,128)(2,1)} copy(bf16[2048,512]{1,0:T(8,128)(2,1)} %param.17) | data formatting | bytes 4194304 | tf_op args[2]
  49.0 2.8 %broadcast_select_fusion = bf16[2048,512]{1,0:T(8,128)(2,1)} fusion(bf16[2048,512]{1,0:T(8,128)(2,1)} %gather_fusion.3, pred[2048]{0:T(1024)(128)(4,1)S(1)} %compare_and_fusion.1), kind=kLoop, calls=%fused_computation.28 | loop fusion | flops 1048576 | bytes 4196352 | tf_op jit(solution)/shard_map/jit(_take)/select_n | solution.py:78
  51.8 0.0 all-to-all-done
  51.8 9.2 %gather_fusion.2 = bf16[2048,512]{1,0:T(8,128)(2,1)} fusion(bf16[256,512]{1,0:T(8,128)(2,1)S(1)} %bitcast.19, s32[2048]{0:T(1024)S(1)} %fusion.19), kind=kCustom, calls=%fused_computation.1.clone | custom fusion | bytes 4202496 | tf_op jit(solution)/shard_map/jit(_take)/gather | solution.py:77
  61.0 1.9 broadcast_select_fusion.1
  62.9 0.0 copy-done
  62.9 0.3 copy-done.7
  63.2 0.6 copy-done.11
  63.8 3.4 %fusion.5 = f32[2048,512]{1,0:T(8,128)S(1)} fusion(bf16[1536,512]{1,0:T(8,128)(2,1)S(1)} %copy-done, bf16[2048,512]{1,0:T(8,128)(2,1)S(1)} %copy-done.7, bf16[2048,512]{1,0:T(8,128)(2,1)S(1)} %broadcast_select_fusion.1, bf16[2048,512]{1,0:T(8,128)(2,1)S(1)} %copy-done.11), kind=kOutput, calls=%fused_computation.27 | convolution fusion | flops 3240099840 | bytes 12058624 | tf_op jit(solution)/shard_map/dot_general | solution.py:12
  67.3 0.0 copy-done.9
  67.3 0.0 copy-done.12
  67.3 1.7 add_reduce_fusion
  69.1 0.0 copy-start.10
  69.1 0.6 multiply_reduce_fusion.2
  69.7 0.9 copy-done.3
  70.6 0.6 copy-done.4
  71.3 2.9 %multiply_reduce_fusion = (f32[512]{0:T(512)S(1)}, f32[2048]{0:T(1024)S(1)}, f32[2048]{0:T(1024)S(1)}) fusion(f32[2048,512]{0,1:T(8,128)S(1)} %get-tuple-element.24, bf16[2048,512]{0,1:T(8,128)(2,1)S(1)} %copy-done.4, f32[2048]{0:T(1024)S(1)} %add_rsqrt_fusion, f32[2048]{0:T(1024)S(1)} %broadcast_multiply_fusion.2, f32[512]{0:T(512)S(1)} %copy-done.9, ...), kind=kLoop, calls=%fused_computation.12 | loop fusion | flops 14675456 | bytes 8437760 | tf_op jit(solution)/shard_map/reduce_sum | solution.py:42
  74.2 2.7 %fusion.23 = (f32[512]{0:T(512)S(1)}, bf16[2048,512]{0,1:T(8,128)(2,1)S(1)}) fusion(f32[2048]{0:T(1024)S(1)} %get-tuple-element.27, f32[2048]{0:T(1024)S(1)} %broadcast_multiply_fusion.2, f32[2048,512]{0,1:T(8,128)S(1)} %get-tuple-element.24, f32[512]{0:T(512)S(1)} %copy-done.9, f32[2048]{0:T(1024)S(1)} %get-tuple-element.28, f32[512]{0:T(512)S(1)} %copy-done.10, ...), kind=kLoop, calls=%fused_computation.67 | loop fusion | flops 15728128 | bytes 10534912 | tf_op jit(solution)/shard_map/reduce_sum | solution.py:42
  77.0 3.0 %fusion.24 = (f32[512]{0:T(512)S(1)}, bf16[2048,512]{1,0:T(8,128)(2,1)S(1)}) fusion(f32[2048,512]{1,0:T(8,128)S(1)} %fusion.5, f32[512]{0:T(512)S(1)} %copy-done.13, bf16[512,512]{1,0:T(8,128)(2,1)S(1)} %copy-done.12, bf16[2048,512]{0,1:T(8,128)(2,1)S(1)} %get-tuple-element.22), kind=kOutput, calls=%fused_computation.68 | convolution fusion | flops 1085275648 | bytes 8916992 | tf_op jit(solution)/shard_map/dot_general | solution.py:29
  80.0 0.0 copy-start.14
  80.0 2.3 %fusion.9 = f32[512,512]{1,0:T(8,128)} fusion(bf16[2048,512]{0,1:T(8,128)(2,1)S(1)} %get-tuple-element.22, f32[2048,512]{1,0:T(8,128)S(1)} %fusion.5, f32[512]{0:T(512)S(1)} %copy-done.13), kind=kOutput, calls=%fused_computation.36 | convolution fusion | flops 1080033280 | bytes 7342080 | tf_op jit(solution)/shard_map/dot_general | solution.py:26
  82.3 0.0 copy-done.14
  82.3 4.9 %fusion.4 = f32[1536,512]{1,0:T(8,128)} fusion(bf16[2048,512]{1,0:T(8,128)(2,1)S(1)} %copy-done.7, bf16[2048,512]{1,0:T(8,128)(2,1)S(1)} %broadcast_select_fusion.1, bf16[2048,512]{1,0:T(8,128)(2,1)S(1)} %copy-done.11, bf16[2048,512]{1,0:T(8,128)(2,1)S(1)} %get-tuple-element.26), kind=kOutput, calls=%fused_computation.26 | convolution fusion | flops 3240099840 | bytes 11534336 | tf_op jit(solution)/shard_map/dot_general | solution.py:35
  87.3 0.0 all-reduce.3.cloned.1.call-update
  87.3 0.7 copy-done.8
  88.0 0.1 reshape.153
  88.1 5.2 %fusion.7 = f32[2048,1536]{1,0:T(8,128)S(1)} fusion(bf16[1536,512]{1,0:T(8,128)(2,1)S(1)} %copy-done, bf16[2048,512]{1,0:T(8,128)(2,1)} %copy-done.14), kind=kOutput, calls=%fused_computation.34 | convolution fusion | flops 3221225472 | bytes 16252928 | tf_op jit(solution)/shard_map/dot_general | solution.py:38
  93.3 4.7 %copy-done.5 = f32[2048,1536]{1,0:T(8,128)} copy-done((f32[2048,1536]{1,0:T(8,128)}, f32[2048,1536]{1,0:T(8,128)S(1)}, u32[]{:S(2)}) %copy-start.5) | copy-done | bytes 12582936
  98.0 2.4 %slice.20 = f32[2048,512]{1,0:T(8,128)} slice(f32[2048,1536]{1,0:T(8,128)S(1)} %fusion.7), slice={[0:2048], [0:512]} | slice | bytes 8388608 | tf_op jit(solution)/shard_map/slice | solution.py:44
  100.3 13.7 %scatter_custom_fusion.1 = f32[256,512]{1,0:T(8,128)S(1)} fusion(s32[2048]{0:T(1024)} %param.25, f32[2048,1536]{1,0:T(8,128)} %copy-done.5, f32[]{:T(128)} %constant.32.clone.1), kind=kCustom, calls=%fused_computation.8 | custom fusion | flops 1048576 | bytes 4719104 | tf_op jit(solution)/shard_map/scatter-add | solution.py:86
  114.0 0.7 convert_element_type.48
  114.7 6.1 %all-to-all-start.1 = ((bf16[16,16,512]{2,1,0:T(8,128)(2,1)}), bf16[16,16,512]{2,1,0:T(8,128)(2,1)S(1)}, u32[]{:S(2)}, u32[]{:S(2)}) async-start(bf16[16,16,512]{2,1,0:T(8,128)(2,1)} %bitcast.4), calls=%async_computation.1 | async-start | bytes 524288 | tf_op jit(solution)/shard_map/all_to_all | solution.py:87
  120.8 5.4 %copy.26 = f32[2048,512]{0,1:T(8,128)} copy(f32[2048,512]{1,0:T(8,128)} %slice.20) | data formatting | bytes 8388608
  126.3 6.0 %add_convert_fusion = bf16[2048,512]{0,1:T(8,128)(2,1)} fusion(f32[2048,512]{0,1:T(8,128)} %copy.26, bf16[2048,512]{0,1:T(8,128)(2,1)} %copy.22, f32[2048]{0:T(1024)S(1)} %fusion.17, bf16[2048,512]{0,1:T(8,128)(2,1)} %copy.23, pred[2048]{0:T(1024)(128)(4,1)S(1)} %compare_and_fusion.1), kind=kLoop, calls=%fused_computation.13 | loop fusion | flops 7340032 | bytes 10496000 | tf_op jit(solution)/shard_map/convert_element_type | solution.py:44
  132.3 13.6 %scatter_custom_fusion = f32[256,512]{1,0:T(8,128)S(1)} fusion(s32[2048]{0:T(1024)} %param.26, f32[2048,1536]{1,0:T(8,128)} %copy-done.5, f32[]{:T(128)} %constant.32.clone.1), kind=kCustom, calls=%fused_computation.10 | custom fusion | flops 1048576 | bytes 4719104 | tf_op jit(solution)/shard_map/scatter-add | solution.py:94
  145.9 3.9 %copy.25 = bf16[2048,512]{1,0:T(8,128)(2,1)} copy(bf16[2048,512]{0,1:T(8,128)(2,1)} %add_convert_fusion) | data formatting | bytes 4194304
  149.9 34.8 %psum.23 = f32[3,512]{1,0:T(4,128)S(1)} all-reduce(f32[3,512]{1,0:T(4,128)S(1)} %pad_maximum_fusion.3), channel_id=1, replica_groups=mesh['rep'=2,'region'=16] {'region'}, use_global_device_ids=true, to_apply=%region_14.16 | all-reduce | flops 1536 | bytes 12288 | tf_op jit(solution)/shard_map/psum | solution.py:101
  184.7 0.6 multiply_reduce_fusion.6
  185.3 0.0 all-to-all-done.1
  185.3 2.2 %scatter_custom_fusion.2 = f32[256,512]{1,0:T(8,128)S(1)} fusion(s32[256]{0:T(256)S(1)} %reshape.153, bf16[256,512]{1,0:T(8,128)(2,1)S(1)} %bitcast.21, f32[]{:T(128)} %constant.32.clone.1), kind=kCustom, calls=%fused_computation.39 | custom fusion | flops 262144 | bytes 786436 | tf_op jit(solution)/shard_map/scatter-add | solution.py:95
  187.5 0.9 add.107
  188.4 14.4 %all-reduce.3.cloned.1.call-done = (f32[1536,512]{1,0:T(8,128)}, f32[512,512]{1,0:T(8,128)}) async-done(((f32[1536,512]{1,0:T(8,128)}, f32[512,512]{1,0:T(8,128)}), (f32[1536,512]{1,0:T(8,128)}, f32[512,512]{1,0:T(8,128)})) %all-reduce.3.cloned.1.call-update) | async-done | bytes 4194320 | tf_op jit(solution)/shard_map/psum | solution.py:101
  202.8 3.4 %multiply_reduce_fusion.4 = f32[]{:T(128)} fusion(f32[1536,512]{1,0:T(8,128)} %get-tuple-element.19), kind=kLoop, calls=%fused_computation.25 | loop fusion | flops 1572863 | bytes 3145732 | tf_op jit(solution)/shard_map/reduce_sum | solution.py:102
  206.1 2.1 multiply_reduce_fusion.5
  210.1 0.6 multiply_convert_fusion.3
  210.7 0.9 multiply_convert_fusion.2
  211.6 3.5 %multiply_convert_fusion.1 = bf16[1536,512]{1,0:T(8,128)(2,1)} fusion(f32[1536,512]{1,0:T(8,128)} %get-tuple-element.19, f32[]{:T(128)S(6)} %min.3), kind=kLoop, calls=%fused_computation.24 | loop fusion | flops 1572864 | bytes 4718596 | tf_op jit(solution)/shard_map/convert_element_type | solution.py:104
  (21 shorter events, 0.1 us)
Async XLA Ops:
  7.2 55.7 %copy-start = (bf16[1536,512]{1,0:T(8,128)(2,1)S(1)}, bf16[1536,512]{1,0:T(8,128)(2,1)}, u32[]{:S(2)}) copy-start(bf16[1536,512]{1,0:T(8,128)(2,1)} %param.19) | copy-start | bytes 4718596
  7.2 14.9 %copy-start.1 = (bf16[256,512]{1,0:T(8,128)(2,1)S(1)}, bf16[256,512]{1,0:T(8,128)(2,1)}, u32[]{:S(2)}) copy-start(bf16[256,512]{1,0:T(8,128)(2,1)} %param.15) | copy-start | bytes 786436
  11.8 40.0 %all-to-all-start = ((bf16[16,16,512]{2,1,0:T(8,128)(2,1)}), bf16[16,16,512]{2,1,0:T(8,128)(2,1)S(1)}, u32[]{:S(2)}, u32[]{:S(2)}) async-start(bf16[16,16,512]{2,1,0:T(8,128)(2,1)} %broadcast_select_fusion.3), calls=%async_computation | async-start | bytes 524288 | tf_op jit(solution)/shard_map/all_to_all | solution.py:75
  19.2 183.5 %all-reduce.3.cloned.1.call-start = ((), (), s32[]{:S(2)}) async-start(), calls=%async_computation.2 | async-start | bytes 8388608 | tf_op jit(solution)/shard_map/psum | solution.py:101
  22.1 9.2 %copy-start.2 = (bf16[256,512]{1,0:T(8,128)(2,1)S(1)}, bf16[256,512]{1,0:T(8,128)(2,1)}, u32[]{:S(2)}) copy-start(bf16[256,512]{1,0:T(8,128)(2,1)} %param.18) | copy-start | bytes 786436
  61.0 2.2 %copy-start.7 = (bf16[2048,512]{1,0:T(8,128)(2,1)S(1)}, bf16[2048,512]{1,0:T(8,128)(2,1)}, u32[]{:S(2)}) copy-start(bf16[2048,512]{1,0:T(8,128)(2,1)} %broadcast_select_fusion) | copy-start | bytes 6291460
  61.0 2.9 %copy-start.11 = (bf16[2048,512]{1,0:T(8,128)(2,1)S(1)}, bf16[2048,512]{1,0:T(8,128)(2,1)}, u32[]{:S(2)}) copy-start(bf16[2048,512]{1,0:T(8,128)(2,1)} %param.16) | copy-start | bytes 6291460
  63.8 3.5 %copy-start.9 = (f32[512]{0:T(512)S(1)}, f32[512]{0:T(512)}, u32[]{:S(2)}) copy-start(f32[512]{0:T(512)} %param.22) | copy-start | bytes 6148
  63.8 3.5 %copy-start.12 = (bf16[512,512]{1,0:T(8,128)(2,1)S(1)}, bf16[512,512]{1,0:T(8,128)(2,1)}, u32[]{:S(2)}) copy-start(bf16[512,512]{1,0:T(8,128)(2,1)} %param.21) | copy-start | bytes 1572868
  63.8 3.5 %copy-start.13 = (f32[512]{0:T(512)S(1)}, f32[512]{0:T(512)}, u32[]{:S(2)}) copy-start(f32[512]{0:T(512)} %param.20) | copy-start | bytes 6148
  69.0 1.6 copy-start.3
  69.1 2.2 copy-start.4
  69.1 2.2 copy-start.10
  80.0 2.3 %copy-start.14 = (bf16[2048,512]{1,0:T(8,128)(2,1)}, bf16[2048,512]{1,0:T(8,128)(2,1)S(1)}, u32[]{:S(2)}) copy-start(bf16[2048,512]{1,0:T(8,128)(2,1)S(1)} %get-tuple-element.26) | copy-start | bytes 6291460
  87.3 0.7 copy-start.8
  93.3 4.7 %copy-start.5 = (f32[2048,1536]{1,0:T(8,128)}, f32[2048,1536]{1,0:T(8,128)S(1)}, u32[]{:S(2)}) copy-start(f32[2048,1536]{1,0:T(8,128)S(1)} %fusion.7) | copy-start | bytes 37748740
  114.7 70.5 %all-to-all-start.1 = ((bf16[16,16,512]{2,1,0:T(8,128)(2,1)}), bf16[16,16,512]{2,1,0:T(8,128)(2,1)S(1)}, u32[]{:S(2)}, u32[]{:S(2)}) async-start(bf16[16,16,512]{2,1,0:T(8,128)(2,1)} %bitcast.4), calls=%async_computation.1 | async-start | bytes 524288 | tf_op jit(solution)/shard_map/all_to_all | solution.py:87
  202.8 8.0 %copy-start.6 = (f32[512,512]{1,0:T(8,128)S(1)}, f32[512,512]{1,0:T(8,128)}, u32[]{:S(2)}) copy-start(f32[512,512]{1,0:T(8,128)} %get-tuple-element.20) | copy-start | bytes 3145732
Sparse Core Ops, SparseCore 0:
  87.4 115.2 all-reduce.2
where the time goes:
time: 223 us; the launch traced here: 222 us
  other arithmetic  63.5 us (28%)
  local copies, waits for them, and re-layouts  58.2 us (26%)
  blocking collectives  34.8 us (16%)
  matrix products  20.7 us (9%)
  between operations  16.8 us (8%)
  waiting for transfers between devices  14.4 us (6%)
  starting transfers between devices  13.5 us (6%)
    psum x1, blocking collectives, body(): sum_in, sum_out, sum_vec = lax.psum((dw_in, dw_out, vectors), 'region')  34.8 us
    unnamed x33, local copies, waits for them, and re-layouts  21.2 us
    psum x1, waiting for transfers between devices, body(): sum_in, sum_out, sum_vec = lax.psum((dw_in, dw_out, vectors), 'region')  14.4 us
    scatter-add x1, other arithmetic, body(): jax.ops.segment_sum(d_send, edge_slot, num_segments=regions * capacity)  13.7 us
    scatter-add x1, other arithmetic, body(): jax.ops.segment_sum(d_recv, edge_receiver, num_segments=node_rows)  13.6 us
    gather x2, local copies, waits for them, and re-layouts, body(): jnp.take(agg_cot, edge_receiver, axis=0).astype(jnp.float32)  13.1 us
    gather x1, local copies, waits for them, and re-layouts, body(): receivers = jnp.take(nodes, edge_receiver, axis=0)  9.21 us
    gather x1, local copies, waits for them, and re-layouts, body(): senders = jnp.take(halo_rows, edge_slot, axis=0)  9.16 us
  transfers between devices with their start and end apart: 3, of which 1 were waited for; matrix products, arithmetic and copies ran while one was open for 39% of the time, Pallas kernels for 0%

commit v1 on v0

v1 whole, which is shorter than its diff:
```python
import functools
import math

import jax
import jax.numpy as jnp
from jax import lax
from jax.experimental import pallas as pl
from jax.experimental.pallas import tpu as pltpu
from jax.sharding import PartitionSpec as P

BF = jnp.bfloat16
F32 = jnp.float32
VMEM = pltpu.VMEM
SMEM = pltpu.SMEM
LIMIT = 60 * 1024 * 1024
SMALL = 16 * 1024 * 1024
EXTRA = 16


def dot(a, b, dims):
    return lax.dot_general(a, b, ((dims[0], dims[1]), ((), ())), preferred_element_type=F32)


NN = ((1,), (0,))
NT = ((1,), (1,))
TN = ((0,), (0,))


def one_hot_t(index_row, count):
    wide = lax.broadcasted_iota(jnp.int32, (count, index_row.shape[1]), 0) == index_row
    return jnp.where(wide, 1.0, 0.0).astype(BF)


def params(semantics=None):
    if semantics is None:
        return pltpu.CompilerParams(vmem_limit_bytes=LIMIT)
    return pltpu.CompilerParams(vmem_limit_bytes=LIMIT, dimension_semantics=semantics)


def whole(shape):
    return pl.BlockSpec(shape, lambda *i: (0,) * len(shape))


def cost(flops, nbytes):
    return pl.CostEstimate(flops=int(flops), bytes_accessed=int(nbytes), transcendentals=0)


def pick_kernel(index_ref, nodes_ref, out_ref):
    out_ref[...] = dot(one_hot_t(index_ref[...], nodes_ref.shape[0]), nodes_ref[...], TN).astype(BF)


def pick_rows(index_row, nodes):
    return pl.pallas_call(
        pick_kernel,
        out_shape=jax.ShapeDtypeStruct((index_row.shape[1], nodes.shape[1]), BF),
        compiler_params=params(),
    )(index_row, nodes)


def local_kernel(recv_ref, edges_ref, nodes_ref, w_e_ref, w_r_ref, b_ref, pre_ref, table):
    @pl.when(pl.program_id(0) == 0)
    def _():
        table[...] = dot(nodes_ref[...], w_r_ref[...], NN).astype(BF)

    got = dot(one_hot_t(recv_ref[...], nodes_ref.shape[0]), table[...], TN)
    pre_ref[...] = (dot(edges_ref[...], w_e_ref[...], NN) + got + b_ref[...]).astype(BF)


def local_part(recv_row, edges, nodes, w_in, b_row, block):
    total, f = edges.shape
    n = nodes.shape[0]
    edge_spec = pl.BlockSpec((block, f), lambda i: (i, 0))
    return pl.pallas_call(
        local_kernel,
        grid=(total // block,),
        in_specs=[
            pl.BlockSpec((1, block), lambda i: (0, i)),
            edge_spec,
            whole((n, f)),
            pl.BlockSpec((f, f), lambda i: (0, 0)),
            pl.BlockSpec((f, f), lambda i: (2, 0)),
            whole((1, f)),
        ],
        out_specs=edge_spec,
        out_shape=jax.ShapeDtypeStruct((total, f), BF),
        scratch_shapes=[VMEM((n, f), BF)],
        compiler_params=params(("arbitrary",)),
        cost_estimate=cost(2 * total * f * (f + n), 4 * total * f),
    )(recv_row, edges, nodes, w_in, w_in, b_row)


def slot_of(position, order):
    slot = 0
    for bit, mask in enumerate(reversed(order)):
        if position >> bit & 1:
            slot |= mask
    return slot


def write_slots(me, parts, keep_ref, send_ref, order, first=0):
    pieces = 2 ** len(order)
    home = me & (pieces - 1)
    r = parts[0].shape[0] // pieces
    for position in range(pieces):
        piece = home ^ slot_of(position, order)
        start = pl.multiple_of(piece * r, r)
        half, at = divmod(position, pieces // 2)
        ref = send_ref if half else keep_ref
        for k, acc in enumerate(parts):
            row = first + (at * len(parts) + k) * r
            ref[row : row + r, :] = acc[pl.ds(start, r), :].astype(ref.dtype)


def edge_kernel(order_p, order_q, blocks, me_ref, count_ref, slot_ref, recv_ref, edges_ref, cot_ref, pre_ref,
                nodes_ref, agg_ref, halo_ref, w_s_ref, w_out_ref, b_ref, gain_ref,
                dp_ref, keep_p, send_p, keep_q, send_q, sum_s_ref, sum_r_ref,
                table, acc_o, acc_e, acc_s, acc_r, acc_x, acc_y, sums):
    step = pl.program_id(0)
    rows, f = edges_ref.shape

    @pl.when(step == 0)
    def _():
        table[...] = dot(halo_ref[...], w_s_ref[...], NN).astype(BF)
        for ref in (acc_o, acc_e, acc_s, acc_r, sums):
            ref[...] = jnp.zeros_like(ref)

    hot_s = one_hot_t(slot_ref[...], halo_ref.shape[0])
    hot_r = one_hot_t(recv_ref[...], nodes_ref.shape[0])
    pre = pre_ref[...].astype(F32) + dot(hot_s, table[...], TN)
    sig = 0.5 * jnp.tanh(0.5 * pre) + 0.5
    silu = pre * sig
    act = silu.astype(BF)
    slope = sig + silu * (1.0 - sig)
    live = lax.broadcasted_iota(jnp.int32, (rows, f), 0) < count_ref[0] - step * rows
    mc = jnp.where(live, cot_ref[...].astype(F32) + dot(hot_r, agg_ref[...], TN), 0.0)
    norm_in = dot(act, w_out_ref[...], NN) + b_ref[...]
    inverse = 1.0 / f
    centered = norm_in - jnp.sum(norm_in, axis=1, keepdims=True) * inverse
    inv_std = lax.rsqrt(jnp.sum(centered * centered, axis=1, keepdims=True) * inverse + 1e-05)
    normed = centered * inv_std
    scaled = mc * gain_ref[...]
    mean_s = jnp.sum(scaled, axis=1, keepdims=True) * inverse
    mean_sn = jnp.sum(scaled * normed, axis=1, keepdims=True) * inverse
    dn = inv_std * (scaled - mean_s - normed * mean_sn)
    dn_b = dn.astype(BF)
    acc_o[...] += dot(act, dn_b, TN)
    sums[0:8, :] += jnp.sum(dn.reshape(rows // 8, 8, f), axis=0)
    sums[8:16, :] += jnp.sum((mc * normed).reshape(rows // 8, 8, f), axis=0)
    dp_b = (dot(dn_b, w_out_ref[...], NT) * slope).astype(BF)
    dp_ref[...] = dp_b
    acc_e[...] += dot(edges_ref[...], dp_b, TN)
    acc_s[...] += dot(hot_s, dp_b, NN)
    acc_r[...] += dot(hot_r, dp_b, NN)

    @pl.when(step == blocks - 1)
    def _():
        sum_s = acc_s[...].astype(BF)
        sum_r = acc_r[...].astype(BF)
        sum_s_ref[...] = sum_s
        sum_r_ref[...] = sum_r
        acc_x[...] = dot(halo_ref[...], sum_s, TN)
        acc_y[...] = dot(nodes_ref[...], sum_r, TN)
        me = me_ref[0]
        write_slots(me, (acc_x, acc_y), keep_p, send_p, order_p)
        write_slots(me, (acc_e, acc_o), keep_q, send_q, order_q, EXTRA)
        row = lax.broadcasted_iota(jnp.int32, (EXTRA // 2, f), 0)
        exact = jnp.where(row == 0, jnp.sum(acc_r[...], axis=0, keepdims=True), 0.0)
        exact = jnp.where(row == 1, jnp.sum(sums[0:8, :], axis=0, keepdims=True), exact)
        exact = jnp.where(row == 2, jnp.sum(sums[8:16, :], axis=0, keepdims=True), exact)
        high = exact.astype(BF).astype(F32)
        vectors = jnp.concatenate([high, exact - high], axis=0)
        keep_q[:EXTRA, :] = vectors
        send_q[:EXTRA, :] = vectors.astype(BF)


def edge_part(me, count, slot_row, recv_row, edges, edge_cot, pre, nodes, agg, halo, w_in, w_out, b_row, gain_row,
              order_p, order_q, block):
    total, f = edges.shape
    slots, n = halo.shape[0], nodes.shape[0]
    edge_spec = pl.BlockSpec((block, f), lambda i: (i, 0))
    index_spec = pl.BlockSpec((1, block), lambda i: (0, i))
    smem = pl.BlockSpec(memory_space=SMEM)
    shapes = [
        ((total, f), BF), ((f, f), F32), ((f, f), BF), ((f + EXTRA, f), F32), ((f + EXTRA, f), BF),
        ((slots, f), BF), ((n, f), BF),
    ]
    return pl.pallas_call(
        functools.partial(edge_kernel, order_p, order_q, total // block),
        grid=(total // block,),
        in_specs=[
            smem,
            smem,
            index_spec,
            index_spec,
            edge_spec,
            edge_spec,
            edge_spec,
            whole((n, f)),
            whole((n, f)),
            whole((slots, f)),
            pl.BlockSpec((f, f), lambda i: (1, 0)),
            whole((f, f)),
            whole((1, f)),
            whole((1, f)),
        ],
        out_specs=[edge_spec] + [whole(s) for s, _ in shapes[1:]],
        out_shape=[jax.ShapeDtypeStruct(s, d) for s, d in shapes],
        scratch_shapes=[
            VMEM((slots, f), BF), VMEM((f, f), F32), VMEM((f, f), F32), VMEM((slots, f), F32), VMEM((n, f), F32),
            VMEM((f, f), F32), VMEM((f, f), F32), VMEM((16, f), F32),
        ],
        compiler_params=params(("arbitrary",)),
        cost_estimate=cost(2 * total * f * (4 * f + 2 * slots + 2 * n), 8 * total * f),
    )(me, count, slot_row, recv_row, edges, edge_cot, pre, nodes, agg, halo, w_in, w_out, b_row, gain_row)


def edge_grad_kernel(count_ref, recv_ref, dp_ref, cot_ref, agg_ref, w_ref, out_ref):
    rows, f = dp_ref.shape
    got = dot(one_hot_t(recv_ref[...], agg_ref.shape[0]), agg_ref[...], TN)
    live = lax.broadcasted_iota(jnp.int32, (rows, f), 0) < count_ref[0] - pl.program_id(0) * rows
    mc = jnp.where(live, cot_ref[...].astype(F32) + got, 0.0)
    out_ref[...] = (mc + dot(dp_ref[...], w_ref[...], NT)).astype(BF)


def edge_grad(count, recv_row, dp, edge_cot, agg, w_in, block):
    total, f = dp.shape
    n = agg.shape[0]
    edge_spec = pl.BlockSpec((block, f), lambda i: (i, 0))
    return pl.pallas_call(
        edge_grad_kernel,
        grid=(total // block,),
        in_specs=[
            pl.BlockSpec(memory_space=SMEM),
            pl.BlockSpec((1, block), lambda i: (0, i)),
            edge_spec,
            edge_spec,
            whole((n, f)),
            pl.BlockSpec((f, f), lambda i: (0, 0)),
        ],
        out_specs=edge_spec,
        out_shape=jax.ShapeDtypeStruct((total, f), BF),
        compiler_params=params(("arbitrary",)),
        cost_estimate=cost(2 * total * f * (f + n), 6 * total * f),
    )(count, recv_row, dp, edge_cot, agg, w_in)


def node_grad_kernel(index_ref, returned_ref, sum_r_ref, w_s_ref, w_r_ref, out_ref):
    hot = one_hot_t(index_ref[...], out_ref.shape[0])
    sum_s = dot(hot, returned_ref[...], NN).astype(BF)
    out_ref[...] = dot(sum_s, w_s_ref[...], NT) + dot(sum_r_ref[...], w_r_ref[...], NT)


def node_grad(index_row, returned, sum_r, w_in):
    n, f = sum_r.shape
    slots = returned.shape[0]
    return pl.pallas_call(
        node_grad_kernel,
        grid=(1,),
        in_specs=[
            whole((1, slots)),
            whole((slots, f)),
            whole((n, f)),
            pl.BlockSpec((f, f), lambda i: (1, 0)),
            pl.BlockSpec((f, f), lambda i: (2, 0)),
        ],
        out_specs=whole((n, f)),
        out_shape=jax.ShapeDtypeStruct((n, f), F32),
        compiler_params=params(("arbitrary",)),
        cost_estimate=cost(2 * n * f * (slots + 2 * f), 4 * n * f + 8 * f * f),
    )(index_row, returned, sum_r, w_in, w_in)


def add_split_kernel(extra, keep_ref, got_ref, keep_out, send_out):
    half = keep_out.shape[0] - extra
    total = keep_ref[: extra + half, :] + got_ref[: extra + half, :].astype(F32)
    keep_out[...] = total
    if extra:
        send_out[:extra, :] = total[:extra, :].astype(BF)
    away = keep_ref[extra + half :, :] + got_ref[extra + half :, :].astype(F32)
    send_out[extra:, :] = away.astype(BF)


def add_split(keep, got, extra):
    rows, f = keep.shape
    half = (rows - extra) // 2 + extra
    return pl.pallas_call(
        functools.partial(add_split_kernel, extra),
        out_shape=[jax.ShapeDtypeStruct((half, f), F32), jax.ShapeDtypeStruct((half, f), BF)],
        compiler_params=pltpu.CompilerParams(vmem_limit_bytes=SMALL),
    )(keep, got)


def add_kernel(keep_ref, got_ref, out_ref):
    out_ref[...] = (keep_ref[...].astype(F32) + got_ref[...].astype(F32)).astype(BF)


def add(keep, got):
    return pl.pallas_call(
        add_kernel,
        out_shape=jax.ShapeDtypeStruct(keep.shape, BF),
        compiler_params=pltpu.CompilerParams(vmem_limit_bytes=SMALL),
    )(keep, got)


def swap(x, mask, regions):
    return lax.ppermute(x, "region", [(i, i ^ mask) for i in range(regions)])


def finish_kernel(order_p, order_q, limit, me_ref, p0, p1, q0, q1, vec_ref, w_in_ref, w_out_ref, vec_out):
    f = w_out_ref.shape[1]
    vec = vec_ref[...].astype(F32)
    vec = vec[: EXTRA // 2, :] + vec[EXTRA // 2 :, :]
    squares = jnp.sum(vec * vec, axis=0, keepdims=True)
    for ref in (p0, p1, q0, q1):
        x = ref[...].astype(F32)
        x = x * x
        squares = squares + jnp.sum(jnp.sum(x.reshape(-1, 8, f), axis=0), axis=0, keepdims=True)
    total = jnp.sum(squares, axis=1, keepdims=True)
    scale = jnp.minimum(1.0, limit * lax.rsqrt(total + 1e-06))
    vec_out[...] = (vec[0:3, :] * scale).astype(BF)
    me = me_ref[0]
    targets = [(p0, p1, order_p, ((w_in_ref, f), (w_in_ref, 2 * f))), (q0, q1, order_q, ((w_in_ref, 0), (w_out_ref, 0)))]
    for low, high, order, outs in targets:
        pieces = 2 ** len(order)
        home = me & (pieces - 1)
        r = f // pieces
        for position in range(pieces):
            half, at = divmod(position, pieces // 2)
            piece = home ^ slot_of(position, order)
            for k, (out, offset) in enumerate(outs):
                row = (at * len(outs) + k) * r
                x = (high if half else low)[row : row + r, :].astype(F32)
                start = pl.multiple_of(offset + piece * r, r)
                out[pl.ds(start, r), :] = (x * scale).astype(BF)


def finish(me, p, q, vec, order_p, order_q):
    f = vec.shape[1]
    limit = math.sqrt(4.0 * f * f + 3.0 * f)
    return pl.pallas_call(
        functools.partial(finish_kernel, order_p, order_q, limit),
        in_specs=[pl.BlockSpec(memory_space=SMEM)] + [pl.BlockSpec(memory_space=VMEM)] * 5,
        out_shape=[
            jax.ShapeDtypeStruct((3 * f, f), BF),
            jax.ShapeDtypeStruct((f, f), BF),
            jax.ShapeDtypeStruct((3, f), BF),
        ],
        compiler_params=pltpu.CompilerParams(vmem_limit_bytes=SMALL),
    )(me, *p, *q, vec)


def all_to_all(x, regions):
    rows, f = x.shape
    out = lax.all_to_all(x.reshape(regions, rows // regions, f), "region", split_axis=0, concat_axis=0, tiled=True)
    return out.reshape(rows, f)


def body(nodes, edges, edge_cot, agg_cot, w_in, b_in, w_out, b_out, gain, send_rows, edge_slot, edge_receiver, edge_count):
    regions = lax.axis_size("region")
    f = edges.shape[1]
    me = lax.axis_index("region").astype(jnp.int32).reshape(1)
    masks = [2**k for k in range(regions.bit_length() - 1)]
    last = masks[-1]
    order_p = masks[:-1]
    order_q = order_p[:1] + order_p[1:][::-1]
    index_row = send_rows.reshape(1, -1)
    slot_row = edge_slot.reshape(1, -1)
    recv_row = edge_receiver.reshape(1, -1)
    after = lax.optimization_barrier

    halo = all_to_all(pick_rows(index_row, nodes), regions)
    pre = local_part(recv_row, edges, nodes, w_in, b_in.reshape(1, f), 1024)
    dp, keep_p, send_p, keep_q, send_q, sum_s, sum_r = edge_part(
        me, edge_count, slot_row, recv_row, edges, edge_cot, pre, nodes, agg_cot, halo, w_in, w_out,
        b_out.reshape(1, f), gain.reshape(1, f), order_p, order_q, 512
    )

    steps = len(order_p)
    for step in range(steps):
        got_p = swap(send_p, order_p[step], regions)
        got_q = swap(send_q, order_q[step], regions)
        if step < steps - 1:
            keep_p, send_p = add_split(keep_p, got_p, 0)
            keep_q, send_q = add_split(keep_q, got_q, EXTRA)
        else:
            keep_p, keep_q = add(keep_p, got_p), add(keep_q, got_q)
        if step == 0:
            sum_s, dp, send_p, send_q = after((sum_s, dp, send_p, send_q))
            returned = all_to_all(sum_s, regions)
            grad_edges = edge_grad(edge_count, recv_row, dp, edge_cot, agg_cot, w_in, 512)
        if step == 1:
            keep_p, keep_q, grad_edges = after((keep_p, keep_q, grad_edges))
    part_p = add(keep_p, swap(keep_p, last, regions))
    part_q = add(keep_q, swap(keep_q, last, regions))
    vec, part_q = part_q[:EXTRA], part_q[EXTRA:]
    for step in range(steps - 1, -1, -1):
        got_p = swap(part_p, order_p[step], regions)
        got_q = swap(part_q, order_q[step], regions)
        if step:
            part_p = jnp.concatenate([part_p, got_p], axis=0)
            part_q = jnp.concatenate([part_q, got_q], axis=0)
        if step == steps - 1:
            part_p, part_q, returned = after((part_p, part_q, returned))
            grad_nodes = node_grad(index_row, returned, sum_r, w_in)
        if step == 1:
            part_p, part_q, grad_nodes = after((part_p, part_q, grad_nodes))
    grad_w_in, grad_w_out, grad_vectors = finish(me, (part_p, got_p), (part_q, got_q), vec, order_p, order_q)
    return (grad_edges, grad_nodes, grad_w_in, grad_w_out, grad_vectors)


def solution(mesh):
    split = P(("rep", "region"), None)
    return jax.shard_map(
        body,
        mesh=mesh,
        in_specs=(split, split, split, split, P(), P(), P(), P(), P(), P("region", None), P("region"), P("region"), P("region")),
        out_specs=(split, split, P("rep", None), P("rep", None), P("rep", None)),
        check_vma=False,
    )
```

time: 223 us -> 99.6 us (0.45)
  other arithmetic: 63.5 us -> 0.11 us
  local copies, waits for them, and re-layouts: 58.2 us -> 3.29 us
  blocking collectives: 34.8 us -> 0 us
  Pallas kernels: 0 us -> 34.1 us
  waiting for transfers between devices: 14.4 us -> 35.4 us
  matrix products: 20.7 us -> 0 us
  between operations: 16.8 us -> 1.44 us
  starting transfers between devices: 13.5 us -> 24.6 us
    psum x1 -> x0, blocking collectives: 34.8 us -> none  [body(): sum_in, sum_out, sum_vec = lax.psum((dw_in, dw_out, vectors), 'region')]
    pallas_call x0 -> x14, Pallas kernels: none -> 34.1 us  [the longest x1 16.5 us: edge_part(): pl.pallas_call(functools.partial(edge_kernel, order_p, order_q, total //...]
    gather x5 -> x0, local copies, waits for them, and re-layouts: 33.7 us -> none  [the longest x2 13.1 us: body(): jnp.take(agg_cot, edge_receiver, axis=0).astype(jnp.float32)]
    ppermute x0 -> x14, waiting for transfers between devices: none -> 31 us  [swap(): return lax.ppermute(x, 'region', [(i, i ^ mask) for i in range(regions)])]
    scatter-add x3 -> x0, other arithmetic: 29.5 us -> none  [the longest x1 13.7 us: body(): jax.ops.segment_sum(d_send, edge_slot, num_segments=regions * capacity)]
    dot_general x6 -> x0, matrix products: 20.7 us -> none  [the longest x1 5.23 us: edge_backward(): lax.dot_general(d_pre_b, w_in, (((1,), (1,)), ((), ())), preferred_elemen...]
    unnamed x33 -> x8, local copies, waits for them, and re-layouts: 21.2 us -> 1.94 us
    psum x1 -> x0, waiting for transfers between devices: 14.4 us -> none  [body(): sum_in, sum_out, sum_vec = lax.psum((dw_in, dw_out, vectors), 'region')]
  transfers between devices with their start and end apart: 3 -> 16, of which waited for: 1 -> 9; matrix products, arithmetic and copies ran while one was open for 39% -> 0% of each run, Pallas kernels for 0% -> 14%
where the time goes in v1:
time: 99.6 us; the launch traced here: 99 us
  waiting for transfers between devices  35.4 us (36%)
  Pallas kernels  34.1 us (34%)
  starting transfers between devices  24.6 us (25%)
  local copies, waits for them, and re-layouts  3.29 us (3%)
  between operations  1.44 us (1%)
    ppermute x14, waiting for transfers between devices, swap(): return lax.ppermute(x, 'region', [(i, i ^ mask) for i in range(regions)])  31 us
    pallas_call x1, Pallas kernels, edge_part(): pl.pallas_call(functools.partial(edge_kernel, order_p, order_q, total //...  16.5 us
    ppermute x14, starting transfers between devices, swap(): return lax.ppermute(x, 'region', [(i, i ^ mask) for i in range(regions)])  12.8 us
    all_to_all x2, starting transfers between devices, all_to_all(): lax.all_to_all(x.reshape(regions, rows // regions, f), 'region', split_ax...  11.8 us
    pallas_call x1, Pallas kernels, edge_grad(): pl.pallas_call(edge_grad_kernel, grid=(total // block,), in_specs=[pl.Blo...  5.82 us
    pallas_call x1, Pallas kernels, local_part(): pl.pallas_call(local_kernel, grid=(total // block,), in_specs=[pl.BlockSp...  4.99 us
    all_to_all x2, waiting for transfers between devices, all_to_all(): lax.all_to_all(x.reshape(regions, rows // regions, f), 'region', split_ax...  4.41 us
    pallas_call x1, Pallas kernels, node_grad(): pl.pallas_call(node_grad_kernel, grid=(1,), in_specs=[whole((1, slots)),...  2.68 us
  transfers between devices with their start and end apart: 16, of which 9 were waited for; matrix products, arithmetic and copies ran while one was open for 0% of the time, Pallas kernels for 14%

profile of v1, /device:TPU:0, one launch (start us, length us, event | category | flops | bytes accessed | tf_op | source)
XLA Modules:
  0.0 99.0 jit_solution(5012143627247013214)
XLA Ops:
  0.6 1.3 %reshape.47.index_ref = s32[1,256]{1,0:T(1,128)} reshape(s32[16,16]{1,0:T(8,128)} %param.22) | data formatting | bytes 2048 | tf_op jit(solution)/shard_map/reshape | solution.py:366
  2.0 1.9 %shard_map.165 = bf16[256,512]{1,0:T(8,128)(2,1)} custom-call(s32[1,256]{1,0:T(1,128)} %reshape.47.index_ref, bf16[256,512]{1,0:T(8,128)(2,1)} %nodes_ref.5), custom_call_target="tpu_custom_call" | custom-call | tf_op jit(solution)/shard_map/pallas_call | solution.py:53
  3.9 7.4 %all-to-all-start = ((bf16[16,16,512]{2,1,0:T(8,128)(2,1)}), bf16[16,16,512]{2,1,0:T(8,128)(2,1)S(1)}, u32[]{:S(2)}, u32[]{:S(2)}) async-start(bf16[16,16,512]{2,1,0:T(8,128)(2,1)} %bitcast.11), calls=%async_computation | async-start | bytes 524288 | tf_op jit(solution)/shard_map/all_to_all | solution.py:354
  11.9 5.0 %shard_map.164.pre_ref = bf16[2048,512]{1,0:T(8,128)(2,1)} custom-call(s32[1,2048]{1,0:T(1,128)} %bitcast.13, bf16[2048,512]{1,0:T(8,128)(2,1)} %edges_ref.3, bf16[256,512]{1,0:T(8,128)(2,1)} %nodes_ref.5, bf16[1536,512]{1,0:T(8,128)(2,1)} %w_r_ref.3, bf16[1536,512]{1,0:T(8,128)(2,1)} %w_r_ref.3, f32[1,512]{1,0:T(1,128)} %bitcast.16), custom_call_target="tpu_custom_call" | custom-call | flops 1610612736 | bytes 4194304 | tf_op jit(solution)/shard_map/pallas_call | solution.py:73
  16.9 4.4 %all-to-all-done = bf16[16,16,512]{2,1,0:T(8,128)(2,1)S(1)} async-done(((bf16[16,16,512]{2,1,0:T(8,128)(2,1)}), bf16[16,16,512]{2,1,0:T(8,128)(2,1)S(1)}, u32[]{:S(2)}, u32[]{:S(2)}) %all-to-all-start) | async-done | bytes 262176 | tf_op jit(solution)/shard_map/all_to_all | solution.py:354
  21.3 0.0 copy-start.3
  21.3 0.7 copy-done.3
  22.0 16.5 %shard_map.166 = (bf16[2048,512]{1,0:T(8,128)(2,1)}, f32[512,512]{1,0:T(8,128)}, bf16[512,512]{1,0:T(8,128)(2,1)}, f32[528,512]{1,0:T(8,128)}, bf16[528,512]{1,0...) custom-call(s32[1]{0:T(128)} %bitcast.me_ref, s32[1]{0:T(128)S(6)} %copy.18.count_ref, ...), custom_call_target="tpu_custom_call" | custom-call | flops 6442450944 | bytes 8388608 | tf_op jit(solution)/shard_map/pallas_call | solution.py:187
  38.5 0.0 copy-start
  38.5 0.1 collective-permute-start.1
  38.6 0.5 collective-permute-start
  39.1 2.4 %collective-permute-done.got_ref = bf16[512,512]{1,0:T(8,128)(2,1)S(1)} collective-permute-done((bf16[512,512]{1,0:T(8,128)(2,1)}, bf16[512,512]{1,0:T(8,128)(2,1)S(1)}, u32[]{:S(2)}, u32[]{:S(2)}) %collective-permute-start) | collective-permute-done | bytes 524320 | tf_op jit(solution)/shard_map/ppermute | solution.py:306
  41.5 0.0 copy-start.1
  41.5 1.2 %copy-done.1 = f32[512,512]{1,0:T(8,128)S(1)} copy-done((f32[512,512]{1,0:T(8,128)S(1)}, f32[512,512]{1,0:T(8,128)}, u32[]{:S(2)}) %copy-start.1) | copy-done | bytes 1048600
  42.7 0.1 shard_map.167
  42.8 0.0 collective-permute-done.1.got_ref
  42.8 0.0 copy-done
  42.8 0.1 shard_map.168
  42.9 0.4 collective-permute-start.3
  43.4 0.8 collective-permute-start.2
  44.2 7.5 %collective-permute-done.2.got_ref = bf16[256,512]{1,0:T(8,128)(2,1)S(1)} collective-permute-done((bf16[256,512]{1,0:T(8,128)(2,1)S(1)}, bf16[256,512]{1,0:T(8,128)(2,1)S(1)}, u32[]{:S(2)}, u32[]{:S(2)}) %collective-permute-start.2) | collective-permute-done | bytes 262176 | tf_op jit(solution)/shard_map/ppermute | solution.py:306
  51.7 1.5 %collective-permute-start.4 = (bf16[128,512]{1,0:T(8,128)(2,1)S(1)}, bf16[128,512]{1,0:T(8,128)(2,1)S(1)}, u32[]{:S(2)}, u32[]{:S(2)}) collective-permute-start(bf16[128,512]{1,0:T(8,128)(2,1)S(1)} %get-tuple-element.53), channel_id=1, source_target_pairs={{0,4},{1,5},{2,6},{3,7},{4,0},{5,1},{6,2},{7,3},{8,12},{9,13},{10,... | collective-permute-start | bytes 393224 | tf_op jit(solution)/shard_map/ppermute | solution.py:306
  53.2 0.0 collective-permute-done.3.got_ref
  53.3 0.5 collective-permute-start.7
  53.8 5.8 %shard_map.171 = bf16[2048,512]{1,0:T(8,128)(2,1)} custom-call(s32[1]{0:T(128)S(6)} %copy.18.count_ref, s32[1,2048]{1,0:T(1,128)} %bitcast.15, bf16[2048,512]{1,0:T(8,128)(2,1)} %get-tuple-element.50.dp_ref, bf16[2048,512]{1,0:T(8,128)(2,1)} %cot_ref.3, bf16[256,512]{1,0:T(8,128)(2,1)} %agg_ref.3, bf16[1536,512]{1,0:T(8,128)(2,1)} %w_r_ref.3), custom_call_target="tpu_custom_call" | custom-call | flops 1610612736 | bytes 6291456 | tf_op jit(solution)/shard_map/pallas_call | solution.py:229
  59.6 0.0 collective-permute-done.4.got_ref
  59.6 1.0 %collective-permute-start.5 = (bf16[128,512]{1,0:T(8,128)(2,1)S(1)}, bf16[128,512]{1,0:T(8,128)(2,1)S(1)}, u32[]{:S(2)}, u32[]{:S(2)}) collective-permute-start(bf16[128,512]{1,0:T(8,128)(2,1)S(1)} %shard_map.172.keep_ref), channel_id=1, source_target_pairs={{0,8},{1,9},{2,10},{3,11},{4,12},{5,13},{6,14},{7,15},{8,0},{9,1},... | collective-permute-start | bytes 393224 | tf_op jit(solution)/shard_map/ppermute | solution.py:306
  60.6 4.4 %all-to-all-start.1 = ((bf16[16,16,512]{2,1,0:T(8,128)(2,1)}), bf16[16,16,512]{2,1,0:T(8,128)(2,1)S(1)}, u32[]{:S(2)}, u32[]{:S(2)}) async-start(bf16[16,16,512]{2,1,0:T(8,128)(2,1)} %bitcast.8), calls=%async_computation.1 | async-start | bytes 524288 | tf_op jit(solution)/shard_map/all_to_all | solution.py:354
  65.0 0.0 collective-permute-done.7.got_ref
  65.1 2.9 %collective-permute-start.8 = (bf16[144,512]{1,0:T(8,128)(2,1)S(1)}, bf16[144,512]{1,0:T(8,128)(2,1)S(1)}, u32[]{:S(2)}, u32[]{:S(2)}) collective-permute-start(bf16[144,512]{1,0:T(8,128)(2,1)S(1)} %shard_map.174.keep_ref), channel_id=1, source_target_pairs={{0,8},{1,9},{2,10},{3,11},{4,12},{5,13},{6,14},{7,15},{8,0},{9,1},... | collective-permute-start | bytes 442376 | tf_op jit(solution)/shard_map/ppermute | solution.py:306
  68.0 0.0 collective-permute-done.5.got_ref
  68.0 1.5 %collective-permute-start.6 = (bf16[128,512]{1,0:T(8,128)(2,1)S(1)}, bf16[128,512]{1,0:T(8,128)(2,1)S(1)}, u32[]{:S(2)}, u32[]{:S(2)}) collective-permute-start(bf16[128,512]{1,0:T(8,128)(2,1)S(1)} %shard_map.173), channel_id=1, source_target_pairs={{0,4},{1,5},{2,6},{3,7},{4,0},{5,1},{6,2},{7,3},{8,12},{9,13},{10,... | collective-permute-start | bytes 393224 | tf_op jit(solution)/shard_map/ppermute | solution.py:306
  69.5 11.5 %collective-permute-done.8.got_ref = bf16[144,512]{1,0:T(8,128)(2,1)S(1)} collective-permute-done((bf16[144,512]{1,0:T(8,128)(2,1)S(1)}, bf16[144,512]{1,0:T(8,128)(2,1)S(1)}, u32[]{:S(2)}, u32[]{:S(2)}) %collective-permute-start.8) | collective-permute-done | bytes 147488 | tf_op jit(solution)/shard_map/ppermute | solution.py:306
  81.1 1.5 %collective-permute-start.9 = (bf16[128,512]{1,0:T(8,128)(2,1)S(1)}, bf16[128,512]{1,0:T(8,128)(2,1)S(1)}, u32[]{:S(2)}, u32[]{:S(2)}) collective-permute-start(bf16[128,512]{1,0:T(8,128)(2,1)S(1)} %slice.8), channel_id=1, source_target_pairs={{0,2},{1,3},{2,0},{3,1},{4,6},{5,7},{6,4},{7,5},{8,10},{9,11},{10,... | collective-permute-start | bytes 393224 | tf_op jit(solution)/shard_map/ppermute | solution.py:306
  82.6 0.0 collective-permute-done.6
  82.6 3.6 %collective-permute-done.9 = bf16[128,512]{1,0:T(8,128)(2,1)S(1)} collective-permute-done((bf16[128,512]{1,0:T(8,128)(2,1)S(1)}, bf16[128,512]{1,0:T(8,128)(2,1)S(1)}, u32[]{:S(2)}, u32[]{:S(2)}) %collective-permute-start.9) | collective-permute-done | bytes 131104 | tf_op jit(solution)/shard_map/ppermute | solution.py:306
  86.2 0.0 all-to-all-done.1
  86.2 0.0 copy-start.2
  86.2 1.5 %collective-permute-start.10 = (bf16[256,512]{1,0:T(8,128)(2,1)S(1)}, bf16[256,512]{1,0:T(8,128)(2,1)S(1)}, u32[]{:S(2)}, u32[]{:S(2)}) collective-permute-start(bf16[256,512]{1,0:T(8,128)(2,1)S(1)} %pad_maximum_fusion.2), channel_id=1, source_target_pairs={{0,2},{1,3},{2,0},{3,1},{4,6},{5,7},{6,4},{7,5},{8,10},{9,11},{10,... | collective-permute-start | bytes 786440 | tf_op jit(solution)/shard_map/ppermute | solution.py:306
  87.7 0.0 collective-permute-start.11
  87.7 0.0 copy-done.2
  87.7 2.7 %shard_map.176 = f32[256,512]{1,0:T(8,128)} custom-call(s32[1,256]{1,0:T(1,128)} %reshape.47.index_ref, bf16[256,512]{1,0:T(8,128)(2,1)} %bitcast.10, bf16[256,512]{1,0:T(8,128)(2,1)} %get-tuple-element.60.sum_r_ref, bf16[1536,512]{1,0:T(8,128)(2,1)} %w_r_ref.3, bf16[1536,512]{1,0:T(8,128)(2,1)} %w_r_ref.3), custom_call_target="tpu_custom_call" | custom-call | flops 335544320 | bytes 2621440 | tf_op jit(solution)/shard_map/pallas_call | solution.py:256
  90.4 2.8 %collective-permute-done.10 = bf16[256,512]{1,0:T(8,128)(2,1)S(1)} collective-permute-done((bf16[256,512]{1,0:T(8,128)(2,1)S(1)}, bf16[256,512]{1,0:T(8,128)(2,1)S(1)}, u32[]{:S(2)}, u32[]{:S(2)}) %collective-permute-start.10) | collective-permute-done | bytes 262176 | tf_op jit(solution)/shard_map/ppermute | solution.py:306
  93.3 1.1 %collective-permute-done.11 = bf16[256,512]{1,0:T(8,128)(2,1)S(1)} collective-permute-done((bf16[256,512]{1,0:T(8,128)(2,1)S(1)}, bf16[256,512]{1,0:T(8,128)(2,1)S(1)}, u32[]{:S(2)}, u32[]{:S(2)}) %collective-permute-start.11) | collective-permute-done | bytes 262176 | tf_op jit(solution)/shard_map/ppermute | solution.py:306
  94.4 0.1 collective-permute-start.12
  94.5 0.5 collective-permute-start.13
  95.0 1.4 %collective-permute-done.12.p1 = bf16[512,512]{1,0:T(8,128)(2,1)S(1)} collective-permute-done((bf16[512,512]{1,0:T(8,128)(2,1)S(1)}, bf16[512,512]{1,0:T(8,128)(2,1)S(1)}, u32[]{:S(2)}, u32[]{:S(2)}) %collective-permute-start.12) | collective-permute-done | bytes 524320 | tf_op jit(solution)/shard_map/ppermute | solution.py:306
  96.4 0.7 collective-permute-done.13.q1
  97.2 1.8 %shard_map.177 = (bf16[1536,512]{1,0:T(8,128)(2,1)}, bf16[512,512]{1,0:T(8,128)(2,1)}, bf16[3,512]{1,0:T(4,128)(2,1)}) custom-call(s32[1]{0:T(128)} %bitcast.me_ref, bf16[512,512]{1,0:T(8,128)(2,1)S(1)} %pad_maximum_fusion.p0, bf16[512,512]{1,0:T(8,128)(2,1)S(1)} %collective-permute-done.12.p1, bf16[512,512]{1,0:T(8,128)(2,1)S(1)} %pad_maximum_fusion.1.q0, ...), custom_call_target="tpu_custom_call" | custom-call | tf_op jit(solution)/shard_map/pallas_call | solution.py:340
  (12 shorter events, 0.3 us)
Async XLA Ops:
  3.9 17.4 %all-to-all-start = ((bf16[16,16,512]{2,1,0:T(8,128)(2,1)}), bf16[16,16,512]{2,1,0:T(8,128)(2,1)S(1)}, u32[]{:S(2)}, u32[]{:S(2)}) async-start(bf16[16,16,512]{2,1,0:T(8,128)(2,1)} %bitcast.11), calls=%async_computation | async-start | bytes 524288 | tf_op jit(solution)/shard_map/all_to_all | solution.py:354
  21.3 0.7 copy-start.3
  38.5 4.3 %copy-start = (f32[528,512]{1,0:T(8,128)S(1)}, f32[528,512]{1,0:T(8,128)}, u32[]{:S(2)}) copy-start(f32[528,512]{1,0:T(8,128)} %get-tuple-element.42.keep_ref) | copy-start | bytes 3244036
  38.5 4.3 %collective-permute-start.1 = (bf16[528,512]{1,0:T(8,128)(2,1)}, bf16[528,512]{1,0:T(8,128)(2,1)S(1)}, u32[]{:S(2)}, u32[]{:S(2)}) collective-permute-start(bf16[528,512]{1,0:T(8,128)(2,1)} %get-tuple-element.43), channel_id=1, source_target_pairs={{0,1},{1,0},{2,3},{3,2},{4,5},{5,4},{6,7},{7,6},{8,9},{9,8},{10,11... | collective-permute-start | bytes 1622024 | tf_op jit(solution)/shard_map/ppermute | solution.py:306
  38.6 2.9 %collective-permute-start = (bf16[512,512]{1,0:T(8,128)(2,1)}, bf16[512,512]{1,0:T(8,128)(2,1)S(1)}, u32[]{:S(2)}, u32[]{:S(2)}) collective-permute-start(bf16[512,512]{1,0:T(8,128)(2,1)} %get-tuple-element.37), channel_id=1, source_target_pairs={{0,1},{1,0},{2,3},{3,2},{4,5},{5,4},{6,7},{7,6},{8,9},{9,8},{10,11... | collective-permute-start | bytes 1572872 | tf_op jit(solution)/shard_map/ppermute | solution.py:306
  41.5 1.2 %copy-start.1 = (f32[512,512]{1,0:T(8,128)S(1)}, f32[512,512]{1,0:T(8,128)}, u32[]{:S(2)}) copy-start(f32[512,512]{1,0:T(8,128)} %get-tuple-element.36.keep_ref) | copy-start | bytes 3145732
  42.9 10.3 %collective-permute-start.3 = (bf16[272,512]{1,0:T(8,128)(2,1)S(1)}, bf16[272,512]{1,0:T(8,128)(2,1)S(1)}, u32[]{:S(2)}, u32[]{:S(2)}) collective-permute-start(bf16[272,512]{1,0:T(8,128)(2,1)S(1)} %get-tuple-element.48), channel_id=1, source_target_pairs={{0,4},{1,5},{2,6},{3,7},{4,0},{5,1},{6,2},{7,3},{8,12},{9,13},{10,... | collective-permute-start | bytes 835592 | tf_op jit(solution)/shard_map/ppermute | solution.py:306
  43.4 8.3 %collective-permute-start.2 = (bf16[256,512]{1,0:T(8,128)(2,1)S(1)}, bf16[256,512]{1,0:T(8,128)(2,1)S(1)}, u32[]{:S(2)}, u32[]{:S(2)}) collective-permute-start(bf16[256,512]{1,0:T(8,128)(2,1)S(1)} %get-tuple-element.45), channel_id=1, source_target_pairs={{0,2},{1,3},{2,0},{3,1},{4,6},{5,7},{6,4},{7,5},{8,10},{9,11},{10,... | collective-permute-start | bytes 786440 | tf_op jit(solution)/shard_map/ppermute | solution.py:306
  51.7 7.9 %collective-permute-start.4 = (bf16[128,512]{1,0:T(8,128)(2,1)S(1)}, bf16[128,512]{1,0:T(8,128)(2,1)S(1)}, u32[]{:S(2)}, u32[]{:S(2)}) collective-permute-start(bf16[128,512]{1,0:T(8,128)(2,1)S(1)} %get-tuple-element.53), channel_id=1, source_target_pairs={{0,4},{1,5},{2,6},{3,7},{4,0},{5,1},{6,2},{7,3},{8,12},{9,13},{10,... | collective-permute-start | bytes 393224 | tf_op jit(solution)/shard_map/ppermute | solution.py:306
  53.3 11.8 %collective-permute-start.7 = (bf16[144,512]{1,0:T(8,128)(2,1)S(1)}, bf16[144,512]{1,0:T(8,128)(2,1)S(1)}, u32[]{:S(2)}, u32[]{:S(2)}) collective-permute-start(bf16[144,512]{1,0:T(8,128)(2,1)S(1)} %get-tuple-element.55), channel_id=1, source_target_pairs={{0,2},{1,3},{2,0},{3,1},{4,6},{5,7},{6,4},{7,5},{8,10},{9,11},{10,... | collective-permute-start | bytes 442376 | tf_op jit(solution)/shard_map/ppermute | solution.py:306
  59.6 8.4 %collective-permute-start.5 = (bf16[128,512]{1,0:T(8,128)(2,1)S(1)}, bf16[128,512]{1,0:T(8,128)(2,1)S(1)}, u32[]{:S(2)}, u32[]{:S(2)}) collective-permute-start(bf16[128,512]{1,0:T(8,128)(2,1)S(1)} %shard_map.172.keep_ref), channel_id=1, source_target_pairs={{0,8},{1,9},{2,10},{3,11},{4,12},{5,13},{6,14},{7,15},{8,0},{9,1},... | collective-permute-start | bytes 393224 | tf_op jit(solution)/shard_map/ppermute | solution.py:306
  60.6 25.6 %all-to-all-start.1 = ((bf16[16,16,512]{2,1,0:T(8,128)(2,1)}), bf16[16,16,512]{2,1,0:T(8,128)(2,1)S(1)}, u32[]{:S(2)}, u32[]{:S(2)}) async-start(bf16[16,16,512]{2,1,0:T(8,128)(2,1)} %bitcast.8), calls=%async_computation.1 | async-start | bytes 524288 | tf_op jit(solution)/shard_map/all_to_all | solution.py:354
  65.1 15.9 %collective-permute-start.8 = (bf16[144,512]{1,0:T(8,128)(2,1)S(1)}, bf16[144,512]{1,0:T(8,128)(2,1)S(1)}, u32[]{:S(2)}, u32[]{:S(2)}) collective-permute-start(bf16[144,512]{1,0:T(8,128)(2,1)S(1)} %shard_map.174.keep_ref), channel_id=1, source_target_pairs={{0,8},{1,9},{2,10},{3,11},{4,12},{5,13},{6,14},{7,15},{8,0},{9,1},... | collective-permute-start | bytes 442376 | tf_op jit(solution)/shard_map/ppermute | solution.py:306
  68.0 14.6 %collective-permute-start.6 = (bf16[128,512]{1,0:T(8,128)(2,1)S(1)}, bf16[128,512]{1,0:T(8,128)(2,1)S(1)}, u32[]{:S(2)}, u32[]{:S(2)}) collective-permute-start(bf16[128,512]{1,0:T(8,128)(2,1)S(1)} %shard_map.173), channel_id=1, source_target_pairs={{0,4},{1,5},{2,6},{3,7},{4,0},{5,1},{6,2},{7,3},{8,12},{9,13},{10,... | collective-permute-start | bytes 393224 | tf_op jit(solution)/shard_map/ppermute | solution.py:306
  81.1 5.1 %collective-permute-start.9 = (bf16[128,512]{1,0:T(8,128)(2,1)S(1)}, bf16[128,512]{1,0:T(8,128)(2,1)S(1)}, u32[]{:S(2)}, u32[]{:S(2)}) collective-permute-start(bf16[128,512]{1,0:T(8,128)(2,1)S(1)} %slice.8), channel_id=1, source_target_pairs={{0,2},{1,3},{2,0},{3,1},{4,6},{5,7},{6,4},{7,5},{8,10},{9,11},{10,... | collective-permute-start | bytes 393224 | tf_op jit(solution)/shard_map/ppermute | solution.py:306
  86.2 1.5 %copy-start.2 = (bf16[16,16,512]{2,1,0:T(8,128)(2,1)}, bf16[16,16,512]{2,1,0:T(8,128)(2,1)S(1)}, u32[]{:S(2)}) copy-start(bf16[16,16,512]{2,1,0:T(8,128)(2,1)S(1)} %all-to-all-done.1) | copy-start | bytes 786436
  86.2 7.0 %collective-permute-start.10 = (bf16[256,512]{1,0:T(8,128)(2,1)S(1)}, bf16[256,512]{1,0:T(8,128)(2,1)S(1)}, u32[]{:S(2)}, u32[]{:S(2)}) collective-permute-start(bf16[256,512]{1,0:T(8,128)(2,1)S(1)} %pad_maximum_fusion.2), channel_id=1, source_target_pairs={{0,2},{1,3},{2,0},{3,1},{4,6},{5,7},{6,4},{7,5},{8,10},{9,11},{10,... | collective-permute-start | bytes 786440 | tf_op jit(solution)/shard_map/ppermute | solution.py:306
  87.7 6.7 %collective-permute-start.11 = (bf16[256,512]{1,0:T(8,128)(2,1)S(1)}, bf16[256,512]{1,0:T(8,128)(2,1)S(1)}, u32[]{:S(2)}, u32[]{:S(2)}) collective-permute-start(bf16[256,512]{1,0:T(8,128)(2,1)S(1)} %pad_maximum_fusion.3), channel_id=1, source_target_pairs={{0,4},{1,5},{2,6},{3,7},{4,0},{5,1},{6,2},{7,3},{8,12},{9,13},{10,... | collective-permute-start | bytes 786440 | tf_op jit(solution)/shard_map/ppermute | solution.py:306
  94.4 2.0 %collective-permute-start.12 = (bf16[512,512]{1,0:T(8,128)(2,1)S(1)}, bf16[512,512]{1,0:T(8,128)(2,1)S(1)}, u32[]{:S(2)}, u32[]{:S(2)}) collective-permute-start(bf16[512,512]{1,0:T(8,128)(2,1)S(1)} %pad_maximum_fusion.p0), channel_id=1, source_target_pairs={{0,1},{1,0},{2,3},{3,2},{4,5},{5,4},{6,7},{7,6},{8,9},{9,8},{10,11... | collective-permute-start | bytes 1572872 | tf_op jit(solution)/shard_map/ppermute | solution.py:306
  94.5 2.6 %collective-permute-start.13 = (bf16[512,512]{1,0:T(8,128)(2,1)S(1)}, bf16[512,512]{1,0:T(8,128)(2,1)S(1)}, u32[]{:S(2)}, u32[]{:S(2)}) collective-permute-start(bf16[512,512]{1,0:T(8,128)(2,1)S(1)} %pad_maximum_fusion.1.q0), channel_id=1, source_target_pairs={{0,1},{1,0},{2,3},{3,2},{4,5},{5,4},{6,7},{7,6},{8,9},{9,8},{10,11... | collective-permute-start | bytes 1572872 | tf_op jit(solution)/shard_map/ppermute | solution.py:306

commit v2 on v1

v2 whole, which is shorter than its diff:
```python
import functools
import math

import jax
import jax.numpy as jnp
from jax import lax
from jax.experimental import pallas as pl
from jax.experimental.pallas import tpu as pltpu
from jax.sharding import PartitionSpec as P

BF = jnp.bfloat16
F32 = jnp.float32
VMEM = pltpu.VMEM
SMEM = pltpu.SMEM
PICK, LOCAL, EDGE, GRAD, SMALL = 60, 60, 48, 60, 16
PARTS = 2
STRIP = 16
EXTRA = 16


def dot(a, b, dims):
    return lax.dot_general(a, b, ((dims[0], dims[1]), ((), ())), preferred_element_type=F32)


NN = ((1,), (0,))
NT = ((1,), (1,))
TN = ((0,), (0,))


def one_hot_t(index_row, count):
    wide = lax.broadcasted_iota(jnp.int32, (count, index_row.shape[1]), 0) == index_row
    return jnp.where(wide, 1.0, 0.0).astype(BF)


def params(limit):
    return pltpu.CompilerParams(vmem_limit_bytes=limit * 1024 * 1024)


def whole(shape):
    return pl.BlockSpec(shape, lambda *i: (0,) * len(shape))


def cost(flops, nbytes):
    return pl.CostEstimate(flops=int(flops), bytes_accessed=int(nbytes), transcendentals=0)


def flat_row(table):
    a, b = table.shape
    lane = lax.broadcasted_iota(jnp.int32, (b, a * b), 1)
    spread = jnp.where(lane % b == lax.broadcasted_iota(jnp.int32, (b, a * b), 0), 1.0, 0.0).astype(BF)
    wide = dot(table.astype(F32).astype(BF), spread, NN)
    lane = lax.broadcasted_iota(jnp.int32, (a, a * b), 1)
    own = lane // b == lax.broadcasted_iota(jnp.int32, (a, a * b), 0)
    return jnp.sum(jnp.where(own, wide, 0.0), axis=0, keepdims=True).astype(jnp.int32)


def pick_kernel(rows_ref, nodes_ref, out_ref):
    hot = one_hot_t(flat_row(rows_ref[...]), nodes_ref.shape[0])
    out_ref[...] = dot(hot, nodes_ref[...], TN).astype(BF)


def pick_rows(send_rows, nodes):
    return pl.pallas_call(
        pick_kernel,
        out_shape=jax.ShapeDtypeStruct((send_rows.size, nodes.shape[1]), BF),
        compiler_params=params(PICK),
    )(send_rows, nodes)


def fetcher(sems):
    used = []

    def fetch(source, target):
        copy = pltpu.make_async_copy(source, target, sems.at[len(used)])
        used.append(copy)
        copy.start()
        return copy

    return fetch


def strips(first, rows):
    return [pl.ds(first + at, STRIP) for at in range(0, rows, STRIP)]


def local_kernel(count_ref, recv_ref, b_ref, edges_hbm, cot_hbm, nodes_hbm, agg_hbm, w_in_hbm, pre_hbm, mc_hbm,
                 edges, cot, nodes, w_e, w_r, pre, mc, table, got, sems):
    total, f = edges.shape
    n = nodes.shape[0]
    rows = total // PARTS
    fetch = fetcher(sems)
    get_nodes = fetch(nodes_hbm, nodes)
    get_w_r = fetch(w_in_hbm.at[pl.ds(2 * f, f)], w_r)
    get_agg = fetch(agg_hbm, table.at[:, pl.ds(f, f)])
    get_w_e = fetch(w_in_hbm.at[pl.ds(0, f)], w_e)
    gets = []
    for part in range(PARTS):
        at = pl.ds(part * rows, rows)
        gets.append((fetch(edges_hbm.at[at], edges.at[at]), fetch(cot_hbm.at[at], cot.at[at])))
    get_nodes.wait()
    get_w_r.wait()
    table[:, :f] = dot(nodes[...], w_r[...], NN).astype(BF)
    get_agg.wait()
    get_w_e.wait()
    puts = []
    for part in range(PARTS):
        at = pl.ds(part * rows, rows)
        hot = one_hot_t(recv_ref[:, part * rows : (part + 1) * rows], n)
        got[...] = dot(hot, table[...], TN)
        gets[part][0].wait()
        pre[at, :] = (dot(edges[at, :], w_e[...], NN) + got[:, :f] + b_ref[...]).astype(BF)
        puts.append(fetch(pre.at[at], pre_hbm.at[at]))
        gets[part][1].wait()
        live = lax.broadcasted_iota(jnp.int32, (rows, f), 0) < count_ref[0] - part * rows
        mc[at, :] = jnp.where(live, cot[at, :].astype(F32) + got[:, f:], 0.0)
        puts.append(fetch(mc.at[at], mc_hbm.at[at]))
    for put in puts:
        put.wait()


def local_part(count, recv_row, edges, edge_cot, nodes, agg, w_in, b_row):
    total, f = edges.shape
    n = nodes.shape[0]
    anywhere = pl.BlockSpec(memory_space=pl.ANY)
    return pl.pallas_call(
        local_kernel,
        in_specs=[
            pl.BlockSpec(memory_space=SMEM),
            pl.BlockSpec(memory_space=VMEM),
            pl.BlockSpec(memory_space=VMEM),
            anywhere,
            anywhere,
            anywhere,
            anywhere,
            anywhere,
        ],
        out_specs=[anywhere, anywhere],
        out_shape=[jax.ShapeDtypeStruct((total, f), BF), jax.ShapeDtypeStruct((total, f), F32)],
        scratch_shapes=[
            VMEM((total, f), BF), VMEM((total, f), BF), VMEM((n, f), BF), VMEM((f, f), BF), VMEM((f, f), BF),
            VMEM((total, f), BF), VMEM((total, f), F32), VMEM((n, 2 * f), BF), VMEM((total // PARTS, 2 * f), F32),
            pltpu.SemaphoreType.DMA((4 + 4 * PARTS,)),
        ],
        compiler_params=params(LOCAL),
        cost_estimate=cost(2 * total * f * (f + 2 * n), 10 * total * f),
    )(count, recv_row, b_row, edges, edge_cot, nodes, agg, w_in)


def slot_of(position, order):
    slot = 0
    for bit, mask in enumerate(reversed(order)):
        if position >> bit & 1:
            slot |= mask
    return slot


def write_slots(me, parts, keep_ref, send_ref, order, first=0):
    pieces = 2 ** len(order)
    home = me & (pieces - 1)
    r = parts[0].shape[0] // pieces
    for position in range(pieces):
        piece = home ^ slot_of(position, order)
        start = pl.multiple_of(piece * r, r)
        half, at = divmod(position, pieces // 2)
        ref = send_ref if half else keep_ref
        for k, acc in enumerate(parts):
            row = first + (at * len(parts) + k) * r
            ref[row : row + r, :] = acc[pl.ds(start, r), :].astype(ref.dtype)


def edge_kernel(order_p, order_q, me_ref, slot_ref, recv_ref, b_ref, gain_ref, edges_hbm, pre_hbm, mc_hbm, nodes_hbm,
                halo_hbm, w_in_hbm, w_out_hbm, dp_hbm, keep_p, send_p, keep_q, send_q, sum_s_ref, sum_r_ref,
                edges, pre, mc, nodes, halo, w_s, w_out, dp, table, hot, wide, slope, act, dn,
                acc_o, acc_e, acc_n, acc_x, acc_y, sems):
    total, f = edges.shape
    slots, n = halo.shape[0], nodes.shape[0]
    rows = total // PARTS
    inverse = 1.0 / f
    fetch = fetcher(sems)
    get_halo = fetch(halo_hbm, halo)
    get_w_s = fetch(w_in_hbm.at[pl.ds(f, f)], w_s)
    get_pre, get_mc, puts = [], [], []
    for part in range(PARTS):
        at = pl.ds(part * rows, rows)
        get_pre.append(fetch(pre_hbm.at[at], pre.at[at]))
        if part == 0:
            get_w_out = fetch(w_out_hbm, w_out)
        get_mc.append(fetch(mc_hbm.at[at], mc.at[at]))
    get_edges = fetch(edges_hbm, edges)
    get_nodes = fetch(nodes_hbm, nodes)
    sum_dn, sum_mn = [], []

    def gather(part):
        at, columns = pl.ds(part * rows, rows), slice(part * rows, (part + 1) * rows)
        hot[:slots, columns] = one_hot_t(slot_ref[:, columns], slots)
        hot[slots:, columns] = one_hot_t(recv_ref[:, columns], n)
        if part == 0:
            table[...] = dot(halo[...], w_s[...], NN).astype(BF)
        wide[at, :] = dot(hot[:slots, columns], table[...], TN)
        for r in strips(part * rows, rows):
            x = pre[r, :].astype(F32) + wide[r, :]
            sig = 0.5 * jnp.tanh(0.5 * x) + 0.5
            silu = x * sig
            act[r, :] = silu.astype(BF)
            slope[r, :] = sig + silu * (1.0 - sig)

    def norm(part):
        at = pl.ds(part * rows, rows)
        wide[at, :] = dot(act[at, :], w_out[...], NN)
        total_dn = total_mn = jnp.zeros((8, f), F32)
        for r in strips(part * rows, rows):
            x = wide[r, :] + b_ref[...]
            centered = x - jnp.sum(x, axis=1, keepdims=True) * inverse
            inv_std = lax.rsqrt(jnp.sum(centered * centered, axis=1, keepdims=True) * inverse + 1e-05)
            normed = centered * inv_std
            cot = mc[r, :]
            scaled = cot * gain_ref[...]
            mean_s = jnp.sum(scaled, axis=1, keepdims=True) * inverse
            mean_sn = jnp.sum(scaled * normed, axis=1, keepdims=True) * inverse
            d = inv_std * (scaled - mean_s - normed * mean_sn)
            dn[r, :] = d.astype(BF)
            total_dn = total_dn + jnp.sum(d.reshape(STRIP // 8, 8, f), axis=0)
            total_mn = total_mn + jnp.sum((cot * normed).reshape(STRIP // 8, 8, f), axis=0)
        sum_dn.append(total_dn)
        sum_mn.append(total_mn)

    def back(part):
        at = pl.ds(part * rows, rows)
        more = dot(act[at, :], dn[at, :], TN)
        acc_o[...] = more if part == 0 else acc_o[...] + more
        wide[at, :] = dot(dn[at, :], w_out[...], NT)
        for r in strips(part * rows, rows):
            dp[r, :] = (wide[r, :] * slope[r, :]).astype(BF)
        puts.append(fetch(dp.at[at], dp_hbm.at[at]))

    def weights(part):
        at, columns = pl.ds(part * rows, rows), slice(part * rows, (part + 1) * rows)
        more = dot(hot[:, columns], dp[at, :], NN)
        acc_n[...] = more if part == 0 else acc_n[...] + more
        more = dot(edges[at, :], dp[at, :], TN)
        acc_e[...] = more if part == 0 else acc_e[...] + more

    stages = (gather, norm, back, weights)
    for turn in range(PARTS + len(stages) - 1):
        if turn == 0:
            for g in [get_halo, get_w_s] + get_pre:
                g.wait()
        if turn == 1:
            for g in [get_w_out, get_edges, get_nodes] + get_mc:
                g.wait()
        for at in range(len(stages) - 1, -1, -1):
            if 0 <= turn - at < PARTS:
                stages[at](turn - at)

    sum_s = acc_n[:slots, :].astype(BF)
    sum_r = acc_n[slots:, :].astype(BF)
    sum_s_ref[...] = sum_s
    sum_r_ref[...] = sum_r
    acc_x[...] = dot(halo[...], sum_s, TN)
    acc_y[...] = dot(nodes[...], sum_r, TN)
    me = me_ref[0]
    write_slots(me, (acc_x, acc_y), keep_p, send_p, order_p)
    write_slots(me, (acc_e, acc_o), keep_q, send_q, order_q, EXTRA)
    row = lax.broadcasted_iota(jnp.int32, (EXTRA // 2, f), 0)
    exact = jnp.where(row == 0, jnp.sum(acc_n[slots:, :], axis=0, keepdims=True), 0.0)
    exact = jnp.where(row == 1, jnp.sum(sum(sum_dn), axis=0, keepdims=True), exact)
    exact = jnp.where(row == 2, jnp.sum(sum(sum_mn), axis=0, keepdims=True), exact)
    high = exact.astype(BF).astype(F32)
    vectors = jnp.concatenate([high, exact - high], axis=0)
    keep_q[:EXTRA, :] = vectors
    send_q[:EXTRA, :] = vectors.astype(BF)
    for put in puts:
        put.wait()


def edge_part(me, slot_row, recv_row, edges, pre, mc, nodes, halo, w_in, w_out, b_row, gain_row, order_p, order_q):
    total, f = edges.shape
    slots, n = halo.shape[0], nodes.shape[0]
    inside = pl.BlockSpec(memory_space=VMEM)
    anywhere = pl.BlockSpec(memory_space=pl.ANY)
    shapes = [
        ((total, f), BF), ((f, f), F32), ((f, f), BF), ((f + EXTRA, f), F32), ((f + EXTRA, f), BF),
        ((slots, f), BF), ((n, f), BF),
    ]
    return pl.pallas_call(
        functools.partial(edge_kernel, order_p, order_q),
        in_specs=[pl.BlockSpec(memory_space=SMEM)] + [inside] * 4 + [anywhere] * 7,
        out_specs=[anywhere] + [inside] * 6,
        out_shape=[jax.ShapeDtypeStruct(s, d) for s, d in shapes],
        scratch_shapes=[
            VMEM((total, f), BF), VMEM((total, f), BF), VMEM((total, f), F32), VMEM((n, f), BF), VMEM((slots, f), BF),
            VMEM((f, f), BF), VMEM((f, f), BF), VMEM((total, f), BF), VMEM((slots, f), BF),
            VMEM((slots + n, total), BF), VMEM((total, f), F32), VMEM((total, f), F32), VMEM((total, f), BF),
            VMEM((total, f), BF), VMEM((f, f), F32), VMEM((f, f), F32), VMEM((slots + n, f), F32),
            VMEM((f, f), F32), VMEM((f, f), F32), pltpu.SemaphoreType.DMA((5 + 3 * PARTS,)),
        ],
        compiler_params=params(EDGE),
        cost_estimate=cost(2 * total * f * (4 * f + 2 * slots + n), 10 * total * f),
    )(me, slot_row, recv_row, b_row, gain_row, edges, pre, mc, nodes, halo, w_in, w_out)


def edge_grad_kernel(dp_ref, mc_ref, w_ref, out_ref):
    out_ref[...] = (mc_ref[...] + dot(dp_ref[...], w_ref[...], NT)).astype(BF)


def edge_grad(dp, mc, w_in, block):
    total, f = dp.shape
    edge_spec = pl.BlockSpec((block, f), lambda i: (i, 0))
    return pl.pallas_call(
        edge_grad_kernel,
        grid=(total // block,),
        in_specs=[edge_spec, edge_spec, pl.BlockSpec((f, f), lambda i: (0, 0))],
        out_specs=edge_spec,
        out_shape=jax.ShapeDtypeStruct((total, f), BF),
        compiler_params=params(GRAD),
        cost_estimate=cost(2 * total * f * f, 8 * total * f),
    )(dp, mc, w_in)


def node_grad_kernel(rows_ref, returned_ref, sum_r_ref, w_s_ref, w_r_ref, out_ref):
    hot = one_hot_t(flat_row(rows_ref[...]), out_ref.shape[0])
    sum_s = dot(hot, returned_ref[...], NN).astype(BF)
    out_ref[...] = dot(sum_s, w_s_ref[...], NT) + dot(sum_r_ref[...], w_r_ref[...], NT)


def node_grad(send_rows, returned, sum_r, w_in):
    n, f = sum_r.shape
    slots = returned.shape[0]
    return pl.pallas_call(
        node_grad_kernel,
        grid=(1,),
        in_specs=[
            whole(send_rows.shape),
            whole((slots, f)),
            whole((n, f)),
            pl.BlockSpec((f, f), lambda i: (1, 0)),
            pl.BlockSpec((f, f), lambda i: (2, 0)),
        ],
        out_specs=whole((n, f)),
        out_shape=jax.ShapeDtypeStruct((n, f), F32),
        compiler_params=params(GRAD),
        cost_estimate=cost(2 * n * f * (slots + 2 * f), 4 * n * f + 8 * f * f),
    )(send_rows, returned, sum_r, w_in, w_in)


def add_split_kernel(extra, keep_ref, got_ref, keep_out, send_out):
    half = keep_out.shape[0] - extra
    total = keep_ref[: extra + half, :] + got_ref[: extra + half, :].astype(F32)
    keep_out[...] = total
    if extra:
        send_out[:extra, :] = total[:extra, :].astype(BF)
    away = keep_ref[extra + half :, :] + got_ref[extra + half :, :].astype(F32)
    send_out[extra:, :] = away.astype(BF)


def add_split(keep, got, extra):
    rows, f = keep.shape
    half = (rows - extra) // 2 + extra
    return pl.pallas_call(
        functools.partial(add_split_kernel, extra),
        out_shape=[jax.ShapeDtypeStruct((half, f), F32), jax.ShapeDtypeStruct((half, f), BF)],
        compiler_params=params(SMALL),
    )(keep, got)


def add_kernel(keep_ref, got_ref, out_ref):
    out_ref[...] = (keep_ref[...].astype(F32) + got_ref[...].astype(F32)).astype(BF)


def add(keep, got):
    return pl.pallas_call(
        add_kernel,
        out_shape=jax.ShapeDtypeStruct(keep.shape, BF),
        compiler_params=params(SMALL),
    )(keep, got)


def swap(x, mask, regions):
    return lax.ppermute(x, "region", [(i, i ^ mask) for i in range(regions)])


def finish_kernel(order_p, order_q, limit, me_ref, p0, p1, q0, q1, vec_ref, w_in_ref, w_out_ref, vec_out):
    f = w_out_ref.shape[1]
    vec = vec_ref[...].astype(F32)
    vec = vec[: EXTRA // 2, :] + vec[EXTRA // 2 :, :]
    squares = jnp.sum(vec * vec, axis=0, keepdims=True)
    for ref in (p0, p1, q0, q1):
        x = ref[...].astype(F32)
        x = x * x
        squares = squares + jnp.sum(jnp.sum(x.reshape(-1, 8, f), axis=0), axis=0, keepdims=True)
    total = jnp.sum(squares, axis=1, keepdims=True)
    scale = jnp.minimum(1.0, limit * lax.rsqrt(total + 1e-06))
    vec_out[...] = (vec[0:3, :] * scale).astype(BF)
    me = me_ref[0]
    targets = [(p0, p1, order_p, ((w_in_ref, f), (w_in_ref, 2 * f))), (q0, q1, order_q, ((w_in_ref, 0), (w_out_ref, 0)))]
    for low, high, order, outs in targets:
        pieces = 2 ** len(order)
        home = me & (pieces - 1)
        r = f // pieces
        for position in range(pieces):
            half, at = divmod(position, pieces // 2)
            piece = home ^ slot_of(position, order)
            for k, (out, offset) in enumerate(outs):
                row = (at * len(outs) + k) * r
                x = (high if half else low)[row : row + r, :].astype(F32)
                start = pl.multiple_of(offset + piece * r, r)
                out[pl.ds(start, r), :] = (x * scale).astype(BF)


def finish(me, p, q, vec, order_p, order_q):
    f = vec.shape[1]
    limit = math.sqrt(4.0 * f * f + 3.0 * f)
    return pl.pallas_call(
        functools.partial(finish_kernel, order_p, order_q, limit),
        in_specs=[pl.BlockSpec(memory_space=SMEM)] + [pl.BlockSpec(memory_space=VMEM)] * 5,
        out_shape=[
            jax.ShapeDtypeStruct((3 * f, f), BF),
            jax.ShapeDtypeStruct((f, f), BF),
            jax.ShapeDtypeStruct((3, f), BF),
        ],
        compiler_params=params(SMALL),
    )(me, *p, *q, vec)


def all_to_all(x, regions):
    rows, f = x.shape
    out = lax.all_to_all(x.reshape(regions, rows // regions, f), "region", split_axis=0, concat_axis=0, tiled=True)
    return out.reshape(rows, f)


def body(nodes, edges, edge_cot, agg_cot, w_in, b_in, w_out, b_out, gain, send_rows, edge_slot, edge_receiver, edge_count):
    regions = lax.axis_size("region")
    f = edges.shape[1]
    me = lax.axis_index("region").astype(jnp.int32).reshape(1)
    masks = [2**k for k in range(regions.bit_length() - 1)]
    last = masks[-1]
    order_p = masks[:-1]
    order_q = order_p[:1] + order_p[1:][::-1]
    slot_row = edge_slot.reshape(1, -1)
    recv_row = edge_receiver.reshape(1, -1)
    after = lax.optimization_barrier

    halo = all_to_all(pick_rows(send_rows, nodes), regions)
    pre, mc = local_part(edge_count, recv_row, edges, edge_cot, nodes, agg_cot, w_in, b_in.reshape(1, f))
    dp, keep_p, send_p, keep_q, send_q, sum_s, sum_r = edge_part(
        me, slot_row, recv_row, edges, pre, mc, nodes, halo, w_in, w_out,
        b_out.reshape(1, f), gain.reshape(1, f), order_p, order_q
    )

    steps = len(order_p)
    for step in range(steps):
        got_p = swap(send_p, order_p[step], regions)
        got_q = swap(send_q, order_q[step], regions)
        if step == 1:
            got_p, got_q, returned = after((got_p, got_q, returned))
        if step < steps - 1:
            keep_p, send_p = add_split(keep_p, got_p, 0)
            keep_q, send_q = add_split(keep_q, got_q, EXTRA)
        else:
            keep_p, keep_q = add(keep_p, got_p), add(keep_q, got_q)
        if step == 0:
            sum_s, send_p, send_q = after((sum_s, send_p, send_q))
            returned = all_to_all(sum_s, regions)
    got_p = swap(keep_p, last, regions)
    got_q = swap(keep_q, last, regions)
    keep_p, keep_q, dp, sum_r = after((keep_p, keep_q, dp, sum_r))
    grad_edges = edge_grad(dp, mc, w_in, 512)
    grad_nodes = node_grad(send_rows, returned, sum_r, w_in)
    got_p, got_q, grad_edges, grad_nodes = after((got_p, got_q, grad_edges, grad_nodes))
    part_p = add(keep_p, got_p)
    part_q = add(keep_q, got_q)
    vec, part_q = part_q[:EXTRA], part_q[EXTRA:]
    for step in range(steps - 1, -1, -1):
        got_p = swap(part_p, order_p[step], regions)
        got_q = swap(part_q, order_q[step], regions)
        if step:
            part_p = jnp.concatenate([part_p, got_p], axis=0)
            part_q = jnp.concatenate([part_q, got_q], axis=0)
    grad_w_in, grad_w_out, grad_vectors = finish(me, (part_p, got_p), (part_q, got_q), vec, order_p, order_q)
    return (grad_edges, grad_nodes, grad_w_in, grad_w_out, grad_vectors)


def solution(mesh):
    split = P(("rep", "region"), None)
    return jax.shard_map(
        body,
        mesh=mesh,
        in_specs=(split, split, split, split, P(), P(), P(), P(), P(), P("region", None), P("region"), P("region"), P("region")),
        out_specs=(split, split, P("rep", None), P("rep", None), P("rep", None)),
        check_vma=False,
    )
```

time: 99.6 us -> 90.8 us (0.912)
  waiting for transfers between devices: 35.4 us -> 29.3 us
  local copies, waits for them, and re-layouts: 3.29 us -> 0.06 us
  starting transfers between devices: 24.6 us -> 26.1 us
    ppermute x14, waiting for transfers between devices: 31 us -> 27.3 us  [swap(): return lax.ppermute(x, 'region', [(i, i ^ mask) for i in range(regions)])]
    all_to_all x2, waiting for transfers between devices: 4.41 us -> 2.01 us  [all_to_all(): lax.all_to_all(x.reshape(regions, rows // regions, f), 'region', split_ax...]
    unnamed x8 -> x16, local copies, waits for them, and re-layouts: 1.94 us -> 0.05 us
    ppermute x14, starting transfers between devices: 12.8 us -> 14.7 us  [swap(): return lax.ppermute(x, 'region', [(i, i ^ mask) for i in range(regions)])]
    reshape x1 -> x0, local copies, waits for them, and re-layouts: 1.34 us -> none  [body(): index_row = send_rows.reshape(1, -1)]
  transfers between devices with their start and end apart: 16 -> 16, of which waited for: 9 -> 11; matrix products, arithmetic and copies ran while one was open for 0% -> 0% of each run, Pallas kernels for 14% -> 18%
where the time goes in v2:
time: 90.8 us; the launch traced here: 90.4 us
  Pallas kernels  33.2 us (37%)
  waiting for transfers between devices  29.3 us (32%)
  starting transfers between devices  26.1 us (29%)
  between operations  1.53 us (2%)
    ppermute x14, waiting for transfers between devices, swap(): return lax.ppermute(x, 'region', [(i, i ^ mask) for i in range(regions)])  27.3 us
    ppermute x14, starting transfers between devices, swap(): return lax.ppermute(x, 'region', [(i, i ^ mask) for i in range(regions)])  14.7 us
    pallas_call x1, Pallas kernels, edge_part(): pl.pallas_call(functools.partial(edge_kernel, order_p, order_q), in_specs...  13.1 us
    all_to_all x2, starting transfers between devices, all_to_all(): lax.all_to_all(x.reshape(regions, rows // regions, f), 'region', split_ax...  11.4 us
    pallas_call x1, Pallas kernels, local_part(): pl.pallas_call(local_kernel, in_specs=[pl.BlockSpec(memory_space=SMEM), p...  7.31 us
    pallas_call x1, Pallas kernels, edge_grad(): pl.pallas_call(edge_grad_kernel, grid=(total // block,), in_specs=[edge_s...  5.76 us
    pallas_call x1, Pallas kernels, node_grad(): pl.pallas_call(node_grad_kernel, grid=(1,), in_specs=[whole(send_rows.sha...  2.77 us
    pallas_call x1, Pallas kernels, pick_rows(): pl.pallas_call(pick_kernel, out_shape=jax.ShapeDtypeStruct((send_rows.siz...  2.05 us
  transfers between devices with their start and end apart: 16, of which 11 were waited for; matrix products, arithmetic and copies ran while one was open for 0% of the time, Pallas kernels for 18%

profile of v2, /device:TPU:0, one launch (start us, length us, event | category | flops | bytes accessed | tf_op | source)
XLA Modules:
  0.0 90.4 jit_solution(7981842413674940286)
XLA Ops:
  0.6 2.1 %shard_map.165 = bf16[256,512]{1,0:T(8,128)(2,1)} custom-call(s32[16,16]{1,0:T(8,128)} %rows_ref.3, bf16[256,512]{1,0:T(8,128)(2,1)} %nodes_hbm.3), custom_call_target="tpu_custom_call" | custom-call | tf_op jit(solution)/shard_map/pallas_call | solution.py:63
  2.7 7.4 %all-to-all-start = ((bf16[16,16,512]{2,1,0:T(8,128)(2,1)}), bf16[16,16,512]{2,1,0:T(8,128)(2,1)S(1)}, u32[]{:S(2)}, u32[]{:S(2)}) async-start(bf16[16,16,512]{2,1,0:T(8,128)(2,1)} %bitcast.17), calls=%async_computation | async-start | bytes 524288 | tf_op jit(solution)/shard_map/all_to_all | solution.py:427
  10.7 0.0 copy-start.1
  10.7 0.0 copy-start.2
  10.8 0.0 copy-start.3
  10.8 0.0 copy-start.4
  10.8 0.0 copy-start.5
  10.8 0.0 copy-start.6
  10.8 7.3 %shard_map.164 = (bf16[2048,512]{1,0:T(8,128)(2,1)}, f32[2048,512]{1,0:T(8,128)}) custom-call(s32[1]{0:T(128)S(6)} %copy.18.count_ref, s32[1,2048]{1,0:T(1,128)} %bitcast.12, f32[1,512]{1,0:T(1,128)} %bitcast.18, bf16[2048,512]{1,0:T(8,128)(2,1)} %edges_hbm.3, bf16[2048,512]{1,0:T(8,128)(2,1)} %cot_hbm.1, bf16[256,512]{1,0:T(8,128)(2,1)} %nodes_hbm.3, ...), custom_call_target="tpu_custom_call" | custom-call | flops 2147483648 | bytes 10485760 | tf_op jit(solution)/shard_map/pallas_call | solution.py:125
  18.1 2.0 %all-to-all-done = bf16[16,16,512]{2,1,0:T(8,128)(2,1)S(1)} async-done(((bf16[16,16,512]{2,1,0:T(8,128)(2,1)}), bf16[16,16,512]{2,1,0:T(8,128)(2,1)S(1)}, u32[]{:S(2)}, u32[]{:S(2)}) %all-to-all-start) | async-done | bytes 262176 | tf_op jit(solution)/shard_map/all_to_all | solution.py:427
  20.1 0.0 copy-done.1
  20.1 0.0 copy-done.2
  20.1 0.0 copy-done.3
  20.1 0.0 copy-done.4
  20.2 0.0 copy-done.5
  20.2 0.0 copy-done.6
  20.2 13.1 %shard_map.166 = (bf16[2048,512]{1,0:T(8,128)(2,1)}, f32[512,512]{1,0:T(8,128)S(1)}, bf16[512,512]{1,0:T(8,128)(2,1)S(1)}, f32[528,512]{1,0:T(8,128)S(1)}, bf16[...) custom-call(s32[1]{0:T(128)} %bitcast.me_ref, s32[1,2048]{1,0:T(1,128)S(1)} %bitcast.11, ...), custom_call_target="tpu_custom_call" | custom-call | flops 5905580032 | bytes 10485760 | tf_op jit(solution)/shard_map/pallas_call | solution.py:285
  33.3 0.0 copy-start
  33.3 0.1 collective-permute-start.1
  33.4 0.5 collective-permute-start
  33.9 2.2 %collective-permute-done.got_ref = bf16[512,512]{1,0:T(8,128)(2,1)S(1)} collective-permute-done((bf16[512,512]{1,0:T(8,128)(2,1)S(1)}, bf16[512,512]{1,0:T(8,128)(2,1)S(1)}, u32[]{:S(2)}, u32[]{:S(2)}) %collective-permute-start) | collective-permute-done | bytes 524320 | tf_op jit(solution)/shard_map/ppermute | solution.py:379
  36.1 0.1 shard_map.167
  36.1 0.0 collective-permute-done.1.got_ref
  36.2 0.1 shard_map.168
  36.3 0.0 copy-done
  36.3 4.0 %all-to-all-start.1 = ((bf16[16,16,512]{2,1,0:T(8,128)(2,1)}), bf16[16,16,512]{2,1,0:T(8,128)(2,1)S(1)}, u32[]{:S(2)}, u32[]{:S(2)}) async-start(bf16[16,16,512]{2,1,0:T(8,128)(2,1)} %bitcast.8), calls=%async_computation.1 | async-start | bytes 524288 | tf_op jit(solution)/shard_map/all_to_all | solution.py:427
  40.3 2.0 %collective-permute-start.3 = (bf16[272,512]{1,0:T(8,128)(2,1)S(1)}, bf16[272,512]{1,0:T(8,128)(2,1)S(1)}, u32[]{:S(2)}, u32[]{:S(2)}) collective-permute-start(bf16[272,512]{1,0:T(8,128)(2,1)S(1)} %get-tuple-element.50), channel_id=1, source_target_pairs={{0,4},{1,5},{2,6},{3,7},{4,0},{5,1},{6,2},{7,3},{8,12},{9,13},{10,... | collective-permute-start | bytes 835592 | tf_op jit(solution)/shard_map/ppermute | solution.py:379
  42.3 1.5 %collective-permute-start.2 = (bf16[256,512]{1,0:T(8,128)(2,1)S(1)}, bf16[256,512]{1,0:T(8,128)(2,1)S(1)}, u32[]{:S(2)}, u32[]{:S(2)}) collective-permute-start(bf16[256,512]{1,0:T(8,128)(2,1)S(1)} %get-tuple-element.49), channel_id=1, source_target_pairs={{0,2},{1,3},{2,0},{3,1},{4,6},{5,7},{6,4},{7,5},{8,10},{9,11},{10,... | collective-permute-start | bytes 786440 | tf_op jit(solution)/shard_map/ppermute | solution.py:379
  43.8 8.5 %collective-permute-done.2.got_ref = bf16[256,512]{1,0:T(8,128)(2,1)S(1)} collective-permute-done((bf16[256,512]{1,0:T(8,128)(2,1)S(1)}, bf16[256,512]{1,0:T(8,128)(2,1)S(1)}, u32[]{:S(2)}, u32[]{:S(2)}) %collective-permute-start.2) | collective-permute-done | bytes 262176 | tf_op jit(solution)/shard_map/ppermute | solution.py:379
  52.2 1.4 %collective-permute-done.3.got_ref = bf16[272,512]{1,0:T(8,128)(2,1)S(1)} collective-permute-done((bf16[272,512]{1,0:T(8,128)(2,1)S(1)}, bf16[272,512]{1,0:T(8,128)(2,1)S(1)}, u32[]{:S(2)}, u32[]{:S(2)}) %collective-permute-start.3) | collective-permute-done | bytes 278560 | tf_op jit(solution)/shard_map/ppermute | solution.py:379
  53.6 0.0 all-to-all-done.1
  53.6 0.0 copy-start.7
  53.7 1.5 %collective-permute-start.6 = (bf16[144,512]{1,0:T(8,128)(2,1)S(1)}, bf16[144,512]{1,0:T(8,128)(2,1)S(1)}, u32[]{:S(2)}, u32[]{:S(2)}) collective-permute-start(bf16[144,512]{1,0:T(8,128)(2,1)S(1)} %get-tuple-element.58), channel_id=1, source_target_pairs={{0,2},{1,3},{2,0},{3,1},{4,6},{5,7},{6,4},{7,5},{8,10},{9,11},{10,... | collective-permute-start | bytes 442376 | tf_op jit(solution)/shard_map/ppermute | solution.py:379
  55.3 0.6 collective-permute-start.4
  55.9 3.3 %collective-permute-done.6.got_ref = bf16[144,512]{1,0:T(8,128)(2,1)S(1)} collective-permute-done((bf16[144,512]{1,0:T(8,128)(2,1)S(1)}, bf16[144,512]{1,0:T(8,128)(2,1)S(1)}, u32[]{:S(2)}, u32[]{:S(2)}) %collective-permute-start.6) | collective-permute-done | bytes 147488 | tf_op jit(solution)/shard_map/ppermute | solution.py:379
  59.2 2.4 %collective-permute-start.7 = (bf16[144,512]{1,0:T(8,128)(2,1)S(1)}, bf16[144,512]{1,0:T(8,128)(2,1)S(1)}, u32[]{:S(2)}, u32[]{:S(2)}) collective-permute-start(bf16[144,512]{1,0:T(8,128)(2,1)S(1)} %shard_map.172.keep_ref), channel_id=1, source_target_pairs={{0,8},{1,9},{2,10},{3,11},{4,12},{5,13},{6,14},{7,15},{8,0},{9,1},... | collective-permute-start | bytes 442376 | tf_op jit(solution)/shard_map/ppermute | solution.py:379
  61.6 0.0 collective-permute-done.4.got_ref
  61.6 1.3 %collective-permute-start.5 = (bf16[128,512]{1,0:T(8,128)(2,1)S(1)}, bf16[128,512]{1,0:T(8,128)(2,1)S(1)}, u32[]{:S(2)}, u32[]{:S(2)}) collective-permute-start(bf16[128,512]{1,0:T(8,128)(2,1)S(1)} %shard_map.170.keep_ref), channel_id=1, source_target_pairs={{0,8},{1,9},{2,10},{3,11},{4,12},{5,13},{6,14},{7,15},{8,0},{9,1},... | collective-permute-start | bytes 393224 | tf_op jit(solution)/shard_map/ppermute | solution.py:379
  62.9 0.0 copy-done.7
  62.9 2.8 %shard_map.174 = f32[256,512]{1,0:T(8,128)} custom-call(s32[16,16]{1,0:T(8,128)} %rows_ref.3, bf16[256,512]{1,0:T(8,128)(2,1)} %bitcast.16, bf16[256,512]{1,0:T(8,128)(2,1)} %copy-done, bf16[1536,512]{1,0:T(8,128)(2,1)} %w_r_ref.1, bf16[1536,512]{1,0:T(8,128)(2,1)} %w_r_ref.1), custom_call_target="tpu_custom_call" | custom-call | flops 335544320 | bytes 2621440 | tf_op jit(solution)/shard_map/pallas_call | solution.py:329
  65.7 5.8 %shard_map.173 = bf16[2048,512]{1,0:T(8,128)(2,1)} custom-call(bf16[2048,512]{1,0:T(8,128)(2,1)} %get-tuple-element.61.dp_ref, f32[2048,512]{1,0:T(8,128)} %get-tuple-element.40.mc_hbm.mc_ref, bf16[1536,512]{1,0:T(8,128)(2,1)} %w_r_ref.1), custom_call_target="tpu_custom_call" | custom-call | flops 1073741824 | bytes 8388608 | tf_op jit(solution)/shard_map/pallas_call | solution.py:309
  71.4 2.0 %collective-permute-done.5.got_ref = bf16[128,512]{1,0:T(8,128)(2,1)S(1)} collective-permute-done((bf16[128,512]{1,0:T(8,128)(2,1)S(1)}, bf16[128,512]{1,0:T(8,128)(2,1)S(1)}, u32[]{:S(2)}, u32[]{:S(2)}) %collective-permute-start.5) | collective-permute-done | bytes 131104 | tf_op jit(solution)/shard_map/ppermute | solution.py:379
  73.4 0.0 collective-permute-done.7.got_ref
  73.5 0.1 collective-permute-start.8
  73.6 1.5 %collective-permute-start.11 = (bf16[128,512]{1,0:T(8,128)(2,1)S(1)}, bf16[128,512]{1,0:T(8,128)(2,1)S(1)}, u32[]{:S(2)}, u32[]{:S(2)}) collective-permute-start(bf16[128,512]{1,0:T(8,128)(2,1)S(1)} %slice.8), channel_id=1, source_target_pairs={{0,2},{1,3},{2,0},{3,1},{4,6},{5,7},{6,4},{7,5},{8,10},{9,11},{10,... | collective-permute-start | bytes 393224 | tf_op jit(solution)/shard_map/ppermute | solution.py:379
  75.1 3.4 %collective-permute-done.8 = bf16[128,512]{1,0:T(8,128)(2,1)S(1)} collective-permute-done((bf16[128,512]{1,0:T(8,128)(2,1)S(1)}, bf16[128,512]{1,0:T(8,128)(2,1)S(1)}, u32[]{:S(2)}, u32[]{:S(2)}) %collective-permute-start.8) | collective-permute-done | bytes 131104 | tf_op jit(solution)/shard_map/ppermute | solution.py:379
  78.5 1.5 %collective-permute-start.9 = (bf16[256,512]{1,0:T(8,128)(2,1)S(1)}, bf16[256,512]{1,0:T(8,128)(2,1)S(1)}, u32[]{:S(2)}, u32[]{:S(2)}) collective-permute-start(bf16[256,512]{1,0:T(8,128)(2,1)S(1)} %pad_maximum_fusion.2), channel_id=1, source_target_pairs={{0,2},{1,3},{2,0},{3,1},{4,6},{5,7},{6,4},{7,5},{8,10},{9,11},{10,... | collective-permute-start | bytes 786440 | tf_op jit(solution)/shard_map/ppermute | solution.py:379
  80.0 0.0 collective-permute-done.11
  80.1 1.6 %collective-permute-start.12 = (bf16[256,512]{1,0:T(8,128)(2,1)S(1)}, bf16[256,512]{1,0:T(8,128)(2,1)S(1)}, u32[]{:S(2)}, u32[]{:S(2)}) collective-permute-start(bf16[256,512]{1,0:T(8,128)(2,1)S(1)} %pad_maximum_fusion.3), channel_id=1, source_target_pairs={{0,4},{1,5},{2,6},{3,7},{4,0},{5,1},{6,2},{7,3},{8,12},{9,13},{10,... | collective-permute-start | bytes 786440 | tf_op jit(solution)/shard_map/ppermute | solution.py:379
  81.6 3.3 %collective-permute-done.9 = bf16[256,512]{1,0:T(8,128)(2,1)S(1)} collective-permute-done((bf16[256,512]{1,0:T(8,128)(2,1)S(1)}, bf16[256,512]{1,0:T(8,128)(2,1)S(1)}, u32[]{:S(2)}, u32[]{:S(2)}) %collective-permute-start.9) | collective-permute-done | bytes 262176 | tf_op jit(solution)/shard_map/ppermute | solution.py:379
  85.0 0.1 collective-permute-start.10
  85.1 1.4 %collective-permute-done.12 = bf16[256,512]{1,0:T(8,128)(2,1)S(1)} collective-permute-done((bf16[256,512]{1,0:T(8,128)(2,1)S(1)}, bf16[256,512]{1,0:T(8,128)(2,1)S(1)}, u32[]{:S(2)}, u32[]{:S(2)}) %collective-permute-start.12) | collective-permute-done | bytes 262176 | tf_op jit(solution)/shard_map/ppermute | solution.py:379
  86.5 0.1 collective-permute-start.13
  86.6 0.3 collective-permute-done.10.p1
  87.0 1.5 %collective-permute-done.13.q1 = bf16[512,512]{1,0:T(8,128)(2,1)S(1)} collective-permute-done((bf16[512,512]{1,0:T(8,128)(2,1)S(1)}, bf16[512,512]{1,0:T(8,128)(2,1)S(1)}, u32[]{:S(2)}, u32[]{:S(2)}) %collective-permute-start.13) | collective-permute-done | bytes 524320 | tf_op jit(solution)/shard_map/ppermute | solution.py:379
  88.5 1.8 %shard_map.177 = (bf16[1536,512]{1,0:T(8,128)(2,1)}, bf16[512,512]{1,0:T(8,128)(2,1)}, bf16[3,512]{1,0:T(4,128)(2,1)}) custom-call(s32[1]{0:T(128)} %bitcast.me_ref, bf16[512,512]{1,0:T(8,128)(2,1)S(1)} %pad_maximum_fusion.p0, bf16[512,512]{1,0:T(8,128)(2,1)S(1)} %collective-permute-done.10.p1, bf16[512,512]{1,0:T(8,128)(2,1)S(1)} %pad_maximum_fusion.1.q0, ...), custom_call_target="tpu_custom_call" | custom-call | tf_op jit(solution)/shard_map/pallas_call | solution.py:413
  (12 shorter events, 0.3 us)
Async XLA Ops:
  2.7 17.4 %all-to-all-start = ((bf16[16,16,512]{2,1,0:T(8,128)(2,1)}), bf16[16,16,512]{2,1,0:T(8,128)(2,1)S(1)}, u32[]{:S(2)}, u32[]{:S(2)}) async-start(bf16[16,16,512]{2,1,0:T(8,128)(2,1)} %bitcast.17), calls=%async_computation | async-start | bytes 524288 | tf_op jit(solution)/shard_map/all_to_all | solution.py:427
  10.7 9.4 %copy-start.1 = (bf16[256,512]{1,0:T(8,128)(2,1)S(1)}, bf16[256,512]{1,0:T(8,128)(2,1)}, u32[]{:S(2)}) copy-start(bf16[256,512]{1,0:T(8,128)(2,1)} %nodes_hbm.3) | copy-start | bytes 786436
  10.7 9.4 %copy-start.2 = (bf16[512,512]{1,0:T(8,128)(2,1)S(1)}, bf16[512,512]{1,0:T(8,128)(2,1)}, u32[]{:S(2)}) copy-start(bf16[512,512]{1,0:T(8,128)(2,1)} %w_out_hbm.1) | copy-start | bytes 1572868
  10.8 9.4 %copy-start.3 = (s32[2048]{0:T(1024)S(1)}, s32[2048]{0:T(1024)}, u32[]{:S(2)}) copy-start(s32[2048]{0:T(1024)} %param.23) | copy-start | bytes 24580
  10.8 9.4 %copy-start.4 = (s32[2048]{0:T(1024)S(1)}, s32[2048]{0:T(1024)}, u32[]{:S(2)}) copy-start(s32[2048]{0:T(1024)} %param.24) | copy-start | bytes 24580
  10.8 9.4 %copy-start.5 = (f32[512]{0:T(512)S(1)}, f32[512]{0:T(512)}, u32[]{:S(2)}) copy-start(f32[512]{0:T(512)} %param.20) | copy-start | bytes 6148
  10.8 9.4 %copy-start.6 = (f32[512]{0:T(512)S(1)}, f32[512]{0:T(512)}, u32[]{:S(2)}) copy-start(f32[512]{0:T(512)} %param.21) | copy-start | bytes 6148
  33.3 3.0 %copy-start = (bf16[256,512]{1,0:T(8,128)(2,1)}, bf16[256,512]{1,0:T(8,128)(2,1)S(1)}, u32[]{:S(2)}) copy-start(bf16[256,512]{1,0:T(8,128)(2,1)S(1)} %get-tuple-element.63.sum_r_ref) | copy-start | bytes 786436
  33.3 2.8 %collective-permute-start.1 = (bf16[528,512]{1,0:T(8,128)(2,1)S(1)}, bf16[528,512]{1,0:T(8,128)(2,1)S(1)}, u32[]{:S(2)}, u32[]{:S(2)}) collective-permute-start(bf16[528,512]{1,0:T(8,128)(2,1)S(1)} %get-tuple-element.47), channel_id=1, source_target_pairs={{0,1},{1,0},{2,3},{3,2},{4,5},{5,4},{6,7},{7,6},{8,9},{9,8},{10,11... | collective-permute-start | bytes 1622024 | tf_op jit(solution)/shard_map/ppermute | solution.py:379
  33.4 2.7 %collective-permute-start = (bf16[512,512]{1,0:T(8,128)(2,1)S(1)}, bf16[512,512]{1,0:T(8,128)(2,1)S(1)}, u32[]{:S(2)}, u32[]{:S(2)}) collective-permute-start(bf16[512,512]{1,0:T(8,128)(2,1)S(1)} %get-tuple-element.42), channel_id=1, source_target_pairs={{0,1},{1,0},{2,3},{3,2},{4,5},{5,4},{6,7},{7,6},{8,9},{9,8},{10,11... | collective-permute-start | bytes 1572872 | tf_op jit(solution)/shard_map/ppermute | solution.py:379
  36.3 17.4 %all-to-all-start.1 = ((bf16[16,16,512]{2,1,0:T(8,128)(2,1)}), bf16[16,16,512]{2,1,0:T(8,128)(2,1)S(1)}, u32[]{:S(2)}, u32[]{:S(2)}) async-start(bf16[16,16,512]{2,1,0:T(8,128)(2,1)} %bitcast.8), calls=%async_computation.1 | async-start | bytes 524288 | tf_op jit(solution)/shard_map/all_to_all | solution.py:427
  40.3 13.3 %collective-permute-start.3 = (bf16[272,512]{1,0:T(8,128)(2,1)S(1)}, bf16[272,512]{1,0:T(8,128)(2,1)S(1)}, u32[]{:S(2)}, u32[]{:S(2)}) collective-permute-start(bf16[272,512]{1,0:T(8,128)(2,1)S(1)} %get-tuple-element.50), channel_id=1, source_target_pairs={{0,4},{1,5},{2,6},{3,7},{4,0},{5,1},{6,2},{7,3},{8,12},{9,13},{10,... | collective-permute-start | bytes 835592 | tf_op jit(solution)/shard_map/ppermute | solution.py:379
  42.3 9.9 %collective-permute-start.2 = (bf16[256,512]{1,0:T(8,128)(2,1)S(1)}, bf16[256,512]{1,0:T(8,128)(2,1)S(1)}, u32[]{:S(2)}, u32[]{:S(2)}) collective-permute-start(bf16[256,512]{1,0:T(8,128)(2,1)S(1)} %get-tuple-element.49), channel_id=1, source_target_pairs={{0,2},{1,3},{2,0},{3,1},{4,6},{5,7},{6,4},{7,5},{8,10},{9,11},{10,... | collective-permute-start | bytes 786440 | tf_op jit(solution)/shard_map/ppermute | solution.py:379
  53.6 9.3 %copy-start.7 = (bf16[16,16,512]{2,1,0:T(8,128)(2,1)}, bf16[16,16,512]{2,1,0:T(8,128)(2,1)S(1)}, u32[]{:S(2)}) copy-start(bf16[16,16,512]{2,1,0:T(8,128)(2,1)S(1)} %all-to-all-done.1) | copy-start | bytes 786436
  53.7 5.5 %collective-permute-start.6 = (bf16[144,512]{1,0:T(8,128)(2,1)S(1)}, bf16[144,512]{1,0:T(8,128)(2,1)S(1)}, u32[]{:S(2)}, u32[]{:S(2)}) collective-permute-start(bf16[144,512]{1,0:T(8,128)(2,1)S(1)} %get-tuple-element.58), channel_id=1, source_target_pairs={{0,2},{1,3},{2,0},{3,1},{4,6},{5,7},{6,4},{7,5},{8,10},{9,11},{10,... | collective-permute-start | bytes 442376 | tf_op jit(solution)/shard_map/ppermute | solution.py:379
  55.3 6.4 %collective-permute-start.4 = (bf16[128,512]{1,0:T(8,128)(2,1)S(1)}, bf16[128,512]{1,0:T(8,128)(2,1)S(1)}, u32[]{:S(2)}, u32[]{:S(2)}) collective-permute-start(bf16[128,512]{1,0:T(8,128)(2,1)S(1)} %get-tuple-element.54), channel_id=1, source_target_pairs={{0,4},{1,5},{2,6},{3,7},{4,0},{5,1},{6,2},{7,3},{8,12},{9,13},{10,... | collective-permute-start | bytes 393224 | tf_op jit(solution)/shard_map/ppermute | solution.py:379
  59.2 14.2 %collective-permute-start.7 = (bf16[144,512]{1,0:T(8,128)(2,1)S(1)}, bf16[144,512]{1,0:T(8,128)(2,1)S(1)}, u32[]{:S(2)}, u32[]{:S(2)}) collective-permute-start(bf16[144,512]{1,0:T(8,128)(2,1)S(1)} %shard_map.172.keep_ref), channel_id=1, source_target_pairs={{0,8},{1,9},{2,10},{3,11},{4,12},{5,13},{6,14},{7,15},{8,0},{9,1},... | collective-permute-start | bytes 442376 | tf_op jit(solution)/shard_map/ppermute | solution.py:379
  61.6 11.8 %collective-permute-start.5 = (bf16[128,512]{1,0:T(8,128)(2,1)S(1)}, bf16[128,512]{1,0:T(8,128)(2,1)S(1)}, u32[]{:S(2)}, u32[]{:S(2)}) collective-permute-start(bf16[128,512]{1,0:T(8,128)(2,1)S(1)} %shard_map.170.keep_ref), channel_id=1, source_target_pairs={{0,8},{1,9},{2,10},{3,11},{4,12},{5,13},{6,14},{7,15},{8,0},{9,1},... | collective-permute-start | bytes 393224 | tf_op jit(solution)/shard_map/ppermute | solution.py:379
  73.5 5.0 %collective-permute-start.8 = (bf16[128,512]{1,0:T(8,128)(2,1)S(1)}, bf16[128,512]{1,0:T(8,128)(2,1)S(1)}, u32[]{:S(2)}, u32[]{:S(2)}) collective-permute-start(bf16[128,512]{1,0:T(8,128)(2,1)S(1)} %shard_map.175), channel_id=1, source_target_pairs={{0,4},{1,5},{2,6},{3,7},{4,0},{5,1},{6,2},{7,3},{8,12},{9,13},{10,... | collective-permute-start | bytes 393224 | tf_op jit(solution)/shard_map/ppermute | solution.py:379
  73.6 6.4 %collective-permute-start.11 = (bf16[128,512]{1,0:T(8,128)(2,1)S(1)}, bf16[128,512]{1,0:T(8,128)(2,1)S(1)}, u32[]{:S(2)}, u32[]{:S(2)}) collective-permute-start(bf16[128,512]{1,0:T(8,128)(2,1)S(1)} %slice.8), channel_id=1, source_target_pairs={{0,2},{1,3},{2,0},{3,1},{4,6},{5,7},{6,4},{7,5},{8,10},{9,11},{10,... | collective-permute-start | bytes 393224 | tf_op jit(solution)/shard_map/ppermute | solution.py:379
  78.5 6.4 %collective-permute-start.9 = (bf16[256,512]{1,0:T(8,128)(2,1)S(1)}, bf16[256,512]{1,0:T(8,128)(2,1)S(1)}, u32[]{:S(2)}, u32[]{:S(2)}) collective-permute-start(bf16[256,512]{1,0:T(8,128)(2,1)S(1)} %pad_maximum_fusion.2), channel_id=1, source_target_pairs={{0,2},{1,3},{2,0},{3,1},{4,6},{5,7},{6,4},{7,5},{8,10},{9,11},{10,... | collective-permute-start | bytes 786440 | tf_op jit(solution)/shard_map/ppermute | solution.py:379
  80.1 6.4 %collective-permute-start.12 = (bf16[256,512]{1,0:T(8,128)(2,1)S(1)}, bf16[256,512]{1,0:T(8,128)(2,1)S(1)}, u32[]{:S(2)}, u32[]{:S(2)}) collective-permute-start(bf16[256,512]{1,0:T(8,128)(2,1)S(1)} %pad_maximum_fusion.3), channel_id=1, source_target_pairs={{0,4},{1,5},{2,6},{3,7},{4,0},{5,1},{6,2},{7,3},{8,12},{9,13},{10,... | collective-permute-start | bytes 786440 | tf_op jit(solution)/shard_map/ppermute | solution.py:379
  85.0 2.0 %collective-permute-start.10 = (bf16[512,512]{1,0:T(8,128)(2,1)S(1)}, bf16[512,512]{1,0:T(8,128)(2,1)S(1)}, u32[]{:S(2)}, u32[]{:S(2)}) collective-permute-start(bf16[512,512]{1,0:T(8,128)(2,1)S(1)} %pad_maximum_fusion.p0), channel_id=1, source_target_pairs={{0,1},{1,0},{2,3},{3,2},{4,5},{5,4},{6,7},{7,6},{8,9},{9,8},{10,11... | collective-permute-start | bytes 1572872 | tf_op jit(solution)/shard_map/ppermute | solution.py:379
  86.5 2.0 %collective-permute-start.13 = (bf16[512,512]{1,0:T(8,128)(2,1)S(1)}, bf16[512,512]{1,0:T(8,128)(2,1)S(1)}, u32[]{:S(2)}, u32[]{:S(2)}) collective-permute-start(bf16[512,512]{1,0:T(8,128)(2,1)S(1)} %pad_maximum_fusion.1.q0), channel_id=1, source_target_pairs={{0,1},{1,0},{2,3},{3,2},{4,5},{5,4},{6,7},{7,6},{8,9},{9,8},{10,11... | collective-permute-start | bytes 1572872 | tf_op jit(solution)/shard_map/ppermute | solution.py:379

commit v3 on v2

--- a/solution.py
+++ b/solution.py
@@ -375,6 +375,20 @@
     )(keep, got)
 
 
+def later_kernel(x_ref, *refs):
+    refs[-1][...] = x_ref[...]
+
+
+def later(x, *others):
+    return pl.pallas_call(
+        later_kernel,
+        in_specs=[pl.BlockSpec(memory_space=VMEM)] + [pl.BlockSpec(memory_space=pl.ANY)] * len(others),
+        out_specs=pl.BlockSpec(memory_space=VMEM),
+        out_shape=jax.ShapeDtypeStruct(x.shape, x.dtype),
+        compiler_params=params(SMALL),
+    )(x, *others)
+
+
 def swap(x, mask, regions):
     return lax.ppermute(x, "region", [(i, i ^ mask) for i in range(regions)])
 
@@ -451,16 +465,13 @@
     for step in range(steps):
         got_p = swap(send_p, order_p[step], regions)
         got_q = swap(send_q, order_q[step], regions)
-        if step == 1:
-            got_p, got_q, returned = after((got_p, got_q, returned))
         if step < steps - 1:
             keep_p, send_p = add_split(keep_p, got_p, 0)
             keep_q, send_q = add_split(keep_q, got_q, EXTRA)
         else:
             keep_p, keep_q = add(keep_p, got_p), add(keep_q, got_q)
         if step == 0:
-            sum_s, send_p, send_q = after((sum_s, send_p, send_q))
-            returned = all_to_all(sum_s, regions)
+            returned = all_to_all(later(sum_s, send_p, send_q), regions)
     got_p = swap(keep_p, last, regions)
     got_q = swap(keep_q, last, regions)
     keep_p, keep_q, dp, sum_r = after((keep_p, keep_q, dp, sum_r))

time: 90.8 us -> 82.1 us (0.904)
  waiting for transfers between devices: 29.3 us -> 24.3 us
  starting transfers between devices: 26.1 us -> 21.7 us
    ppermute x14, waiting for transfers between devices: 27.3 us -> 22.3 us  [swap(): return lax.ppermute(x, 'region', [(i, i ^ mask) for i in range(regions)])]
    ppermute x14, starting transfers between devices: 14.7 us -> 10.4 us  [swap(): return lax.ppermute(x, 'region', [(i, i ^ mask) for i in range(regions)])]
  transfers between devices with their start and end apart: 16 -> 16, of which waited for: 11 -> 12; matrix products, arithmetic and copies ran while one was open for 0% -> 0% of each run, Pallas kernels for 18% -> 21%
where the time goes in v3:
time: 82.1 us; the launch traced here: 81.7 us
  Pallas kernels  33.3 us (41%)
  waiting for transfers between devices  24.3 us (30%)
  starting transfers between devices  21.7 us (26%)
  between operations  1.5 us (2%)
    ppermute x14, waiting for transfers between devices, swap(): return lax.ppermute(x, 'region', [(i, i ^ mask) for i in range(regions)])  22.3 us
    pallas_call x1, Pallas kernels, edge_part(): pl.pallas_call(functools.partial(edge_kernel, order_p, order_q), in_specs...  12.4 us
    all_to_all x2, starting transfers between devices, all_to_all(): lax.all_to_all(x.reshape(regions, rows // regions, f), 'region', split_ax...  11.3 us
    ppermute x14, starting transfers between devices, swap(): return lax.ppermute(x, 'region', [(i, i ^ mask) for i in range(regions)])  10.4 us
    pallas_call x1, Pallas kernels, local_part(): pl.pallas_call(local_kernel, in_specs=[pl.BlockSpec(memory_space=SMEM), p...  7.31 us
    pallas_call x1, Pallas kernels, edge_grad(): pl.pallas_call(edge_grad_kernel, grid=(total // block,), in_specs=[edge_s...  5.76 us
    pallas_call x1, Pallas kernels, node_grad(): pl.pallas_call(node_grad_kernel, grid=(1,), in_specs=[whole(send_rows.sha...  2.77 us
    pallas_call x1, Pallas kernels, pick_rows(): pl.pallas_call(pick_kernel, out_shape=jax.ShapeDtypeStruct((send_rows.siz...  2.05 us
  transfers between devices with their start and end apart: 16, of which 12 were waited for; matrix products, arithmetic and copies ran while one was open for 0% of the time, Pallas kernels for 21%

profile of v3, /device:TPU:0, one launch (start us, length us, event | category | flops | bytes accessed | tf_op | source)
XLA Modules:
  0.0 81.7 jit_solution(1144031201340001563)
XLA Ops:
  0.6 2.1 %shard_map.165 = bf16[256,512]{1,0:T(8,128)(2,1)} custom-call(s32[16,16]{1,0:T(8,128)} %rows_ref.3, bf16[256,512]{1,0:T(8,128)(2,1)} %nodes_hbm.3), custom_call_target="tpu_custom_call" | custom-call | tf_op jit(solution)/shard_map/pallas_call | solution.py:63
  2.7 7.4 %all-to-all-start = ((bf16[16,16,512]{2,1,0:T(8,128)(2,1)}), bf16[16,16,512]{2,1,0:T(8,128)(2,1)S(1)}, u32[]{:S(2)}, u32[]{:S(2)}) async-start(bf16[16,16,512]{2,1,0:T(8,128)(2,1)} %bitcast.17), calls=%async_computation | async-start | bytes 524288 | tf_op jit(solution)/shard_map/all_to_all | solution.py:441
  10.7 0.0 copy-start.1
  10.7 0.0 copy-start.2
  10.8 0.0 copy-start.3
  10.8 0.0 copy-start.4
  10.8 0.0 copy-start.5
  10.8 0.0 copy-start.6
  10.8 7.3 %shard_map.164 = (bf16[2048,512]{1,0:T(8,128)(2,1)}, f32[2048,512]{1,0:T(8,128)}) custom-call(s32[1]{0:T(128)S(6)} %copy.18.count_ref, s32[1,2048]{1,0:T(1,128)} %bitcast.12, f32[1,512]{1,0:T(1,128)} %bitcast.18, bf16[2048,512]{1,0:T(8,128)(2,1)} %edges_hbm.3, bf16[2048,512]{1,0:T(8,128)(2,1)} %cot_hbm.1, bf16[256,512]{1,0:T(8,128)(2,1)} %nodes_hbm.3, ...), custom_call_target="tpu_custom_call" | custom-call | flops 2147483648 | bytes 10485760 | tf_op jit(solution)/shard_map/pallas_call | solution.py:125
  18.1 2.0 %all-to-all-done = bf16[16,16,512]{2,1,0:T(8,128)(2,1)S(1)} async-done(((bf16[16,16,512]{2,1,0:T(8,128)(2,1)}), bf16[16,16,512]{2,1,0:T(8,128)(2,1)S(1)}, u32[]{:S(2)}, u32[]{:S(2)}) %all-to-all-start) | async-done | bytes 262176 | tf_op jit(solution)/shard_map/all_to_all | solution.py:441
  20.1 0.0 copy-done.1
  20.1 0.0 copy-done.2
  20.1 0.0 copy-done.3
  20.1 0.0 copy-done.4
  20.2 0.0 copy-done.5
  20.2 0.0 copy-done.6
  20.2 12.4 %shard_map.166 = (bf16[2048,512]{1,0:T(8,128)(2,1)}, f32[512,512]{1,0:T(8,128)S(1)}, bf16[512,512]{1,0:T(8,128)(2,1)S(1)}, f32[528,512]{1,0:T(8,128)S(1)}, bf16[...) custom-call(s32[1]{0:T(128)} %bitcast.me_ref, s32[1,2048]{1,0:T(1,128)S(1)} %bitcast.11, ...), custom_call_target="tpu_custom_call" | custom-call | flops 5905580032 | bytes 10485760 | tf_op jit(solution)/shard_map/pallas_call | solution.py:285
  32.6 0.0 copy-start
  32.6 0.1 collective-permute-start.4
  32.7 0.5 collective-permute-start
  33.2 1.4 %collective-permute-done.4.got_ref = bf16[528,512]{1,0:T(8,128)(2,1)S(1)} collective-permute-done((bf16[528,512]{1,0:T(8,128)(2,1)S(1)}, bf16[528,512]{1,0:T(8,128)(2,1)S(1)}, u32[]{:S(2)}, u32[]{:S(2)}) %collective-permute-start.4) | collective-permute-done | bytes 540704 | tf_op jit(solution)/shard_map/ppermute | solution.py:393
  34.6 0.1 shard_map.170
  34.7 0.4 collective-permute-start.5
  35.1 0.2 collective-permute-done.got_ref
  35.4 0.1 shard_map.167
  35.5 0.9 %collective-permute-start.1 = (bf16[256,512]{1,0:T(8,128)(2,1)S(1)}, bf16[256,512]{1,0:T(8,128)(2,1)S(1)}, u32[]{:S(2)}, u32[]{:S(2)}) collective-permute-start(bf16[256,512]{1,0:T(8,128)(2,1)S(1)} %get-tuple-element.38.refs_0_), channel_id=1, source_target_pairs={{0,2},{1,3},{2,0},{3,1},{4,6},{5,7},{6,4},{7,5},{8,10},{9,11},{10,... | collective-permute-start | bytes 786440 | tf_op jit(solution)/shard_map/ppermute | solution.py:393
  36.4 0.7 shard_map.174
  37.1 0.0 copy-done
  37.1 3.9 %all-to-all-start.1 = ((bf16[16,16,512]{2,1,0:T(8,128)(2,1)}), bf16[16,16,512]{2,1,0:T(8,128)(2,1)S(1)}, u32[]{:S(2)}, u32[]{:S(2)}) async-start(bf16[16,16,512]{2,1,0:T(8,128)(2,1)} %bitcast.8), calls=%async_computation.1 | async-start | bytes 524288 | tf_op jit(solution)/shard_map/all_to_all | solution.py:441
  41.0 2.5 %collective-permute-done.5.got_ref = bf16[272,512]{1,0:T(8,128)(2,1)S(1)} collective-permute-done((bf16[272,512]{1,0:T(8,128)(2,1)S(1)}, bf16[272,512]{1,0:T(8,128)(2,1)S(1)}, u32[]{:S(2)}, u32[]{:S(2)}) %collective-permute-start.5) | collective-permute-done | bytes 278560 | tf_op jit(solution)/shard_map/ppermute | solution.py:393
  43.5 0.4 collective-permute-start.6
  44.0 0.0 collective-permute-done.1.got_ref
  44.0 1.1 %collective-permute-start.2 = (bf16[128,512]{1,0:T(8,128)(2,1)S(1)}, bf16[128,512]{1,0:T(8,128)(2,1)S(1)}, u32[]{:S(2)}, u32[]{:S(2)}) collective-permute-start(bf16[128,512]{1,0:T(8,128)(2,1)S(1)} %get-tuple-element.40), channel_id=1, source_target_pairs={{0,4},{1,5},{2,6},{3,7},{4,0},{5,1},{6,2},{7,3},{8,12},{9,13},{10,... | collective-permute-start | bytes 393224 | tf_op jit(solution)/shard_map/ppermute | solution.py:393
  45.2 4.8 %collective-permute-done.6.got_ref = bf16[144,512]{1,0:T(8,128)(2,1)S(1)} collective-permute-done((bf16[144,512]{1,0:T(8,128)(2,1)S(1)}, bf16[144,512]{1,0:T(8,128)(2,1)S(1)}, u32[]{:S(2)}, u32[]{:S(2)}) %collective-permute-start.6) | collective-permute-done | bytes 147488 | tf_op jit(solution)/shard_map/ppermute | solution.py:393
  50.0 2.6 %collective-permute-start.7 = (bf16[144,512]{1,0:T(8,128)(2,1)S(1)}, bf16[144,512]{1,0:T(8,128)(2,1)S(1)}, u32[]{:S(2)}, u32[]{:S(2)}) collective-permute-start(bf16[144,512]{1,0:T(8,128)(2,1)S(1)} %shard_map.172.keep_ref), channel_id=1, source_target_pairs={{0,8},{1,9},{2,10},{3,11},{4,12},{5,13},{6,14},{7,15},{8,0},{9,1},... | collective-permute-start | bytes 442376 | tf_op jit(solution)/shard_map/ppermute | solution.py:393
  52.6 0.0 collective-permute-done.2.got_ref
  52.6 1.0 %collective-permute-start.3 = (bf16[128,512]{1,0:T(8,128)(2,1)S(1)}, bf16[128,512]{1,0:T(8,128)(2,1)S(1)}, u32[]{:S(2)}, u32[]{:S(2)}) collective-permute-start(bf16[128,512]{1,0:T(8,128)(2,1)S(1)} %shard_map.169.keep_ref), channel_id=1, source_target_pairs={{0,8},{1,9},{2,10},{3,11},{4,12},{5,13},{6,14},{7,15},{8,0},{9,1},... | collective-permute-start | bytes 393224 | tf_op jit(solution)/shard_map/ppermute | solution.py:393
  53.6 5.8 %shard_map.173 = bf16[2048,512]{1,0:T(8,128)(2,1)} custom-call(bf16[2048,512]{1,0:T(8,128)(2,1)} %get-tuple-element.49.dp_ref, f32[2048,512]{1,0:T(8,128)} %get-tuple-element.34.mc_hbm.mc_ref, bf16[1536,512]{1,0:T(8,128)(2,1)} %w_r_ref.1), custom_call_target="tpu_custom_call" | custom-call | flops 1073741824 | bytes 8388608 | tf_op jit(solution)/shard_map/pallas_call | solution.py:309
  59.4 0.0 all-to-all-done.1
  59.4 0.0 copy-start.7
  59.4 0.7 copy-done.7
  60.1 2.8 %shard_map.175 = f32[256,512]{1,0:T(8,128)} custom-call(s32[16,16]{1,0:T(8,128)} %rows_ref.3, bf16[256,512]{1,0:T(8,128)(2,1)} %bitcast.16, bf16[256,512]{1,0:T(8,128)(2,1)} %copy-done, bf16[1536,512]{1,0:T(8,128)(2,1)} %w_r_ref.1, bf16[1536,512]{1,0:T(8,128)(2,1)} %w_r_ref.1), custom_call_target="tpu_custom_call" | custom-call | flops 335544320 | bytes 2621440 | tf_op jit(solution)/shard_map/pallas_call | solution.py:329
  62.9 1.7 %collective-permute-done.3.got_ref = bf16[128,512]{1,0:T(8,128)(2,1)S(1)} collective-permute-done((bf16[128,512]{1,0:T(8,128)(2,1)S(1)}, bf16[128,512]{1,0:T(8,128)(2,1)S(1)}, u32[]{:S(2)}, u32[]{:S(2)}) %collective-permute-start.3) | collective-permute-done | bytes 131104 | tf_op jit(solution)/shard_map/ppermute | solution.py:393
  64.6 0.0 collective-permute-done.7.got_ref
  64.6 0.8 collective-permute-start.8
  65.5 0.5 collective-permute-start.11
  65.9 3.7 %collective-permute-done.8 = bf16[128,512]{1,0:T(8,128)(2,1)S(1)} collective-permute-done((bf16[128,512]{1,0:T(8,128)(2,1)S(1)}, bf16[128,512]{1,0:T(8,128)(2,1)S(1)}, u32[]{:S(2)}, u32[]{:S(2)}) %collective-permute-start.8) | collective-permute-done | bytes 131104 | tf_op jit(solution)/shard_map/ppermute | solution.py:393
  69.7 1.2 %collective-permute-start.9 = (bf16[256,512]{1,0:T(8,128)(2,1)S(1)}, bf16[256,512]{1,0:T(8,128)(2,1)S(1)}, u32[]{:S(2)}, u32[]{:S(2)}) collective-permute-start(bf16[256,512]{1,0:T(8,128)(2,1)S(1)} %pad_maximum_fusion.2), channel_id=1, source_target_pairs={{0,2},{1,3},{2,0},{3,1},{4,6},{5,7},{6,4},{7,5},{8,10},{9,11},{10,... | collective-permute-start | bytes 786440 | tf_op jit(solution)/shard_map/ppermute | solution.py:393
  70.8 0.3 collective-permute-done.11
  71.1 0.7 collective-permute-start.12
  71.9 4.4 %collective-permute-done.9 = bf16[256,512]{1,0:T(8,128)(2,1)S(1)} collective-permute-done((bf16[256,512]{1,0:T(8,128)(2,1)S(1)}, bf16[256,512]{1,0:T(8,128)(2,1)S(1)}, u32[]{:S(2)}, u32[]{:S(2)}) %collective-permute-start.9) | collective-permute-done | bytes 262176 | tf_op jit(solution)/shard_map/ppermute | solution.py:393
  76.3 0.1 collective-permute-start.10
  76.4 1.4 %collective-permute-done.12 = bf16[256,512]{1,0:T(8,128)(2,1)S(1)} collective-permute-done((bf16[256,512]{1,0:T(8,128)(2,1)S(1)}, bf16[256,512]{1,0:T(8,128)(2,1)S(1)}, u32[]{:S(2)}, u32[]{:S(2)}) %collective-permute-start.12) | collective-permute-done | bytes 262176 | tf_op jit(solution)/shard_map/ppermute | solution.py:393
  77.8 0.1 collective-permute-start.13
  77.9 0.4 collective-permute-done.10.p1
  78.3 1.5 %collective-permute-done.13.q1 = bf16[512,512]{1,0:T(8,128)(2,1)S(1)} collective-permute-done((bf16[512,512]{1,0:T(8,128)(2,1)S(1)}, bf16[512,512]{1,0:T(8,128)(2,1)S(1)}, u32[]{:S(2)}, u32[]{:S(2)}) %collective-permute-start.13) | collective-permute-done | bytes 524320 | tf_op jit(solution)/shard_map/ppermute | solution.py:393
  79.8 1.8 %shard_map.178 = (bf16[1536,512]{1,0:T(8,128)(2,1)}, bf16[512,512]{1,0:T(8,128)(2,1)}, bf16[3,512]{1,0:T(4,128)(2,1)}) custom-call(s32[1]{0:T(128)} %bitcast.me_ref, bf16[512,512]{1,0:T(8,128)(2,1)S(1)} %pad_maximum_fusion.p0, bf16[512,512]{1,0:T(8,128)(2,1)S(1)} %collective-permute-done.10.p1, bf16[512,512]{1,0:T(8,128)(2,1)S(1)} %pad_maximum_fusion.1.q0, ...), custom_call_target="tpu_custom_call" | custom-call | tf_op jit(solution)/shard_map/pallas_call | solution.py:427
  (12 shorter events, 0.3 us)
Async XLA Ops:
  2.7 17.4 %all-to-all-start = ((bf16[16,16,512]{2,1,0:T(8,128)(2,1)}), bf16[16,16,512]{2,1,0:T(8,128)(2,1)S(1)}, u32[]{:S(2)}, u32[]{:S(2)}) async-start(bf16[16,16,512]{2,1,0:T(8,128)(2,1)} %bitcast.17), calls=%async_computation | async-start | bytes 524288 | tf_op jit(solution)/shard_map/all_to_all | solution.py:441
  10.7 9.4 %copy-start.1 = (bf16[256,512]{1,0:T(8,128)(2,1)S(1)}, bf16[256,512]{1,0:T(8,128)(2,1)}, u32[]{:S(2)}) copy-start(bf16[256,512]{1,0:T(8,128)(2,1)} %nodes_hbm.3) | copy-start | bytes 786436
  10.7 9.4 %copy-start.2 = (bf16[512,512]{1,0:T(8,128)(2,1)S(1)}, bf16[512,512]{1,0:T(8,128)(2,1)}, u32[]{:S(2)}) copy-start(bf16[512,512]{1,0:T(8,128)(2,1)} %w_out_hbm.1) | copy-start | bytes 1572868
  10.8 9.4 %copy-start.3 = (s32[2048]{0:T(1024)S(1)}, s32[2048]{0:T(1024)}, u32[]{:S(2)}) copy-start(s32[2048]{0:T(1024)} %param.23) | copy-start | bytes 24580
  10.8 9.4 %copy-start.4 = (s32[2048]{0:T(1024)S(1)}, s32[2048]{0:T(1024)}, u32[]{:S(2)}) copy-start(s32[2048]{0:T(1024)} %param.24) | copy-start | bytes 24580
  10.8 9.4 %copy-start.5 = (f32[512]{0:T(512)S(1)}, f32[512]{0:T(512)}, u32[]{:S(2)}) copy-start(f32[512]{0:T(512)} %param.20) | copy-start | bytes 6148
  10.8 9.4 %copy-start.6 = (f32[512]{0:T(512)S(1)}, f32[512]{0:T(512)}, u32[]{:S(2)}) copy-start(f32[512]{0:T(512)} %param.21) | copy-start | bytes 6148
  32.6 4.5 %copy-start = (bf16[256,512]{1,0:T(8,128)(2,1)}, bf16[256,512]{1,0:T(8,128)(2,1)S(1)}, u32[]{:S(2)}) copy-start(bf16[256,512]{1,0:T(8,128)(2,1)S(1)} %get-tuple-element.51.sum_r_ref) | copy-start | bytes 786436
  32.6 2.0 %collective-permute-start.4 = (bf16[528,512]{1,0:T(8,128)(2,1)S(1)}, bf16[528,512]{1,0:T(8,128)(2,1)S(1)}, u32[]{:S(2)}, u32[]{:S(2)}) collective-permute-start(bf16[528,512]{1,0:T(8,128)(2,1)S(1)} %get-tuple-element.42), channel_id=1, source_target_pairs={{0,1},{1,0},{2,3},{3,2},{4,5},{5,4},{6,7},{7,6},{8,9},{9,8},{10,11... | collective-permute-start | bytes 1622024 | tf_op jit(solution)/shard_map/ppermute | solution.py:393
  32.7 2.7 %collective-permute-start = (bf16[512,512]{1,0:T(8,128)(2,1)S(1)}, bf16[512,512]{1,0:T(8,128)(2,1)S(1)}, u32[]{:S(2)}, u32[]{:S(2)}) collective-permute-start(bf16[512,512]{1,0:T(8,128)(2,1)S(1)} %get-tuple-element.36), channel_id=1, source_target_pairs={{0,1},{1,0},{2,3},{3,2},{4,5},{5,4},{6,7},{7,6},{8,9},{9,8},{10,11... | collective-permute-start | bytes 1572872 | tf_op jit(solution)/shard_map/ppermute | solution.py:393
  34.7 8.8 %collective-permute-start.5 = (bf16[272,512]{1,0:T(8,128)(2,1)S(1)}, bf16[272,512]{1,0:T(8,128)(2,1)S(1)}, u32[]{:S(2)}, u32[]{:S(2)}) collective-permute-start(bf16[272,512]{1,0:T(8,128)(2,1)S(1)} %get-tuple-element.44.refs_1_), channel_id=1, source_target_pairs={{0,4},{1,5},{2,6},{3,7},{4,0},{5,1},{6,2},{7,3},{8,12},{9,13},{10,... | collective-permute-start | bytes 835592 | tf_op jit(solution)/shard_map/ppermute | solution.py:393
  35.5 8.5 %collective-permute-start.1 = (bf16[256,512]{1,0:T(8,128)(2,1)S(1)}, bf16[256,512]{1,0:T(8,128)(2,1)S(1)}, u32[]{:S(2)}, u32[]{:S(2)}) collective-permute-start(bf16[256,512]{1,0:T(8,128)(2,1)S(1)} %get-tuple-element.38.refs_0_), channel_id=1, source_target_pairs={{0,2},{1,3},{2,0},{3,1},{4,6},{5,7},{6,4},{7,5},{8,10},{9,11},{10,... | collective-permute-start | bytes 786440 | tf_op jit(solution)/shard_map/ppermute | solution.py:393
  37.1 22.3 %all-to-all-start.1 = ((bf16[16,16,512]{2,1,0:T(8,128)(2,1)}), bf16[16,16,512]{2,1,0:T(8,128)(2,1)S(1)}, u32[]{:S(2)}, u32[]{:S(2)}) async-start(bf16[16,16,512]{2,1,0:T(8,128)(2,1)} %bitcast.8), calls=%async_computation.1 | async-start | bytes 524288 | tf_op jit(solution)/shard_map/all_to_all | solution.py:441
  43.5 6.4 %collective-permute-start.6 = (bf16[144,512]{1,0:T(8,128)(2,1)S(1)}, bf16[144,512]{1,0:T(8,128)(2,1)S(1)}, u32[]{:S(2)}, u32[]{:S(2)}) collective-permute-start(bf16[144,512]{1,0:T(8,128)(2,1)S(1)} %get-tuple-element.46), channel_id=1, source_target_pairs={{0,2},{1,3},{2,0},{3,1},{4,6},{5,7},{6,4},{7,5},{8,10},{9,11},{10,... | collective-permute-start | bytes 442376 | tf_op jit(solution)/shard_map/ppermute | solution.py:393
  44.0 8.6 %collective-permute-start.2 = (bf16[128,512]{1,0:T(8,128)(2,1)S(1)}, bf16[128,512]{1,0:T(8,128)(2,1)S(1)}, u32[]{:S(2)}, u32[]{:S(2)}) collective-permute-start(bf16[128,512]{1,0:T(8,128)(2,1)S(1)} %get-tuple-element.40), channel_id=1, source_target_pairs={{0,4},{1,5},{2,6},{3,7},{4,0},{5,1},{6,2},{7,3},{8,12},{9,13},{10,... | collective-permute-start | bytes 393224 | tf_op jit(solution)/shard_map/ppermute | solution.py:393
  50.0 14.6 %collective-permute-start.7 = (bf16[144,512]{1,0:T(8,128)(2,1)S(1)}, bf16[144,512]{1,0:T(8,128)(2,1)S(1)}, u32[]{:S(2)}, u32[]{:S(2)}) collective-permute-start(bf16[144,512]{1,0:T(8,128)(2,1)S(1)} %shard_map.172.keep_ref), channel_id=1, source_target_pairs={{0,8},{1,9},{2,10},{3,11},{4,12},{5,13},{6,14},{7,15},{8,0},{9,1},... | collective-permute-start | bytes 442376 | tf_op jit(solution)/shard_map/ppermute | solution.py:393
  52.6 11.9 %collective-permute-start.3 = (bf16[128,512]{1,0:T(8,128)(2,1)S(1)}, bf16[128,512]{1,0:T(8,128)(2,1)S(1)}, u32[]{:S(2)}, u32[]{:S(2)}) collective-permute-start(bf16[128,512]{1,0:T(8,128)(2,1)S(1)} %shard_map.169.keep_ref), channel_id=1, source_target_pairs={{0,8},{1,9},{2,10},{3,11},{4,12},{5,13},{6,14},{7,15},{8,0},{9,1},... | collective-permute-start | bytes 393224 | tf_op jit(solution)/shard_map/ppermute | solution.py:393
  59.4 0.7 copy-start.7
  64.6 5.0 %collective-permute-start.8 = (bf16[128,512]{1,0:T(8,128)(2,1)S(1)}, bf16[128,512]{1,0:T(8,128)(2,1)S(1)}, u32[]{:S(2)}, u32[]{:S(2)}) collective-permute-start(bf16[128,512]{1,0:T(8,128)(2,1)S(1)} %shard_map.176), channel_id=1, source_target_pairs={{0,4},{1,5},{2,6},{3,7},{4,0},{5,1},{6,2},{7,3},{8,12},{9,13},{10,... | collective-permute-start | bytes 393224 | tf_op jit(solution)/shard_map/ppermute | solution.py:393
  65.5 5.7 %collective-permute-start.11 = (bf16[128,512]{1,0:T(8,128)(2,1)S(1)}, bf16[128,512]{1,0:T(8,128)(2,1)S(1)}, u32[]{:S(2)}, u32[]{:S(2)}) collective-permute-start(bf16[128,512]{1,0:T(8,128)(2,1)S(1)} %slice.8), channel_id=1, source_target_pairs={{0,2},{1,3},{2,0},{3,1},{4,6},{5,7},{6,4},{7,5},{8,10},{9,11},{10,... | collective-permute-start | bytes 393224 | tf_op jit(solution)/shard_map/ppermute | solution.py:393
  69.7 6.6 %collective-permute-start.9 = (bf16[256,512]{1,0:T(8,128)(2,1)S(1)}, bf16[256,512]{1,0:T(8,128)(2,1)S(1)}, u32[]{:S(2)}, u32[]{:S(2)}) collective-permute-start(bf16[256,512]{1,0:T(8,128)(2,1)S(1)} %pad_maximum_fusion.2), channel_id=1, source_target_pairs={{0,2},{1,3},{2,0},{3,1},{4,6},{5,7},{6,4},{7,5},{8,10},{9,11},{10,... | collective-permute-start | bytes 786440 | tf_op jit(solution)/shard_map/ppermute | solution.py:393
  71.1 6.7 %collective-permute-start.12 = (bf16[256,512]{1,0:T(8,128)(2,1)S(1)}, bf16[256,512]{1,0:T(8,128)(2,1)S(1)}, u32[]{:S(2)}, u32[]{:S(2)}) collective-permute-start(bf16[256,512]{1,0:T(8,128)(2,1)S(1)} %pad_maximum_fusion.3), channel_id=1, source_target_pairs={{0,4},{1,5},{2,6},{3,7},{4,0},{5,1},{6,2},{7,3},{8,12},{9,13},{10,... | collective-permute-start | bytes 786440 | tf_op jit(solution)/shard_map/ppermute | solution.py:393
  76.3 2.0 %collective-permute-start.10 = (bf16[512,512]{1,0:T(8,128)(2,1)S(1)}, bf16[512,512]{1,0:T(8,128)(2,1)S(1)}, u32[]{:S(2)}, u32[]{:S(2)}) collective-permute-start(bf16[512,512]{1,0:T(8,128)(2,1)S(1)} %pad_maximum_fusion.p0), channel_id=1, source_target_pairs={{0,1},{1,0},{2,3},{3,2},{4,5},{5,4},{6,7},{7,6},{8,9},{9,8},{10,11... | collective-permute-start | bytes 1572872 | tf_op jit(solution)/shard_map/ppermute | solution.py:393
  77.8 2.0 %collective-permute-start.13 = (bf16[512,512]{1,0:T(8,128)(2,1)S(1)}, bf16[512,512]{1,0:T(8,128)(2,1)S(1)}, u32[]{:S(2)}, u32[]{:S(2)}) collective-permute-start(bf16[512,512]{1,0:T(8,128)(2,1)S(1)} %pad_maximum_fusion.1.q0), channel_id=1, source_target_pairs={{0,1},{1,0},{2,3},{3,2},{4,5},{5,4},{6,7},{7,6},{8,9},{9,8},{10,11... | collective-permute-start | bytes 1572872 | tf_op jit(solution)/shard_map/ppermute | solution.py:393

commit v4 on v3

--- a/solution.py
+++ b/solution.py
@@ -150,13 +150,17 @@
     slot = 0
     for bit, mask in enumerate(reversed(order)):
         if position >> bit & 1:
-            slot |= mask
+            slot |= 1 << sorted(order).index(mask)
     return slot
+
+
+def home_of(me, order):
+    return sum(((me // mask) & 1) << bit for bit, mask in enumerate(sorted(order)))
 
 
 def write_slots(me, parts, keep_ref, send_ref, order, first=0):
     pieces = 2 ** len(order)
-    home = me & (pieces - 1)
+    home = home_of(me, order)
     r = parts[0].shape[0] // pieces
     for position in range(pieces):
         piece = home ^ slot_of(position, order)
@@ -192,8 +196,6 @@
 
     def gather(part):
         at, columns = pl.ds(part * rows, rows), slice(part * rows, (part + 1) * rows)
-        hot[:slots, columns] = one_hot_t(slot_ref[:, columns], slots)
-        hot[slots:, columns] = one_hot_t(recv_ref[:, columns], n)
         if part == 0:
             table[...] = dot(halo[...], w_s[...], NN).astype(BF)
         wide[at, :] = dot(hot[:slots, columns], table[...], TN)
@@ -240,13 +242,20 @@
         more = dot(edges[at, :], dp[at, :], TN)
         acc_e[...] = more if part == 0 else acc_e[...] + more
 
+    for part in range(PARTS):
+        columns = slice(part * rows, (part + 1) * rows)
+        hot[:slots, columns] = one_hot_t(slot_ref[:, columns], slots)
+        hot[slots:, columns] = one_hot_t(recv_ref[:, columns], n)
     stages = (gather, norm, back, weights)
     for turn in range(PARTS + len(stages) - 1):
         if turn == 0:
-            for g in [get_halo, get_w_s] + get_pre:
+            for g in [get_halo, get_w_s, get_pre[0]]:
                 g.wait()
         if turn == 1:
-            for g in [get_w_out, get_edges, get_nodes] + get_mc:
+            for g in [get_w_out] + get_pre[1:] + get_mc[:1]:
+                g.wait()
+        if turn == 2:
+            for g in get_mc[1:] + [get_edges, get_nodes]:
                 g.wait()
         for at in range(len(stages) - 1, -1, -1):
             if 0 <= turn - at < PARTS:
@@ -393,47 +402,68 @@
     return lax.ppermute(x, "region", [(i, i ^ mask) for i in range(regions)])
 
 
-def finish_kernel(order_p, order_q, limit, me_ref, p0, p1, q0, q1, vec_ref, w_in_ref, w_out_ref, vec_out):
+def square_sums(refs):
+    total = jnp.zeros((8, refs[0].shape[1]), F32)
+    for ref in refs:
+        for at in range(0, ref.shape[0], STRIP):
+            x = ref[at : at + STRIP, :].astype(F32)
+            total = total + jnp.sum((x * x).reshape(STRIP // 8, 8, -1), axis=0)
+    return total
+
+
+def squares_kernel(*refs):
+    refs[-1][...] = square_sums(refs[:-1])
+
+
+def squares(*arrays):
+    return pl.pallas_call(
+        squares_kernel,
+        out_shape=jax.ShapeDtypeStruct((8, arrays[0].shape[1]), F32),
+        compiler_params=params(SMALL),
+    )(*arrays)
+
+
+def finish_kernel(order_p, order_q, limit, me_ref, p0, p1, p2, p3, q0, q1, q2, q3, vec_ref, known_ref, w_in_ref,
+                  w_out_ref, vec_out):
     f = w_out_ref.shape[1]
     vec = vec_ref[...].astype(F32)
     vec = vec[: EXTRA // 2, :] + vec[EXTRA // 2 :, :]
-    squares = jnp.sum(vec * vec, axis=0, keepdims=True)
-    for ref in (p0, p1, q0, q1):
-        x = ref[...].astype(F32)
-        x = x * x
-        squares = squares + jnp.sum(jnp.sum(x.reshape(-1, 8, f), axis=0), axis=0, keepdims=True)
-    total = jnp.sum(squares, axis=1, keepdims=True)
+    total = known_ref[...] + square_sums((p3, q3)) + vec * vec
+    total = jnp.sum(jnp.sum(total, axis=0, keepdims=True), axis=1, keepdims=True)
     scale = jnp.minimum(1.0, limit * lax.rsqrt(total + 1e-06))
     vec_out[...] = (vec[0:3, :] * scale).astype(BF)
     me = me_ref[0]
-    targets = [(p0, p1, order_p, ((w_in_ref, f), (w_in_ref, 2 * f))), (q0, q1, order_q, ((w_in_ref, 0), (w_out_ref, 0)))]
-    for low, high, order, outs in targets:
+    targets = [
+        ((p0, p1, p2, p3), order_p, ((w_in_ref, f), (w_in_ref, 2 * f))),
+        ((q0, q1, q2, q3), order_q, ((w_in_ref, 0), (w_out_ref, 0))),
+    ]
+    for refs, order, outs in targets:
         pieces = 2 ** len(order)
-        home = me & (pieces - 1)
+        home = home_of(me, order)
         r = f // pieces
         for position in range(pieces):
-            half, at = divmod(position, pieces // 2)
+            ref, at = divmod(position, pieces // 4)
             piece = home ^ slot_of(position, order)
             for k, (out, offset) in enumerate(outs):
                 row = (at * len(outs) + k) * r
-                x = (high if half else low)[row : row + r, :].astype(F32)
+                x = refs[ref][row : row + r, :].astype(F32)
                 start = pl.multiple_of(offset + piece * r, r)
                 out[pl.ds(start, r), :] = (x * scale).astype(BF)
 
 
-def finish(me, p, q, vec, order_p, order_q):
+def finish(me, p, q, vec, known, order_p, order_q):
     f = vec.shape[1]
     limit = math.sqrt(4.0 * f * f + 3.0 * f)
     return pl.pallas_call(
         functools.partial(finish_kernel, order_p, order_q, limit),
-        in_specs=[pl.BlockSpec(memory_space=SMEM)] + [pl.BlockSpec(memory_space=VMEM)] * 5,
+        in_specs=[pl.BlockSpec(memory_space=SMEM)] + [pl.BlockSpec(memory_space=VMEM)] * 10,
         out_shape=[
             jax.ShapeDtypeStruct((3 * f, f), BF),
             jax.ShapeDtypeStruct((f, f), BF),
             jax.ShapeDtypeStruct((3, f), BF),
         ],
         compiler_params=params(SMALL),
-    )(me, *p, *q, vec)
+    )(me, *p, *q, vec, known)
 
 
 def all_to_all(x, regions):
@@ -447,9 +477,8 @@
     f = edges.shape[1]
     me = lax.axis_index("region").astype(jnp.int32).reshape(1)
     masks = [2**k for k in range(regions.bit_length() - 1)]
-    last = masks[-1]
-    order_p = masks[:-1]
-    order_q = order_p[:1] + order_p[1:][::-1]
+    order_p, last_p = masks[:-1], masks[-1]
+    order_q, last_q = order_p[:1] + order_p[1:][::-1], last_p
     slot_row = edge_slot.reshape(1, -1)
     recv_row = edge_receiver.reshape(1, -1)
     after = lax.optimization_barrier
@@ -472,8 +501,8 @@
             keep_p, keep_q = add(keep_p, got_p), add(keep_q, got_q)
         if step == 0:
             returned = all_to_all(later(sum_s, send_p, send_q), regions)
-    got_p = swap(keep_p, last, regions)
-    got_q = swap(keep_q, last, regions)
+    got_p = swap(keep_p, last_p, regions)
+    got_q = swap(keep_q, last_q, regions)
     keep_p, keep_q, dp, sum_r = after((keep_p, keep_q, dp, sum_r))
     grad_edges = edge_grad(dp, mc, w_in, 512)
     grad_nodes = node_grad(send_rows, returned, sum_r, w_in)
@@ -481,13 +510,17 @@
     part_p = add(keep_p, got_p)
     part_q = add(keep_q, got_q)
     vec, part_q = part_q[:EXTRA], part_q[EXTRA:]
-    for step in range(steps - 1, -1, -1):
-        got_p = swap(part_p, order_p[step], regions)
-        got_q = swap(part_q, order_q[step], regions)
-        if step:
-            part_p = jnp.concatenate([part_p, got_p], axis=0)
-            part_q = jnp.concatenate([part_q, got_q], axis=0)
-    grad_w_in, grad_w_out, grad_vectors = finish(me, (part_p, got_p), (part_q, got_q), vec, order_p, order_q)
+    for step in range(steps - 1, 1, -1):
+        part_p = jnp.concatenate([part_p, swap(part_p, order_p[step], regions)], axis=0)
+        part_q = jnp.concatenate([part_q, swap(part_q, order_q[step], regions)], axis=0)
+    got_p = swap(part_p, order_p[1], regions)
+    got_q = swap(part_q, order_q[1], regions)
+    near_p = swap(part_p, order_p[0], regions)
+    near_q = swap(part_q, order_q[0], regions)
+    all_p = (part_p, got_p, near_p, swap(got_p, order_p[0], regions))
+    all_q = (part_q, got_q, near_q, swap(got_q, order_q[0], regions))
+    known = squares(*all_p[:3], *all_q[:3])
+    grad_w_in, grad_w_out, grad_vectors = finish(me, all_p, all_q, vec, known, order_p, order_q)
     return (grad_edges, grad_nodes, grad_w_in, grad_w_out, grad_vectors)
 
 

time: 82.1 us -> 81.1 us (0.988)
  waiting for transfers between devices: 24.3 us -> 23.2 us
    ppermute x14 -> x16, waiting for transfers between devices: 22.3 us -> 21.2 us  [swap(): return lax.ppermute(x, 'region', [(i, i ^ mask) for i in range(regions)])]
    ppermute x14 -> x16, starting transfers between devices: 10.4 us -> 10.8 us  [swap(): return lax.ppermute(x, 'region', [(i, i ^ mask) for i in range(regions)])]
  transfers between devices with their start and end apart: 16 -> 18, of which waited for: 12 -> 11; matrix products, arithmetic and copies ran while one was open for 0% -> 0% of each run, Pallas kernels for 21% -> 21%
where the time goes in v4:
time: 81.1 us; the launch traced here: 80.6 us
  Pallas kernels  33 us (41%)
  waiting for transfers between devices  23.2 us (29%)
  starting transfers between devices  22.1 us (27%)
  between operations  1.49 us (2%)
    ppermute x16, waiting for transfers between devices, swap(): return lax.ppermute(x, 'region', [(i, i ^ mask) for i in range(regions)])  21.2 us
    pallas_call x1, Pallas kernels, edge_part(): pl.pallas_call(functools.partial(edge_kernel, order_p, order_q), in_specs...  12 us
    all_to_all x2, starting transfers between devices, all_to_all(): lax.all_to_all(x.reshape(regions, rows // regions, f), 'region', split_ax...  11.3 us
    ppermute x16, starting transfers between devices, swap(): return lax.ppermute(x, 'region', [(i, i ^ mask) for i in range(regions)])  10.8 us
    pallas_call x1, Pallas kernels, local_part(): pl.pallas_call(local_kernel, in_specs=[pl.BlockSpec(memory_space=SMEM), p...  7.32 us
    pallas_call x1, Pallas kernels, edge_grad(): pl.pallas_call(edge_grad_kernel, grid=(total // block,), in_specs=[edge_s...  5.76 us
    pallas_call x1, Pallas kernels, node_grad(): pl.pallas_call(node_grad_kernel, grid=(1,), in_specs=[whole(send_rows.sha...  2.77 us
    pallas_call x1, Pallas kernels, pick_rows(): pl.pallas_call(pick_kernel, out_shape=jax.ShapeDtypeStruct((send_rows.siz...  2.05 us
  transfers between devices with their start and end apart: 18, of which 11 were waited for; matrix products, arithmetic and copies ran while one was open for 0% of the time, Pallas kernels for 21%

profile of v4, /device:TPU:0, one launch (start us, length us, event | category | flops | bytes accessed | tf_op | source)
XLA Modules:
  0.0 80.6 jit_solution(3986070404821151103)
XLA Ops:
  0.6 2.1 %shard_map.165 = bf16[256,512]{1,0:T(8,128)(2,1)} custom-call(s32[16,16]{1,0:T(8,128)} %rows_ref.3, bf16[256,512]{1,0:T(8,128)(2,1)} %nodes_hbm.3), custom_call_target="tpu_custom_call" | custom-call | tf_op jit(solution)/shard_map/pallas_call | solution.py:63
  2.7 7.4 %all-to-all-start = ((bf16[16,16,512]{2,1,0:T(8,128)(2,1)}), bf16[16,16,512]{2,1,0:T(8,128)(2,1)S(1)}, u32[]{:S(2)}, u32[]{:S(2)}) async-start(bf16[16,16,512]{2,1,0:T(8,128)(2,1)} %bitcast.17), calls=%async_computation | async-start | bytes 524288 | tf_op jit(solution)/shard_map/all_to_all | solution.py:471
  10.7 0.0 copy-start.1
  10.7 0.0 copy-start.2
  10.8 0.0 copy-start.3
  10.8 0.0 copy-start.4
  10.8 0.0 copy-start.5
  10.8 0.0 copy-start.6
  10.8 7.3 %shard_map.164 = (bf16[2048,512]{1,0:T(8,128)(2,1)}, f32[2048,512]{1,0:T(8,128)}) custom-call(s32[1]{0:T(128)S(6)} %copy.18.count_ref, s32[1,2048]{1,0:T(1,128)} %bitcast.12, f32[1,512]{1,0:T(1,128)} %bitcast.18, bf16[2048,512]{1,0:T(8,128)(2,1)} %edges_hbm.3, bf16[2048,512]{1,0:T(8,128)(2,1)} %cot_hbm.1, bf16[256,512]{1,0:T(8,128)(2,1)} %nodes_hbm.3, ...), custom_call_target="tpu_custom_call" | custom-call | flops 2147483648 | bytes 10485760 | tf_op jit(solution)/shard_map/pallas_call | solution.py:125
  18.1 2.0 %all-to-all-done = bf16[16,16,512]{2,1,0:T(8,128)(2,1)S(1)} async-done(((bf16[16,16,512]{2,1,0:T(8,128)(2,1)}), bf16[16,16,512]{2,1,0:T(8,128)(2,1)S(1)}, u32[]{:S(2)}, u32[]{:S(2)}) %all-to-all-start) | async-done | bytes 262176 | tf_op jit(solution)/shard_map/all_to_all | solution.py:471
  20.1 0.0 copy-done.1
  20.1 0.0 copy-done.2
  20.1 0.0 copy-done.3
  20.1 0.0 copy-done.4
  20.2 0.0 copy-done.5
  20.2 0.0 copy-done.6
  20.2 12.0 %shard_map.166 = (bf16[2048,512]{1,0:T(8,128)(2,1)}, f32[512,512]{1,0:T(8,128)S(1)}, bf16[512,512]{1,0:T(8,128)(2,1)S(1)}, f32[528,512]{1,0:T(8,128)S(1)}, bf16[...) custom-call(s32[1]{0:T(128)} %bitcast.me_ref, s32[1,2048]{1,0:T(1,128)S(1)} %bitcast.11, ...), custom_call_target="tpu_custom_call" | custom-call | flops 5905580032 | bytes 10485760 | tf_op jit(solution)/shard_map/pallas_call | solution.py:294
  32.2 0.0 copy-start
  32.2 0.1 collective-permute-start.4
  32.3 0.5 collective-permute-start
  32.8 1.4 %collective-permute-done.4.got_ref = bf16[528,512]{1,0:T(8,128)(2,1)S(1)} collective-permute-done((bf16[528,512]{1,0:T(8,128)(2,1)S(1)}, bf16[528,512]{1,0:T(8,128)(2,1)S(1)}, u32[]{:S(2)}, u32[]{:S(2)}) %collective-permute-start.4) | collective-permute-done | bytes 540704 | tf_op jit(solution)/shard_map/ppermute | solution.py:402
  34.2 0.1 shard_map.170
  34.3 0.4 collective-permute-start.5
  34.7 0.2 collective-permute-done.got_ref
  34.9 0.1 shard_map.167
  35.0 0.9 %collective-permute-start.1 = (bf16[256,512]{1,0:T(8,128)(2,1)S(1)}, bf16[256,512]{1,0:T(8,128)(2,1)S(1)}, u32[]{:S(2)}, u32[]{:S(2)}) collective-permute-start(bf16[256,512]{1,0:T(8,128)(2,1)S(1)} %get-tuple-element.38.refs_0_), channel_id=1, source_target_pairs={{0,2},{1,3},{2,0},{3,1},{4,6},{5,7},{6,4},{7,5},{8,10},{9,11},{10,... | collective-permute-start | bytes 786440 | tf_op jit(solution)/shard_map/ppermute | solution.py:402
  35.9 0.7 shard_map.174
  36.7 0.0 copy-done
  36.7 3.9 %all-to-all-start.1 = ((bf16[16,16,512]{2,1,0:T(8,128)(2,1)}), bf16[16,16,512]{2,1,0:T(8,128)(2,1)S(1)}, u32[]{:S(2)}, u32[]{:S(2)}) async-start(bf16[16,16,512]{2,1,0:T(8,128)(2,1)} %bitcast.8), calls=%async_computation.1 | async-start | bytes 524288 | tf_op jit(solution)/shard_map/all_to_all | solution.py:471
  40.6 2.4 %collective-permute-done.5.got_ref = bf16[272,512]{1,0:T(8,128)(2,1)S(1)} collective-permute-done((bf16[272,512]{1,0:T(8,128)(2,1)S(1)}, bf16[272,512]{1,0:T(8,128)(2,1)S(1)}, u32[]{:S(2)}, u32[]{:S(2)}) %collective-permute-start.5) | collective-permute-done | bytes 278560 | tf_op jit(solution)/shard_map/ppermute | solution.py:402
  43.1 0.5 collective-permute-start.6
  43.6 0.0 collective-permute-done.1.got_ref
  43.6 1.1 %collective-permute-start.2 = (bf16[128,512]{1,0:T(8,128)(2,1)S(1)}, bf16[128,512]{1,0:T(8,128)(2,1)S(1)}, u32[]{:S(2)}, u32[]{:S(2)}) collective-permute-start(bf16[128,512]{1,0:T(8,128)(2,1)S(1)} %get-tuple-element.40), channel_id=1, source_target_pairs={{0,4},{1,5},{2,6},{3,7},{4,0},{5,1},{6,2},{7,3},{8,12},{9,13},{10,... | collective-permute-start | bytes 393224 | tf_op jit(solution)/shard_map/ppermute | solution.py:402
  44.7 4.8 %collective-permute-done.6.got_ref = bf16[144,512]{1,0:T(8,128)(2,1)S(1)} collective-permute-done((bf16[144,512]{1,0:T(8,128)(2,1)S(1)}, bf16[144,512]{1,0:T(8,128)(2,1)S(1)}, u32[]{:S(2)}, u32[]{:S(2)}) %collective-permute-start.6) | collective-permute-done | bytes 147488 | tf_op jit(solution)/shard_map/ppermute | solution.py:402
  49.6 2.6 %collective-permute-start.7 = (bf16[144,512]{1,0:T(8,128)(2,1)S(1)}, bf16[144,512]{1,0:T(8,128)(2,1)S(1)}, u32[]{:S(2)}, u32[]{:S(2)}) collective-permute-start(bf16[144,512]{1,0:T(8,128)(2,1)S(1)} %shard_map.172.keep_ref), channel_id=1, source_target_pairs={{0,8},{1,9},{2,10},{3,11},{4,12},{5,13},{6,14},{7,15},{8,0},{9,1},... | collective-permute-start | bytes 442376 | tf_op jit(solution)/shard_map/ppermute | solution.py:402
  52.2 0.0 collective-permute-done.2.got_ref
  52.2 1.0 %collective-permute-start.3 = (bf16[128,512]{1,0:T(8,128)(2,1)S(1)}, bf16[128,512]{1,0:T(8,128)(2,1)S(1)}, u32[]{:S(2)}, u32[]{:S(2)}) collective-permute-start(bf16[128,512]{1,0:T(8,128)(2,1)S(1)} %shard_map.169.keep_ref), channel_id=1, source_target_pairs={{0,8},{1,9},{2,10},{3,11},{4,12},{5,13},{6,14},{7,15},{8,0},{9,1},... | collective-permute-start | bytes 393224 | tf_op jit(solution)/shard_map/ppermute | solution.py:402
  53.2 5.8 %shard_map.173 = bf16[2048,512]{1,0:T(8,128)(2,1)} custom-call(bf16[2048,512]{1,0:T(8,128)(2,1)} %get-tuple-element.49.dp_ref, f32[2048,512]{1,0:T(8,128)} %get-tuple-element.34.mc_hbm.mc_ref, bf16[1536,512]{1,0:T(8,128)(2,1)} %w_r_ref.1), custom_call_target="tpu_custom_call" | custom-call | flops 1073741824 | bytes 8388608 | tf_op jit(solution)/shard_map/pallas_call | solution.py:318
  59.0 0.0 all-to-all-done.1
  59.0 0.0 copy-start.7
  59.0 0.7 copy-done.7
  59.7 2.8 %shard_map.175 = f32[256,512]{1,0:T(8,128)} custom-call(s32[16,16]{1,0:T(8,128)} %rows_ref.3, bf16[256,512]{1,0:T(8,128)(2,1)} %bitcast.16, bf16[256,512]{1,0:T(8,128)(2,1)} %copy-done, bf16[1536,512]{1,0:T(8,128)(2,1)} %w_r_ref.1, bf16[1536,512]{1,0:T(8,128)(2,1)} %w_r_ref.1), custom_call_target="tpu_custom_call" | custom-call | flops 335544320 | bytes 2621440 | tf_op jit(solution)/shard_map/pallas_call | solution.py:338
  62.5 1.7 %collective-permute-done.3.got_ref = bf16[128,512]{1,0:T(8,128)(2,1)S(1)} collective-permute-done((bf16[128,512]{1,0:T(8,128)(2,1)S(1)}, bf16[128,512]{1,0:T(8,128)(2,1)S(1)}, u32[]{:S(2)}, u32[]{:S(2)}) %collective-permute-start.3) | collective-permute-done | bytes 131104 | tf_op jit(solution)/shard_map/ppermute | solution.py:402
  64.1 0.0 collective-permute-done.7.got_ref
  64.2 0.8 collective-permute-start.8
  65.0 0.5 collective-permute-start.12
  65.5 3.7 %collective-permute-done.8 = bf16[128,512]{1,0:T(8,128)(2,1)S(1)} collective-permute-done((bf16[128,512]{1,0:T(8,128)(2,1)S(1)}, bf16[128,512]{1,0:T(8,128)(2,1)S(1)}, u32[]{:S(2)}, u32[]{:S(2)}) %collective-permute-start.8) | collective-permute-done | bytes 131104 | tf_op jit(solution)/shard_map/ppermute | solution.py:402
  69.2 1.2 %collective-permute-start.9 = (bf16[256,512]{1,0:T(8,128)(2,1)S(1)}, bf16[256,512]{1,0:T(8,128)(2,1)S(1)}, u32[]{:S(2)}, u32[]{:S(2)}) collective-permute-start(bf16[256,512]{1,0:T(8,128)(2,1)S(1)} %pad_maximum_fusion.refs_0_.p0), channel_id=1, source_target_pairs={{0,2},{1,3},{2,0},{3,1},{4,6},{5,7},{6,4},{7,5},{8,10},{9,11},{10,... | collective-permute-start | bytes 786440 | tf_op jit(solution)/shard_map/ppermute | solution.py:402
  70.4 0.3 collective-permute-done.12
  70.7 0.7 collective-permute-start.13
  71.5 0.0 collective-permute-start.10
  71.5 0.5 collective-permute-start.14
  72.0 3.9 %collective-permute-done.9.refs_1_.p1 = bf16[256,512]{1,0:T(8,128)(2,1)S(1)} collective-permute-done((bf16[256,512]{1,0:T(8,128)(2,1)S(1)}, bf16[256,512]{1,0:T(8,128)(2,1)S(1)}, u32[]{:S(2)}, u32[]{:S(2)}) %collective-permute-start.9) | collective-permute-done | bytes 262176 | tf_op jit(solution)/shard_map/ppermute | solution.py:402
  75.8 0.0 collective-permute-start.11
  75.9 1.5 %collective-permute-done.13.refs_4_.q1 = bf16[256,512]{1,0:T(8,128)(2,1)S(1)} collective-permute-done((bf16[256,512]{1,0:T(8,128)(2,1)S(1)}, bf16[256,512]{1,0:T(8,128)(2,1)S(1)}, u32[]{:S(2)}, u32[]{:S(2)}) %collective-permute-start.13) | collective-permute-done | bytes 262176 | tf_op jit(solution)/shard_map/ppermute | solution.py:402
  77.4 0.0 collective-permute-start.15
  77.4 0.0 collective-permute-done.10.refs_2_.p2
  77.4 0.0 collective-permute-done.14.refs_5_.q2
  77.4 0.3 shard_map.178.known_ref
  77.7 0.0 collective-permute-done.11.p3
  77.7 1.2 %collective-permute-done.15.q3 = bf16[256,512]{1,0:T(8,128)(2,1)S(1)} collective-permute-done((bf16[256,512]{1,0:T(8,128)(2,1)S(1)}, bf16[256,512]{1,0:T(8,128)(2,1)S(1)}, u32[]{:S(2)}, u32[]{:S(2)}) %collective-permute-start.15) | collective-permute-done | bytes 262176 | tf_op jit(solution)/shard_map/ppermute | solution.py:402
  78.9 1.7 %shard_map.179 = (bf16[1536,512]{1,0:T(8,128)(2,1)}, bf16[512,512]{1,0:T(8,128)(2,1)}, bf16[3,512]{1,0:T(4,128)(2,1)}) custom-call(s32[1]{0:T(128)} %bitcast.me_ref, bf16[256,512]{1,0:T(8,128)(2,1)S(1)} %pad_maximum_fusion.refs_0_.p0, bf16[256,512]{1,0:T(8,128)(2,1)S(1)} %collective-permute-done.9.refs_1_.p1, ...), custom_call_target="tpu_custom_call" | custom-call | tf_op jit(solution)/shard_map/pallas_call | solution.py:457
  (10 shorter events, 0.3 us)
Async XLA Ops:
  2.7 17.4 %all-to-all-start = ((bf16[16,16,512]{2,1,0:T(8,128)(2,1)}), bf16[16,16,512]{2,1,0:T(8,128)(2,1)S(1)}, u32[]{:S(2)}, u32[]{:S(2)}) async-start(bf16[16,16,512]{2,1,0:T(8,128)(2,1)} %bitcast.17), calls=%async_computation | async-start | bytes 524288 | tf_op jit(solution)/shard_map/all_to_all | solution.py:471
  10.7 9.4 %copy-start.1 = (bf16[256,512]{1,0:T(8,128)(2,1)S(1)}, bf16[256,512]{1,0:T(8,128)(2,1)}, u32[]{:S(2)}) copy-start(bf16[256,512]{1,0:T(8,128)(2,1)} %nodes_hbm.3) | copy-start | bytes 786436
  10.7 9.4 %copy-start.2 = (bf16[512,512]{1,0:T(8,128)(2,1)S(1)}, bf16[512,512]{1,0:T(8,128)(2,1)}, u32[]{:S(2)}) copy-start(bf16[512,512]{1,0:T(8,128)(2,1)} %w_out_hbm.1) | copy-start | bytes 1572868
  10.8 9.4 %copy-start.3 = (s32[2048]{0:T(1024)S(1)}, s32[2048]{0:T(1024)}, u32[]{:S(2)}) copy-start(s32[2048]{0:T(1024)} %param.23) | copy-start | bytes 24580
  10.8 9.4 %copy-start.4 = (s32[2048]{0:T(1024)S(1)}, s32[2048]{0:T(1024)}, u32[]{:S(2)}) copy-start(s32[2048]{0:T(1024)} %param.24) | copy-start | bytes 24580
  10.8 9.4 %copy-start.5 = (f32[512]{0:T(512)S(1)}, f32[512]{0:T(512)}, u32[]{:S(2)}) copy-start(f32[512]{0:T(512)} %param.20) | copy-start | bytes 6148
  10.8 9.4 %copy-start.6 = (f32[512]{0:T(512)S(1)}, f32[512]{0:T(512)}, u32[]{:S(2)}) copy-start(f32[512]{0:T(512)} %param.21) | copy-start | bytes 6148
  32.2 4.5 %copy-start = (bf16[256,512]{1,0:T(8,128)(2,1)}, bf16[256,512]{1,0:T(8,128)(2,1)S(1)}, u32[]{:S(2)}) copy-start(bf16[256,512]{1,0:T(8,128)(2,1)S(1)} %get-tuple-element.51.sum_r_ref) | copy-start | bytes 786436
  32.2 2.0 %collective-permute-start.4 = (bf16[528,512]{1,0:T(8,128)(2,1)S(1)}, bf16[528,512]{1,0:T(8,128)(2,1)S(1)}, u32[]{:S(2)}, u32[]{:S(2)}) collective-permute-start(bf16[528,512]{1,0:T(8,128)(2,1)S(1)} %get-tuple-element.42), channel_id=1, source_target_pairs={{0,1},{1,0},{2,3},{3,2},{4,5},{5,4},{6,7},{7,6},{8,9},{9,8},{10,11... | collective-permute-start | bytes 1622024 | tf_op jit(solution)/shard_map/ppermute | solution.py:402
  32.3 2.7 %collective-permute-start = (bf16[512,512]{1,0:T(8,128)(2,1)S(1)}, bf16[512,512]{1,0:T(8,128)(2,1)S(1)}, u32[]{:S(2)}, u32[]{:S(2)}) collective-permute-start(bf16[512,512]{1,0:T(8,128)(2,1)S(1)} %get-tuple-element.36), channel_id=1, source_target_pairs={{0,1},{1,0},{2,3},{3,2},{4,5},{5,4},{6,7},{7,6},{8,9},{9,8},{10,11... | collective-permute-start | bytes 1572872 | tf_op jit(solution)/shard_map/ppermute | solution.py:402
  34.3 8.8 %collective-permute-start.5 = (bf16[272,512]{1,0:T(8,128)(2,1)S(1)}, bf16[272,512]{1,0:T(8,128)(2,1)S(1)}, u32[]{:S(2)}, u32[]{:S(2)}) collective-permute-start(bf16[272,512]{1,0:T(8,128)(2,1)S(1)} %get-tuple-element.44.refs_1_), channel_id=1, source_target_pairs={{0,4},{1,5},{2,6},{3,7},{4,0},{5,1},{6,2},{7,3},{8,12},{9,13},{10,... | collective-permute-start | bytes 835592 | tf_op jit(solution)/shard_map/ppermute | solution.py:402
  35.0 8.5 %collective-permute-start.1 = (bf16[256,512]{1,0:T(8,128)(2,1)S(1)}, bf16[256,512]{1,0:T(8,128)(2,1)S(1)}, u32[]{:S(2)}, u32[]{:S(2)}) collective-permute-start(bf16[256,512]{1,0:T(8,128)(2,1)S(1)} %get-tuple-element.38.refs_0_), channel_id=1, source_target_pairs={{0,2},{1,3},{2,0},{3,1},{4,6},{5,7},{6,4},{7,5},{8,10},{9,11},{10,... | collective-permute-start | bytes 786440 | tf_op jit(solution)/shard_map/ppermute | solution.py:402
  36.7 22.3 %all-to-all-start.1 = ((bf16[16,16,512]{2,1,0:T(8,128)(2,1)}), bf16[16,16,512]{2,1,0:T(8,128)(2,1)S(1)}, u32[]{:S(2)}, u32[]{:S(2)}) async-start(bf16[16,16,512]{2,1,0:T(8,128)(2,1)} %bitcast.8), calls=%async_computation.1 | async-start | bytes 524288 | tf_op jit(solution)/shard_map/all_to_all | solution.py:471
  43.1 6.4 %collective-permute-start.6 = (bf16[144,512]{1,0:T(8,128)(2,1)S(1)}, bf16[144,512]{1,0:T(8,128)(2,1)S(1)}, u32[]{:S(2)}, u32[]{:S(2)}) collective-permute-start(bf16[144,512]{1,0:T(8,128)(2,1)S(1)} %get-tuple-element.46), channel_id=1, source_target_pairs={{0,2},{1,3},{2,0},{3,1},{4,6},{5,7},{6,4},{7,5},{8,10},{9,11},{10,... | collective-permute-start | bytes 442376 | tf_op jit(solution)/shard_map/ppermute | solution.py:402
  43.6 8.5 %collective-permute-start.2 = (bf16[128,512]{1,0:T(8,128)(2,1)S(1)}, bf16[128,512]{1,0:T(8,128)(2,1)S(1)}, u32[]{:S(2)}, u32[]{:S(2)}) collective-permute-start(bf16[128,512]{1,0:T(8,128)(2,1)S(1)} %get-tuple-element.40), channel_id=1, source_target_pairs={{0,4},{1,5},{2,6},{3,7},{4,0},{5,1},{6,2},{7,3},{8,12},{9,13},{10,... | collective-permute-start | bytes 393224 | tf_op jit(solution)/shard_map/ppermute | solution.py:402
  49.6 14.6 %collective-permute-start.7 = (bf16[144,512]{1,0:T(8,128)(2,1)S(1)}, bf16[144,512]{1,0:T(8,128)(2,1)S(1)}, u32[]{:S(2)}, u32[]{:S(2)}) collective-permute-start(bf16[144,512]{1,0:T(8,128)(2,1)S(1)} %shard_map.172.keep_ref), channel_id=1, source_target_pairs={{0,8},{1,9},{2,10},{3,11},{4,12},{5,13},{6,14},{7,15},{8,0},{9,1},... | collective-permute-start | bytes 442376 | tf_op jit(solution)/shard_map/ppermute | solution.py:402
  52.2 11.9 %collective-permute-start.3 = (bf16[128,512]{1,0:T(8,128)(2,1)S(1)}, bf16[128,512]{1,0:T(8,128)(2,1)S(1)}, u32[]{:S(2)}, u32[]{:S(2)}) collective-permute-start(bf16[128,512]{1,0:T(8,128)(2,1)S(1)} %shard_map.169.keep_ref), channel_id=1, source_target_pairs={{0,8},{1,9},{2,10},{3,11},{4,12},{5,13},{6,14},{7,15},{8,0},{9,1},... | collective-permute-start | bytes 393224 | tf_op jit(solution)/shard_map/ppermute | solution.py:402
  59.0 0.7 copy-start.7
  64.2 5.0 %collective-permute-start.8 = (bf16[128,512]{1,0:T(8,128)(2,1)S(1)}, bf16[128,512]{1,0:T(8,128)(2,1)S(1)}, u32[]{:S(2)}, u32[]{:S(2)}) collective-permute-start(bf16[128,512]{1,0:T(8,128)(2,1)S(1)} %shard_map.176), channel_id=1, source_target_pairs={{0,4},{1,5},{2,6},{3,7},{4,0},{5,1},{6,2},{7,3},{8,12},{9,13},{10,... | collective-permute-start | bytes 393224 | tf_op jit(solution)/shard_map/ppermute | solution.py:402
  65.0 5.7 %collective-permute-start.12 = (bf16[128,512]{1,0:T(8,128)(2,1)S(1)}, bf16[128,512]{1,0:T(8,128)(2,1)S(1)}, u32[]{:S(2)}, u32[]{:S(2)}) collective-permute-start(bf16[128,512]{1,0:T(8,128)(2,1)S(1)} %slice.8), channel_id=1, source_target_pairs={{0,2},{1,3},{2,0},{3,1},{4,6},{5,7},{6,4},{7,5},{8,10},{9,11},{10,... | collective-permute-start | bytes 393224 | tf_op jit(solution)/shard_map/ppermute | solution.py:402
  69.2 6.6 %collective-permute-start.9 = (bf16[256,512]{1,0:T(8,128)(2,1)S(1)}, bf16[256,512]{1,0:T(8,128)(2,1)S(1)}, u32[]{:S(2)}, u32[]{:S(2)}) collective-permute-start(bf16[256,512]{1,0:T(8,128)(2,1)S(1)} %pad_maximum_fusion.refs_0_.p0), channel_id=1, source_target_pairs={{0,2},{1,3},{2,0},{3,1},{4,6},{5,7},{6,4},{7,5},{8,10},{9,11},{10,... | collective-permute-start | bytes 786440 | tf_op jit(solution)/shard_map/ppermute | solution.py:402
  70.7 6.7 %collective-permute-start.13 = (bf16[256,512]{1,0:T(8,128)(2,1)S(1)}, bf16[256,512]{1,0:T(8,128)(2,1)S(1)}, u32[]{:S(2)}, u32[]{:S(2)}) collective-permute-start(bf16[256,512]{1,0:T(8,128)(2,1)S(1)} %pad_maximum_fusion.1.refs_3_.q0), channel_id=1, source_target_pairs={{0,4},{1,5},{2,6},{3,7},{4,0},{5,1},{6,2},{7,3},{8,12},{9,13},{10,... | collective-permute-start | bytes 786440 | tf_op jit(solution)/shard_map/ppermute | solution.py:402
  71.5 5.9 %collective-permute-start.10 = (bf16[256,512]{1,0:T(8,128)(2,1)S(1)}, bf16[256,512]{1,0:T(8,128)(2,1)S(1)}, u32[]{:S(2)}, u32[]{:S(2)}) collective-permute-start(bf16[256,512]{1,0:T(8,128)(2,1)S(1)} %pad_maximum_fusion.refs_0_.p0), channel_id=1, source_target_pairs={{0,1},{1,0},{2,3},{3,2},{4,5},{5,4},{6,7},{7,6},{8,9},{9,8},{10,11... | collective-permute-start | bytes 786440 | tf_op jit(solution)/shard_map/ppermute | solution.py:402
  71.5 5.9 %collective-permute-start.14 = (bf16[256,512]{1,0:T(8,128)(2,1)S(1)}, bf16[256,512]{1,0:T(8,128)(2,1)S(1)}, u32[]{:S(2)}, u32[]{:S(2)}) collective-permute-start(bf16[256,512]{1,0:T(8,128)(2,1)S(1)} %pad_maximum_fusion.1.refs_3_.q0), channel_id=1, source_target_pairs={{0,1},{1,0},{2,3},{3,2},{4,5},{5,4},{6,7},{7,6},{8,9},{9,8},{10,11... | collective-permute-start | bytes 786440 | tf_op jit(solution)/shard_map/ppermute | solution.py:402
  75.8 1.9 %collective-permute-start.11 = (bf16[256,512]{1,0:T(8,128)(2,1)S(1)}, bf16[256,512]{1,0:T(8,128)(2,1)S(1)}, u32[]{:S(2)}, u32[]{:S(2)}) collective-permute-start(bf16[256,512]{1,0:T(8,128)(2,1)S(1)} %collective-permute-done.9.refs_1_.p1), channel_id=1, source_target_pairs={{0,1},{1,0},{2,3},{3,2},{4,5},{5,4},{6,7},{7,6},{8,9},{9,8},{10,11... | collective-permute-start | bytes 786440 | tf_op jit(solution)/shard_map/ppermute | solution.py:402
  77.4 1.5 %collective-permute-start.15 = (bf16[256,512]{1,0:T(8,128)(2,1)S(1)}, bf16[256,512]{1,0:T(8,128)(2,1)S(1)}, u32[]{:S(2)}, u32[]{:S(2)}) collective-permute-start(bf16[256,512]{1,0:T(8,128)(2,1)S(1)} %collective-permute-done.13.refs_4_.q1), channel_id=1, source_target_pairs={{0,1},{1,0},{2,3},{3,2},{4,5},{5,4},{6,7},{7,6},{8,9},{9,8},{10,11... | collective-permute-start | bytes 786440 | tf_op jit(solution)/shard_map/ppermute | solution.py:402
